TPU v7x, 32 devices: a whole 2x2x4 slice. The times are simulated.
32 devices in a mesh: day: 2 (over y), chan: 4 (over z), tf: 4 (over x, core).
Axes of the slice: x: 2, y: 2, z: 4, core: 2. Of those that a mesh axis runs over, the one named last changes fastest.
Arguments:
- samples: bfloat16 [176, 512, 1024], P(('day', 'tf'), None, 'chan'), parts along dimension 0, may hold values from -6 to 6
- quality: int32 [176], P('day'), parts along dimension 0, may hold values from 0 to 3
- substack: int32 [176], P('day'), parts along dimension 0, may hold values from 0 to 1
- sources: int32 [256], replicated, may hold values from 0 to 1023, as said below
Outputs:
- stacks: bfloat16 [96, 4, 2, 256, 1024], P('tf', 'day', None, None, 'chan'), parts along dimension 1
There are 2 independent parts, one for each index of `day`. A program takes and returns all parts, laid end to end along the dimension named above; an argument that names none is the same for every part. Nothing has to cross between parts.
Inputs may be any that keep to these rules, and one draw needn't show every extreme that they name: `sources`: virtual source s is a channel of block s // 64: its index lies in [(s // 64) * 256, (s // 64 + 1) * 256).
All inputs are finite; a program needn't handle non-finite values.
Results may differ from a plain program's by a relative error of at most 0.0084.
Values may be sent and summed in bfloat16 or wider, within the bound.
No kernel may reach another device: no remote copies, remote signals or barrier semaphores. Data moves between devices by JAX's collectives and lax.ppermute only.
A program may use at most 64 MiB of HBM per device.

v0:
```python
import math

import jax
import jax.numpy as jnp
from jax import lax
from jax.sharding import PartitionSpec as P

F = 96
K0 = 8
G = 2


def passed_along(value, axis, steps):
    count = lax.axis_size(axis)
    pairs = [(source, (source + steps) % count) for source in range(count)]
    return lax.ppermute(value, axis, pairs)


def make_table(freq_count, length, first_bin):
    freqs = first_bin + jnp.arange(freq_count, dtype=jnp.int32)
    times = jnp.arange(length, dtype=jnp.int32)
    phase = freqs[:, None] * times[None, :] % length
    angle = phase.astype(jnp.float32) * (2.0 * math.pi / length)
    scale = 1.0 / math.sqrt(length)
    table = jnp.stack([jnp.cos(angle) * scale, -jnp.sin(angle) * scale], axis=1)
    return table.astype(jnp.bfloat16)


def shards(samples, quality, substack, sources):
    win_local, length, chan_local = samples.shape
    table = make_table(F, length, K0).reshape(2 * F, length)
    values = samples.astype(jnp.float32)
    power = jnp.mean(values * values, axis=1, keepdims=True)
    normed = (values / jnp.sqrt(power + 1e-06)).astype(jnp.bfloat16)
    spectra = jnp.einsum("kl,wlc->kwc", table, normed, preferred_element_type=jnp.float32).astype(
        jnp.bfloat16
    )
    spectra = spectra.reshape(F, 2, win_local, chan_local)
    received = lax.all_to_all(spectra, "tf", split_axis=0, concat_axis=2, tiled=True)
    bin_local, _, win_all, _ = received.shape
    flat_received = received.reshape(bin_local, 2 * win_all, chan_local)
    n_chan = lax.axis_size("chan")
    position = lax.axis_index("chan")
    src_local = sources.shape[0] // n_chan
    my_sources = lax.dynamic_slice_in_dim(sources, position * src_local, src_local, 0)
    columns = my_sources - position * chan_local
    selector = (columns[:, None] == jnp.arange(chan_local, dtype=jnp.int32)[None, :]).astype(
        jnp.bfloat16
    )
    panel = jnp.einsum(
        "frwc,sc->fsrw", received, selector, preferred_element_type=jnp.float32
    ).astype(jnp.bfloat16)
    groups = jnp.arange(G, dtype=jnp.int32)
    coef = jnp.where(
        substack[None, :] == groups[:, None],
        (quality[None, :].astype(jnp.float32) + 1.0) / 4.0,
        0.0,
    )
    inv_count = 1.0 / math.sqrt(win_all)

    def cross_block(piece):
        real_src = piece[:, :, 0, :].astype(jnp.float32)
        imag_src = piece[:, :, 1, :].astype(jnp.float32)
        real_part = (
            (coef[None, :, None, :] * real_src[:, None]).astype(jnp.bfloat16).astype(jnp.float32)
        )
        imag_part = (
            (coef[None, :, None, :] * imag_src[:, None]).astype(jnp.bfloat16).astype(jnp.float32)
        )
        first = jnp.concatenate([real_part, imag_part], axis=-1)
        second = jnp.concatenate([-imag_part, real_part], axis=-1)
        matrix = jnp.stack([first, second], axis=2).astype(jnp.bfloat16)
        summed = jnp.einsum(
            "fgosk,fkc->fgosc", matrix, flat_received, preferred_element_type=jnp.float32
        )
        return (summed * inv_count).astype(jnp.bfloat16)

    output = jnp.zeros((bin_local, G, 2, src_local * n_chan, chan_local), jnp.bfloat16)
    output = lax.dynamic_update_slice_in_dim(output, cross_block(panel), position * src_local, 3)

    def one_turn(turn, carry):
        moving, filled = carry
        moving = passed_along(moving, "chan", 1)
        owner = (position - turn) % n_chan
        filled = lax.dynamic_update_slice_in_dim(filled, cross_block(moving), owner * src_local, 3)
        return (moving, filled)

    _, stacks = lax.fori_loop(1, n_chan, one_turn, (panel, output))
    return stacks


def solution(mesh):
    in_specs = (P(("day", "tf"), None, "chan"), P("day"), P("day"), P())
    out_specs = P("tf", "day", None, None, "chan")
    return jax.shard_map(shards, mesh=mesh, in_specs=in_specs, out_specs=out_specs, check_vma=False)
```

profile of v0, /device:TPU:0, one launch (start us, length us, event | category | flops | bytes accessed | tf_op | source)
XLA Modules:
  0.0 143.0 jit_solution(17557563732232112824)
XLA Ops:
  0.0 0.9 multiply_convert_fusion.7
  0.9 0.2 copy.55
  1.1 0.1 reshape.211
  1.2 0.0 copy-start
  1.2 3.9 %fusion.13 = f32[22,256]{1,0:T(8,128)S(1)} fusion(bf16[22,512,256]{2,1,0:T(8,128)(2,1)} %param.6), kind=kLoop, calls=%fused_computation.21 | loop fusion | flops 8645120 | bytes 5789696 | tf_op jit(solution)/shard_map/reduce_sum | solution.py:33
  5.2 0.3 copy-done
  5.5 2.7 %fusion.27 = bf16[192,22,256]{2,0,1:T(8,128)(2,1)} fusion(bf16[192,512,1]{1,0,2:T(8,128)(2,1)S(1)} %reshape.211, bf16[22,512,256]{2,1,0:T(8,128)(2,1)S(1)} %copy-done, f32[22,256]{1,0:T(8,128)S(1)} %add_sqrt_fusion), kind=kOutput, calls=%fused_computation.33 | convolution fusion | flops 1117028352 | bytes 8148992 | tf_op jit(solution)/shard_map/kl,wlc->kwc/dot_general | solution.py:35
  8.2 4.5 %reshape.202 = bf16[96,2,22,256]{3,1,0,2:T(2,128)(2,1)S(1)} reshape(bf16[192,22,256]{2,0,1:T(8,128)(2,1)} %fusion.27) | data formatting | bytes 4325376 | tf_op jit(solution)/shard_map/reshape | solution.py:38
  12.7 2.8 %copy.56 = bf16[96,2,22,256]{3,1,2,0:T(2,128)(2,1)} copy(bf16[96,2,22,256]{3,1,0,2:T(2,128)(2,1)S(1)} %reshape.202) | data formatting | bytes 4325376 | tf_op jit(solution)/shard_map/reshape | solution.py:38
  15.5 0.0 copy-start.2
  15.5 4.3 %all-to-all-start = ((bf16[96,2,22,256]{3,1,2,0:T(2,128)(2,1)}), bf16[96,2,22,256]{3,1,2,0:T(2,128)(2,1)S(1)}, u32[]{:S(2)}, u32[]{:S(2)}) async-start(bf16[96,2,22,256]{3,1,2,0:T(2,128)(2,1)} %copy.56), calls=%async_computation | async-start | bytes 4325376 | tf_op jit(solution)/shard_map/all_to_all | solution.py:39
  19.9 0.0 copy-done.2
  19.9 0.1 dynamic-slice_subtract_fusion
  20.0 0.0 copy-done.3
  20.0 0.0 copy-done.1
  20.0 26.5 %all-to-all-done = bf16[96,2,22,256]{3,1,2,0:T(2,128)(2,1)S(1)} async-done(((bf16[96,2,22,256]{3,1,2,0:T(2,128)(2,1)}), bf16[96,2,22,256]{3,1,2,0:T(2,128)(2,1)S(1)}, u32[]{:S(2)}, u32[]{:S(2)}) %all-to-all-start) | async-done | bytes 2162720 | tf_op jit(solution)/shard_map/all_to_all | solution.py:39
  46.5 0.4 copy.57
  46.8 0.1 copy.58
  47.0 1.0 fusion.33
  48.0 0.2 fusion.36
  48.1 0.9 copy.63
  49.1 0.4 copy.64
  49.5 0.7 negate_convert_fusion.1
  50.2 2.6 %maximum_bitcast_fusion.2 = (bf16[24,2,1,64,176]{4,3,2,1,0:T(8,128)(2,1)S(1)}, bf16[24,2,1,64,176]{4,3,2,1,0:T(8,128)(2,1)}) fusion(bf16[24,2,64,88]{3,2,1,0:T(8,128)(2,1)S(1)} %get-tuple-element.245, bf16[24,2,64,88]{3,2,1,0:T(8,128)(2,1)S(1)} %get-tuple-element.255, bf16[24,2,64,88]{3,2,1,0:T(8,128)(2,1)S(1)} %get-tuple-element.244), kind=kLoop, calls=%fused_computation.34 | loop fusion | flops 4325376 | bytes 3784704 | tf_op jit(solution)/shard_map/stack | solution.py:72
  52.8 6.3 %broadcast_in_dim.20 = bf16[24,2,2,256,256]{4,3,2,1,0:T(8,128)(2,1)} broadcast(bf16[]{:T(256)} %constant.116.clone.1), dimensions={} | broadcast | bytes 12582914 | tf_op jit(solution)/shard_map/broadcast_in_dim | solution.py:78
  59.1 4.5 %fusion.17 = bf16[24,2,2,256,256]{4,3,2,1,0:T(8,128)(2,1)} fusion(bf16[24,2,2,256,256]{4,3,2,1,0:T(8,128)(2,1)} %broadcast_in_dim.20, s32[]{:T(128)S(6)} %select_n.61, bf16[24,2,1,64,176]{4,3,2,1,0:T(8,128)(2,1)} %get-tuple-element.252, bf16[24,2,1,64,176]{4,3,2,1,0:T(8,128)(2,1)S(1)} %get-tuple-element.251, bf16[24,176,256,1,1]{2,0,1,4,3:T(8,128)(2,1)S(1)} %bitcast.62), kind=kOutput, calls=%fused_computation.25 | convolution fusion | flops 557875200 | bytes 7962628 | tf_op jit(solution)/shard_map/fgosk,fkc->fgosc/dot_general | solution.py:73
  63.5 79.4 %while.18 = (s32[]{:T(128)}, bf16[24,64,2,88]{3,1,0,2:T(8,128)(2,1)}, bf16[24,2,2,256,256]{4,3,2,1,0:T(8,128)(2,1)}, bf16[24,176,256]{2,1,0:T(8,128)(2,1)S(1)}, ...) while((s32[]{:T(128)}, ...), condition=%wide.region_2.3_spmd.clone, body=%wide.region_1.2_spmd.clone.sunk | while | flops 564363648 | bytes 18827664 | solution.py:88
  63.5 2.2 %collective-permute-start = (bf16[24,64,2,88]{3,1,0,2:T(8,128)(2,1)}, bf16[24,64,2,88]{3,1,0,2:T(8,128)(2,1)S(1)}, u32[]{:S(2)}, u32[]{:S(2)}) collective-permute-start(bf16[24,64,2,88]{3,1,0,2:T(8,128)(2,1)} %get-tuple-element.329), channel_id=1, source_target_pairs={{0,4},{4,8},{8,12},{12,0},{1,5},{5,9},{9,13},{13,1},{2,6},{6,10},{... | collective-permute-start | bytes 1622024 | tf_op jit(solution)/shard_map/while/body/eval_jaxpr/ppermute | solution.py:16
  65.8 19.6 %collective-permute-done = bf16[24,64,2,88]{3,1,0,2:T(8,128)(2,1)S(1)} collective-permute-done((bf16[24,64,2,88]{3,1,0,2:T(8,128)(2,1)}, bf16[24,64,2,88]{3,1,0,2:T(8,128)(2,1)S(1)}, u32[]{:S(2)}, u32[]{:S(2)}) %collective-permute-start) | collective-permute-done | bytes 540704 | tf_op jit(solution)/shard_map/while/body/eval_jaxpr/ppermute | solution.py:16
  85.4 0.2 fusion.55
  85.5 0.7 negate_convert_fusion.3
  86.2 1.3 maximum_bitcast_fusion.5
  87.5 2.8 %fusion.56 = bf16[24,2,2,256,256]{4,3,2,1,0:T(8,128)(2,1)} fusion(bf16[24,2,2,256,256]{4,3,2,1,0:T(8,128)(2,1)} %get-tuple-element.330, s32[]{:T(128)S(6)} %select_n.86, bf16[24,2,1,64,176]{4,3,2,1,0:T(8,128)(2,1)S(1)} %get-tuple-element.313, bf16[24,2,1,64,176]{4,3,2,1,0:T(8,128)(2,1)S(1)} %get-tuple-element.314, ...), kind=kOutput, calls=%fused_computation.2.clone.1 | convolution fusion | flops 557875200 | bytes 7471108 | tf_op jit(solution)/shard_map/while/body/eval_jaxpr/fgosk,fkc->fgosc/dot_general | solution.py:73
  90.3 0.9 copy.87
  91.2 0.0 collective-permute-start
  91.2 20.5 %collective-permute-done = bf16[24,64,2,88]{3,1,0,2:T(8,128)(2,1)S(1)} collective-permute-done((bf16[24,64,2,88]{3,1,0,2:T(8,128)(2,1)}, bf16[24,64,2,88]{3,1,0,2:T(8,128)(2,1)S(1)}, u32[]{:S(2)}, u32[]{:S(2)}) %collective-permute-start) | collective-permute-done | bytes 540704 | tf_op jit(solution)/shard_map/while/body/eval_jaxpr/ppermute | solution.py:16
  111.7 0.2 fusion.55
  111.9 0.7 negate_convert_fusion.3
  112.5 1.3 maximum_bitcast_fusion.5
  113.9 2.8 %fusion.56 = bf16[24,2,2,256,256]{4,3,2,1,0:T(8,128)(2,1)} fusion(bf16[24,2,2,256,256]{4,3,2,1,0:T(8,128)(2,1)} %get-tuple-element.330, s32[]{:T(128)S(6)} %select_n.86, bf16[24,2,1,64,176]{4,3,2,1,0:T(8,128)(2,1)S(1)} %get-tuple-element.313, bf16[24,2,1,64,176]{4,3,2,1,0:T(8,128)(2,1)S(1)} %get-tuple-element.314, ...), kind=kOutput, calls=%fused_computation.2.clone.1 | convolution fusion | flops 557875200 | bytes 7471108 | tf_op jit(solution)/shard_map/while/body/eval_jaxpr/fgosk,fkc->fgosc/dot_general | solution.py:73
  116.6 0.9 copy.87
  117.5 0.0 collective-permute-start
  117.5 19.6 %collective-permute-done = bf16[24,64,2,88]{3,1,0,2:T(8,128)(2,1)S(1)} collective-permute-done((bf16[24,64,2,88]{3,1,0,2:T(8,128)(2,1)}, bf16[24,64,2,88]{3,1,0,2:T(8,128)(2,1)S(1)}, u32[]{:S(2)}, u32[]{:S(2)}) %collective-permute-start) | collective-permute-done | bytes 540704 | tf_op jit(solution)/shard_map/while/body/eval_jaxpr/ppermute | solution.py:16
  137.1 0.2 fusion.55
  137.3 0.7 negate_convert_fusion.3
  138.0 1.3 maximum_bitcast_fusion.5
  139.3 2.8 %fusion.56 = bf16[24,2,2,256,256]{4,3,2,1,0:T(8,128)(2,1)} fusion(bf16[24,2,2,256,256]{4,3,2,1,0:T(8,128)(2,1)} %get-tuple-element.330, s32[]{:T(128)S(6)} %select_n.86, bf16[24,2,1,64,176]{4,3,2,1,0:T(8,128)(2,1)S(1)} %get-tuple-element.313, bf16[24,2,1,64,176]{4,3,2,1,0:T(8,128)(2,1)S(1)} %get-tuple-element.314, ...), kind=kOutput, calls=%fused_computation.2.clone.1 | convolution fusion | flops 557875200 | bytes 7471108 | tf_op jit(solution)/shard_map/while/body/eval_jaxpr/fgosk,fkc->fgosc/dot_general | solution.py:73
  142.1 0.9 copy.87
  (10 shorter events, 0.1 us)
Async XLA Ops:
  1.2 4.3 %copy-start = (bf16[22,512,256]{2,1,0:T(8,128)(2,1)S(1)}, bf16[22,512,256]{2,1,0:T(8,128)(2,1)}, u32[]{:S(2)}) copy-start(bf16[22,512,256]{2,1,0:T(8,128)(2,1)} %param.6) | copy-start | bytes 17301508
  15.5 4.3 %copy-start.2 = (s32[256]{0:T(256)S(1)}, s32[256]{0:T(256)}, u32[]{:S(2)}) copy-start(s32[256]{0:T(256)} %param.9) | copy-start | bytes 3076
  15.5 4.4 %copy-start.3 = (s32[88]{0:T(128)S(1)}, s32[88]{0:T(128)}, u32[]{:S(2)}) copy-start(s32[88]{0:T(128)} %param.7) | copy-start | bytes 1060
  15.5 4.4 %copy-start.1 = (s32[88]{0:T(128)S(1)}, s32[88]{0:T(128)}, u32[]{:S(2)}) copy-start(s32[88]{0:T(128)} %param.8) | copy-start | bytes 1060
  15.5 30.9 %all-to-all-start = ((bf16[96,2,22,256]{3,1,2,0:T(2,128)(2,1)}), bf16[96,2,22,256]{3,1,2,0:T(2,128)(2,1)S(1)}, u32[]{:S(2)}, u32[]{:S(2)}) async-start(bf16[96,2,22,256]{3,1,2,0:T(2,128)(2,1)} %copy.56), calls=%async_computation | async-start | bytes 4325376 | tf_op jit(solution)/shard_map/all_to_all | solution.py:39
  63.5 21.8 %collective-permute-start = (bf16[24,64,2,88]{3,1,0,2:T(8,128)(2,1)}, bf16[24,64,2,88]{3,1,0,2:T(8,128)(2,1)S(1)}, u32[]{:S(2)}, u32[]{:S(2)}) collective-permute-start(bf16[24,64,2,88]{3,1,0,2:T(8,128)(2,1)} %get-tuple-element.329), channel_id=1, source_target_pairs={{0,4},{4,8},{8,12},{12,0},{1,5},{5,9},{9,13},{13,1},{2,6},{6,10},{... | collective-permute-start | bytes 1622024 | tf_op jit(solution)/shard_map/while/body/eval_jaxpr/ppermute | solution.py:16
  91.2 20.5 %collective-permute-start = (bf16[24,64,2,88]{3,1,0,2:T(8,128)(2,1)}, bf16[24,64,2,88]{3,1,0,2:T(8,128)(2,1)S(1)}, u32[]{:S(2)}, u32[]{:S(2)}) collective-permute-start(bf16[24,64,2,88]{3,1,0,2:T(8,128)(2,1)} %get-tuple-element.329), channel_id=1, source_target_pairs={{0,4},{4,8},{8,12},{12,0},{1,5},{5,9},{9,13},{13,1},{2,6},{6,10},{... | collective-permute-start | bytes 1622024 | tf_op jit(solution)/shard_map/while/body/eval_jaxpr/ppermute | solution.py:16
  117.5 19.6 %collective-permute-start = (bf16[24,64,2,88]{3,1,0,2:T(8,128)(2,1)}, bf16[24,64,2,88]{3,1,0,2:T(8,128)(2,1)S(1)}, u32[]{:S(2)}, u32[]{:S(2)}) collective-permute-start(bf16[24,64,2,88]{3,1,0,2:T(8,128)(2,1)} %get-tuple-element.329), channel_id=1, source_target_pairs={{0,4},{4,8},{8,12},{12,0},{1,5},{5,9},{9,13},{13,1},{2,6},{6,10},{... | collective-permute-start | bytes 1622024 | tf_op jit(solution)/shard_map/while/body/eval_jaxpr/ppermute | solution.py:16
where the time goes:
time: 143 us
  waiting for transfers between devices  86.1 us (60%)
  local copies, waits for them, and re-layouts  18.8 us (13%)
  matrix products  16.4 us (11%)
  other arithmetic  14.8 us (10%)
  starting transfers between devices  6.59 us (5%)
    ppermute x3, waiting for transfers between devices, passed_along(): return lax.ppermute(value, axis, pairs)  59.7 us
    all_to_all x1, waiting for transfers between devices, shards(): lax.all_to_all(spectra, 'tf', split_axis=0, concat_axis=2, tiled=True)  26.5 us
    dot_general x4, matrix products, cross_block(): jnp.einsum('fgosk,fkc->fgosc', matrix, flat_received, preferred_element_t...  12.7 us
    reshape x2, local copies, waits for them, and re-layouts, shards(): spectra = spectra.reshape(F, 2, win_local, chan_local)  7.31 us
    another operation x4, other arithmetic, cross_block(): matrix = jnp.stack([first, second], axis=2).astype(jnp.bfloat16)  6.55 us
    broadcast_in_dim x1, local copies, waits for them, and re-layouts, shards(): jnp.zeros((bin_local, G, 2, src_local * n_chan, chan_local), jnp.bfloat16)  6.33 us
    all_to_all x1, starting transfers between devices, shards(): lax.all_to_all(spectra, 'tf', split_axis=0, concat_axis=2, tiled=True)  4.34 us
    reduce_sum x1, other arithmetic, shards(): power = jnp.mean(values * values, axis=1, keepdims=True)  3.94 us
  transfers between devices with their start and end apart: 4, of which 4 were waited for; matrix products, arithmetic and copies ran while one was open for 0% of the time, Pallas kernels for 0%

commit v1 on v0

v1 whole, which is shorter than its diff:
```python
import math

import jax
import jax.numpy as jnp
import numpy as np
import ml_dtypes
from jax import lax
from jax.experimental import pallas as pl
from jax.experimental.pallas import tpu as pltpu
from jax.sharding import PartitionSpec as P

F = 96
K0 = 8
G = 2
CHUNKS = 3
STEP = 2
f32 = jnp.float32
bf16 = jnp.bfloat16


def make_table(length):
    freqs = K0 + np.arange(F)
    phase = freqs[:, None] * np.arange(length)[None, :] % length
    angle = phase.astype(np.float32) * np.float32(2.0 * math.pi / length)
    scale = np.float32(1.0 / math.sqrt(length))
    table = np.stack([np.cos(angle) * scale, -np.sin(angle) * scale], axis=1)
    return table.astype(np.float32).astype(ml_dtypes.bfloat16)


def make_shuffle():
    shuffle = np.zeros((128, 128), np.float32)
    for w in range(8):
        for r in range(16):
            shuffle[r * 8 + w, w * 16 + r] = 1.0
    return shuffle.astype(ml_dtypes.bfloat16)


def up(n, m):
    return -(-n // m) * m


def head_kernel(cfg, order, samples, table, shuffle, *refs):
    win, wpad, n_tf, bins, chunks = cfg
    outs, (tscr, spec) = refs[:-2], refs[-2:]
    step = pl.program_id(0)

    @pl.when(step == 0)
    def _():
        rows = [table[order[k]].astype(f32) for k in range(n_tf)]
        tscr[...] = jnp.concatenate(rows, axis=0).astype(bf16)
        for w in range(win, wpad):
            spec[w] = jnp.zeros(spec.shape[1:], bf16)

    for i in range(STEP):
        x = samples[i]
        xf = x.astype(f32)
        power = jnp.mean(xf * xf, axis=0, keepdims=True)
        y = jnp.dot(tscr[...], x, preferred_element_type=f32)
        spec[step * STEP + i] = (y * lax.rsqrt(power + 1e-06)).astype(bf16)

    @pl.when(step == pl.num_programs(0) - 1)
    def _():
        per = bins // chunks
        for grp in range(2 * F // 16):
            parts = []
            for wg in range(wpad // 8):
                block = spec[8 * wg : 8 * wg + 8, 16 * grp : 16 * grp + 16, :]
                block = block.reshape(128, block.shape[-1])
                parts.append(jnp.dot(shuffle[...], block, preferred_element_type=f32))
            for j in range(8):
                flat = grp * 8 + j
                k, f = flat // bins, flat % bins
                pieces = []
                for r in range(2):
                    row = (2 * j + r) * 8
                    pieces += [p[row : row + 8] for p in parts]
                value = jnp.concatenate(pieces, axis=0).astype(bf16)
                if k < 2:
                    outs[k][f] = value
                else:
                    outs[2 + (k - 2) * chunks + f // per][f % per] = value


def select_kernel(wpad, cols, *refs):
    slabs, out = refs[:-1], refs[-1]
    bins, rows, chans = slabs[0].shape
    lanes = cols.shape[1]
    pick = (lax.broadcasted_iota(jnp.int32, (chans, lanes), 0) == cols[...]).astype(f32).astype(bf16)
    real = lax.broadcasted_iota(jnp.int32, (wpad, lanes), 1) < lanes // 2
    for d, slab in enumerate(slabs):
        def body(p, _, d=d, slab=slab):
            flat = slab[pl.ds(2 * p, 2)].reshape(2 * rows, chans)
            got = jnp.dot(flat, pick, preferred_element_type=f32)
            both = []
            for j in range(2):
                base = j * rows
                both.append(jnp.where(real, got[base : base + wpad], got[base + wpad : base + rows]))
            out[d, p] = jnp.concatenate(both, axis=0).astype(bf16)
            return 0

        lax.fori_loop(0, bins // 2, body, 0, unroll=True)


def cross_kernel(cfg, blk, coef, eye, *refs):
    wpad, kpad, scale, n_slab, counts = cfg
    out = refs[-1]
    slabs, rest = refs[:n_slab], refs[n_slab:]
    panels = []
    for near, far in counts:
        panels.append((rest[:near], rest[near : near + far]))
        rest = rest[near + far :]
    n_blk = len(panels)
    lanes = panels[0][0][0].shape[-1]
    src = lanes // 2
    chans = slabs[0].shape[-1]
    used = wpad * n_slab

    def merged(group):
        value = group[0][...].astype(f32)
        for other in group[1:]:
            value = value + other[...].astype(f32)
        return value

    loaded = [[merged(near), merged(far)] for near, far in panels]
    for j in range(2):
        re, im = [], []
        for slab in slabs:
            v = slab[j].astype(f32)
            re.append(v[:wpad])
            im.append(v[wpad:])
        if kpad > used:
            pad = [jnp.zeros((kpad - used, chans), f32)]
            re, im = re + pad, im + pad
        re = jnp.concatenate(re, axis=0)
        im = jnp.concatenate(im, axis=0)
        right = jnp.concatenate(
            [jnp.concatenate([re, im], axis=1), jnp.concatenate([im, -re], axis=1)], axis=0
        ).astype(bf16)
        stacked = []
        for near, far in loaded:
            for value in (near, far):
                for d in range(value.shape[0]):
                    stacked.append(value[d, 0, j * wpad : (j + 1) * wpad])
            if kpad > used:
                stacked.append(jnp.zeros((kpad - used, lanes), f32))
        stacked = jnp.concatenate(stacked, axis=0).astype(bf16)
        turned = lax.dot_general(
            eye[...], stacked, (((1,), (1,)), ((), ())), preferred_element_type=f32
        )
        for g in range(G):
            weight = coef[g : g + 1, :]
            rows = []
            for b in range(n_blk):
                t = turned[:, b * kpad : (b + 1) * kpad] * weight
                rows.append(jnp.concatenate([t[:src], t[src:]], axis=1))
            left = jnp.concatenate(rows, axis=0).astype(bf16)
            got = jnp.dot(left, right, preferred_element_type=f32) * scale
            got = got.astype(bf16)
            for b in range(n_blk):
                at = pl.ds(pl.multiple_of(blk[b] * src, src), src)
                for o in range(2):
                    out[j, g, o, at, :] = got[b * src : (b + 1) * src, o * chans : (o + 1) * chans]


def shards(samples, quality, substack, sources):
    win, length, chans = samples.shape
    n_tf = lax.axis_size("tf")
    n_chan = lax.axis_size("chan")
    me = lax.axis_index("tf")
    pos = lax.axis_index("chan")
    bins = F // n_tf
    src = sources.shape[0] // n_chan
    wpad = up(win, 8)
    kpad = up(wpad * n_tf, 128)
    per = bins // CHUNKS
    rows = 2 * wpad
    order = (me ^ jnp.arange(n_tf, dtype=jnp.int32)).astype(jnp.int32)
    table = jnp.asarray(make_table(length).reshape(n_tf, 2 * bins, length))
    smem = pl.BlockSpec(memory_space=pltpu.SMEM)
    vmem = pl.BlockSpec(memory_space=pltpu.VMEM)

    shapes = [jax.ShapeDtypeStruct((bins, rows, chans), bf16)] * 2
    shapes += [jax.ShapeDtypeStruct((per, rows, chans), bf16)] * ((n_tf - 2) * CHUNKS)
    got = pl.pallas_call(
        lambda *refs: head_kernel((win, wpad, n_tf, bins, CHUNKS), *refs),
        grid=(win // STEP,),
        in_specs=[
            smem,
            pl.BlockSpec((STEP, length, chans), lambda i: (i, 0, 0)),
            pl.BlockSpec((n_tf, 2 * bins, length), lambda i: (0, 0, 0)),
            pl.BlockSpec((128, 128), lambda i: (0, 0)),
        ],
        out_specs=[pl.BlockSpec(s.shape, lambda i: (0, 0, 0)) for s in shapes],
        out_shape=shapes,
        scratch_shapes=[
            pltpu.VMEM((2 * F, length), bf16),
            pltpu.VMEM((wpad, 2 * F, chans), bf16),
        ],
        compiler_params=pltpu.CompilerParams(vmem_limit_bytes=48 * 1024 * 1024),
        name="head",
    )(order, samples, table, jnp.asarray(make_shuffle()))
    own, for_core = got[0], got[1]

    def across(value, k):
        return lax.ppermute(value, "tf", [(i, i ^ k) for i in range(n_tf)])

    core = across(for_core, 1)
    far = [
        [across(got[2 + (k - 2) * CHUNKS + q], k) for k in range(2, n_tf)] for q in range(CHUNKS)
    ]

    mine = lax.dynamic_slice_in_dim(sources, pos * src, src, 0) - pos * chans
    cols = jnp.concatenate([mine, mine])[None, :]

    def select(slabs):
        count = slabs[0].shape[0]
        return pl.pallas_call(
            lambda *refs: select_kernel(wpad, *refs),
            in_specs=[vmem] * (1 + len(slabs)),
            out_specs=vmem,
            out_shape=jax.ShapeDtypeStruct((len(slabs), count // 2, 2 * wpad, 2 * src), bf16),
            compiler_params=pltpu.CompilerParams(vmem_limit_bytes=32 * 1024 * 1024),
            name="select",
        )(cols, *slabs)

    def spread(panel):
        if n_chan == 4:
            one = lax.ppermute(panel, "chan", [(i, i ^ 1) for i in range(4)])
            two = lax.ppermute(panel, "chan", [(i, i ^ 2) for i in range(4)])
            mid = lax.ppermute(panel, "chan", [(1, 2), (2, 1)])
            end = lax.ppermute(two, "chan", [(2, 3), (1, 0)])
            return [[panel], [one], [two], [mid, end]]
        return [[panel]] + [
            [lax.ppermute(panel, "chan", [(i, (i + k) % n_chan) for i in range(n_chan)])]
            for k in range(1, n_chan)
        ]

    if n_chan == 4:
        blk = pos ^ jnp.arange(4, dtype=jnp.int32)
    else:
        blk = (pos - jnp.arange(n_chan, dtype=jnp.int32)) % n_chan
    blk = blk.astype(jnp.int32)

    coef = jnp.where(
        substack[None, :] == jnp.arange(G, dtype=jnp.int32)[:, None],
        (quality[None, :].astype(f32) + 1.0) / 4.0,
        0.0,
    ).reshape(G, n_tf, win)
    coef = jnp.pad(coef, ((0, 0), (0, 0), (0, wpad - win)))
    coef = jnp.take(coef, order, axis=1).reshape(G, n_tf * wpad)
    coef = jnp.pad(coef, ((0, 0), (0, kpad - n_tf * wpad)))
    eye = jnp.asarray(np.eye(2 * src, dtype=np.float32).astype(ml_dtypes.bfloat16))
    scale = 1.0 / math.sqrt(win * n_tf)

    near = spread(select([own, core]))
    stacks = None
    out_shape = jax.ShapeDtypeStruct((bins, G, 2, src * n_chan, chans), bf16)
    for q in range(CHUNKS):
        away = spread(select(far[q]))
        pairs = per // 2
        lead = q * pairs
        slab_all = pl.BlockSpec((2, rows, chans), lambda i, lead=lead: (lead + i, 0, 0))
        slab_one = pl.BlockSpec((2, rows, chans), lambda i: (i, 0, 0))
        args, specs, counts = [own, core] + far[q], [slab_all] * 2 + [slab_one] * (n_tf - 2), []
        for a, b in zip(near, away):
            args += a + b
            specs += [
                pl.BlockSpec((2, 1, 2 * wpad, 2 * src), lambda i, lead=lead: (0, lead + i, 0, 0))
            ] * len(a)
            specs += [
                pl.BlockSpec((n_tf - 2, 1, 2 * wpad, 2 * src), lambda i: (0, i, 0, 0))
            ] * len(b)
            counts.append((len(a), len(b)))
        cfg = (wpad, kpad, scale, n_tf, counts)
        first = stacks is None
        extra = [] if first else [stacks]

        def body(*refs, cfg=cfg, first=first):
            refs = refs if first else refs[:-2] + refs[-1:]
            cross_kernel(cfg, *refs)

        stacks = pl.pallas_call(
            body,
            grid=(pairs,),
            in_specs=[smem, pl.BlockSpec(coef.shape, lambda i: (0, 0)), pl.BlockSpec(eye.shape, lambda i: (0, 0))]
            + specs
            + [pl.BlockSpec(memory_space=pl.ANY)] * len(extra),
            out_specs=pl.BlockSpec(
                (2, G, 2, src * n_chan, chans), lambda i, lead=lead: (lead + i, 0, 0, 0, 0)
            ),
            out_shape=out_shape,
            input_output_aliases={} if first else {3 + len(args): 0},
            compiler_params=pltpu.CompilerParams(vmem_limit_bytes=32 * 1024 * 1024),
            name="cross",
        )(blk, coef, eye, *args, *extra)
    return stacks


def solution(mesh):
    in_specs = (P(("day", "tf"), None, "chan"), P("day"), P("day"), P())
    out_specs = P("tf", "day", None, None, "chan")
    return jax.shard_map(shards, mesh=mesh, in_specs=in_specs, out_specs=out_specs, check_vma=False)
```

time: 143 us -> 92.6 us (0.65)
  the two profiles are of different devices: /device:TPU:0 before, /device:TPU:8 now
where the time goes in v1:
time: 92.6 us; the launch traced here: 91.7 us
  starting transfers between devices  39.9 us (43%)
  Pallas kernels  27 us (29%)
  local copies, waits for them, and re-layouts  12.3 us (13%)
  waiting for transfers between devices  10.7 us (12%)
  other arithmetic  1.6 us (2%)
    pallas_call x3, Pallas kernels, shards(): pl.pallas_call(body, grid=(pairs,), in_specs=[smem, pl.BlockSpec(coef.sha...  15.3 us
    ppermute x4, starting transfers between devices, spread(): mid = lax.ppermute(panel, 'chan', [(1, 2), (2, 1)])  13.8 us
    unnamed x42, local copies, waits for them, and re-layouts  10.8 us
    pallas_call x1, Pallas kernels, shards(): pl.pallas_call(lambda *refs: head_kernel((win, wpad, n_tf, bins, CHUNKS),...  9.79 us
    ppermute x7, waiting for transfers between devices, across(): return lax.ppermute(value, 'tf', [(i, i ^ k) for i in range(n_tf)])  9.44 us
    ppermute x4, starting transfers between devices, spread(): end = lax.ppermute(two, 'chan', [(2, 3), (1, 0)])  8.24 us
    ppermute x7, starting transfers between devices, across(): return lax.ppermute(value, 'tf', [(i, i ^ k) for i in range(n_tf)])  6.68 us
    ppermute x4, starting transfers between devices, spread(): two = lax.ppermute(panel, 'chan', [(i, i ^ 2) for i in range(4)])  6.24 us
  transfers between devices with their start and end apart: 23, of which 7 were waited for; matrix products, arithmetic and copies ran while one was open for 3% of the time, Pallas kernels for 13%

profile of v1, /device:TPU:8, one launch (start us, length us, event | category | flops | bytes accessed | tf_op | source)
XLA Modules:
  0.0 91.7 jit_solution(16896010512287509729)
XLA Ops:
  0.0 0.9 %copy-done.9 = bf16[4,48,512]{2,1,0:T(8,128)(2,1)S(1)} copy-done((bf16[4,48,512]{2,1,0:T(8,128)(2,1)S(1)}, bf16[4,48,512]{2,1,0:T(8,128)(2,1)}, u32[]{:S(2)}) %copy-start.9) | copy-done | bytes 196632
  0.9 0.8 copy-done.20
  1.7 9.8 %head.1 = (bf16[24,48,256]{2,1,0:T(8,128)(2,1)S(1)}, bf16[24,48,256]{2,1,0:T(8,128)(2,1)S(1)}, bf16[8,48,256]{2,1,0:T(8,128)(2,1)}, bf16[8,48,256]{2,1,0:T(8,128...) custom-call(s32[4]{0:T(128)S(1)} %iota_xor_fusion.refs_0_, ...), custom_call_target="tpu_custom_call" | custom-call | tf_op jit(solution)/shard_map/head/pallas_call | solution.py:184
  11.5 1.5 %collective-permute-start.17 = (bf16[8,48,256]{2,1,0:T(8,128)(2,1)}, bf16[8,48,256]{2,1,0:T(8,128)(2,1)S(1)}, u32[]{:S(2)}, u32[]{:S(2)}) collective-permute-start(bf16[8,48,256]{2,1,0:T(8,128)(2,1)} %get-tuple-element.19), channel_id=1, source_target_pairs={{0,2},{1,3},{2,0},{3,1},{4,6},{5,7},{6,4},{7,5},{8,10},{9,11},{10,... | collective-permute-start | bytes 589832 | tf_op jit(solution)/shard_map/ppermute | solution.py:205
  13.3 1.5 %collective-permute-start.11 = (bf16[8,48,256]{2,1,0:T(8,128)(2,1)}, bf16[8,48,256]{2,1,0:T(8,128)(2,1)S(1)}, u32[]{:S(2)}, u32[]{:S(2)}) collective-permute-start(bf16[8,48,256]{2,1,0:T(8,128)(2,1)} %get-tuple-element.17), channel_id=1, source_target_pairs={{0,2},{1,3},{2,0},{3,1},{4,6},{5,7},{6,4},{7,5},{8,10},{9,11},{10,... | collective-permute-start | bytes 589832 | tf_op jit(solution)/shard_map/ppermute | solution.py:205
  15.0 0.7 add_multiply_fusion
  15.7 0.7 eq.16
  16.5 0.8 dynamic-slice_subtract_fusion
  17.3 1.5 %collective-permute-start.1 = (bf16[8,48,256]{2,1,0:T(8,128)(2,1)S(1)}, bf16[8,48,256]{2,1,0:T(8,128)(2,1)S(1)}, u32[]{:S(2)}, u32[]{:S(2)}) collective-permute-start(bf16[8,48,256]{2,1,0:T(8,128)(2,1)S(1)} %get-tuple-element.15), channel_id=1, source_target_pairs={{0,2},{1,3},{2,0},{3,1},{4,6},{5,7},{6,4},{7,5},{8,10},{9,11},{10,... | collective-permute-start | bytes 589832 | tf_op jit(solution)/shard_map/ppermute | solution.py:205
  18.8 0.5 select.6.refs_7_
  19.4 2.6 %collective-permute-start.5 = (bf16[2,12,48,128]{3,2,1,0:T(8,128)(2,1)S(1)}, bf16[2,12,48,128]{3,2,1,0:T(8,128)(2,1)S(1)}, u32[]{:S(2)}, u32[]{:S(2)}) collective-permute-start(bf16[2,12,48,128]{3,2,1,0:T(8,128)(2,1)S(1)} %select.6.refs_7_), channel_id=1, source_target_pairs={{0,8},{4,12},{8,0},{12,4},{1,9},{5,13},{9,1},{13,5},{2,10},{6,14},... | collective-permute-start | bytes 884744 | tf_op jit(solution)/shard_map/ppermute | solution.py:229
  22.0 0.8 collective-permute-done.18.refs_2_.refs_6_
  22.8 1.7 %collective-permute-start.2 = (bf16[8,48,256]{2,1,0:T(8,128)(2,1)S(1)}, bf16[8,48,256]{2,1,0:T(8,128)(2,1)S(1)}, u32[]{:S(2)}, u32[]{:S(2)}) collective-permute-start(bf16[8,48,256]{2,1,0:T(8,128)(2,1)S(1)} %get-tuple-element.16), channel_id=1, source_target_pairs={{0,3},{1,2},{2,1},{3,0},{4,7},{5,6},{6,5},{7,4},{8,11},{9,10},{10,... | collective-permute-start | bytes 589832 | tf_op jit(solution)/shard_map/ppermute | solution.py:205
  24.8 3.0 %collective-permute-done.11.refs_1_.refs_5_ = bf16[8,48,256]{2,1,0:T(8,128)(2,1)S(1)} collective-permute-done((bf16[8,48,256]{2,1,0:T(8,128)(2,1)}, bf16[8,48,256]{2,1,0:T(8,128)(2,1)S(1)}, u32[]{:S(2)}, u32[]{:S(2)}) %collective-permute-start.11) | collective-permute-done | bytes 196640 | tf_op jit(solution)/shard_map/ppermute | solution.py:205
  27.8 2.6 %collective-permute-start.20 = (bf16[2,4,48,128]{3,2,1,0:T(8,128)(2,1)S(1)}, bf16[2,4,48,128]{3,2,1,0:T(8,128)(2,1)S(1)}, u32[]{:S(2)}, u32[]{:S(2)}) collective-permute-start(bf16[2,4,48,128]{3,2,1,0:T(8,128)(2,1)S(1)} %select.9.refs_8_), channel_id=1, source_target_pairs={{0,8},{4,12},{8,0},{12,4},{1,9},{5,13},{9,1},{13,5},{2,10},{6,14},... | collective-permute-start | bytes 294920 | tf_op jit(solution)/shard_map/ppermute | solution.py:229
  30.4 0.8 collective-permute-done.12.refs_2_.refs_6_
  31.3 0.4 collective-permute-start.19
  31.7 4.6 %collective-permute-done.1.refs_1_.refs_5_ = bf16[8,48,256]{2,1,0:T(8,128)(2,1)S(1)} collective-permute-done((bf16[8,48,256]{2,1,0:T(8,128)(2,1)S(1)}, bf16[8,48,256]{2,1,0:T(8,128)(2,1)S(1)}, u32[]{:S(2)}, u32[]{:S(2)}) %collective-permute-start.1) | collective-permute-done | bytes 196640 | tf_op jit(solution)/shard_map/ppermute | solution.py:205
  36.3 0.7 copy-done
  36.9 3.5 %collective-permute-start.21 = (bf16[2,4,48,128]{3,2,1,0:T(8,128)(2,1)S(1)}, bf16[2,4,48,128]{3,2,1,0:T(8,128)(2,1)S(1)}, u32[]{:S(2)}, u32[]{:S(2)}) collective-permute-start(bf16[2,4,48,128]{3,2,1,0:T(8,128)(2,1)S(1)} %select.9.refs_8_), channel_id=1, source_target_pairs={{4,8},{8,4},{5,9},{9,5},{6,10},{10,6},{7,11},{11,7},{20,24},{24,20... | collective-permute-start | bytes 294920 | tf_op jit(solution)/shard_map/ppermute | solution.py:230
  40.4 0.6 gather_fusion
  41.3 0.7 copy-done.3
  42.0 1.0 %collective-permute-start.14 = (bf16[2,4,48,128]{3,2,1,0:T(8,128)(2,1)S(1)}, bf16[2,4,48,128]{3,2,1,0:T(8,128)(2,1)S(1)}, u32[]{:S(2)}, u32[]{:S(2)}) collective-permute-start(bf16[2,4,48,128]{3,2,1,0:T(8,128)(2,1)S(1)} %select.8.refs_8_), channel_id=1, source_target_pairs={{0,8},{4,12},{8,0},{12,4},{1,9},{5,13},{9,1},{13,5},{2,10},{6,14},... | collective-permute-start | bytes 294920 | tf_op jit(solution)/shard_map/ppermute | solution.py:229
  43.0 0.9 %collective-permute-start.13 = (bf16[2,4,48,128]{3,2,1,0:T(8,128)(2,1)S(1)}, bf16[2,4,48,128]{3,2,1,0:T(8,128)(2,1)S(1)}, u32[]{:S(2)}, u32[]{:S(2)}) collective-permute-start(bf16[2,4,48,128]{3,2,1,0:T(8,128)(2,1)S(1)} %select.8.refs_8_), channel_id=1, source_target_pairs={{0,4},{4,0},{8,12},{12,8},{1,5},{5,1},{9,13},{13,9},{2,6},{6,2},{1... | collective-permute-start | bytes 294920 | tf_op jit(solution)/shard_map/ppermute | solution.py:228
  43.9 0.6 copy-done.12
  44.5 1.1 %collective-permute-start.3 = (bf16[2,12,48,128]{3,2,1,0:T(8,128)(2,1)S(1)}, bf16[2,12,48,128]{3,2,1,0:T(8,128)(2,1)S(1)}, u32[]{:S(2)}, u32[]{:S(2)}) collective-permute-start(bf16[2,12,48,128]{3,2,1,0:T(8,128)(2,1)S(1)} %select.6.refs_7_), channel_id=1, source_target_pairs={{0,4},{4,0},{8,12},{12,8},{1,5},{5,1},{9,13},{13,9},{2,6},{6,2},{1... | collective-permute-start | bytes 884744 | tf_op jit(solution)/shard_map/ppermute | solution.py:228
  45.7 0.6 copy-done.14
  46.3 3.0 %collective-permute-start.7 = (bf16[2,12,48,128]{3,2,1,0:T(8,128)(2,1)S(1)}, bf16[2,12,48,128]{3,2,1,0:T(8,128)(2,1)S(1)}, u32[]{:S(2)}, u32[]{:S(2)}) collective-permute-start(bf16[2,12,48,128]{3,2,1,0:T(8,128)(2,1)S(1)} %select.6.refs_7_), channel_id=1, source_target_pairs={{4,8},{8,4},{5,9},{9,5},{6,10},{10,6},{7,11},{11,7},{20,24},{24,20... | collective-permute-start | bytes 884744 | tf_op jit(solution)/shard_map/ppermute | solution.py:230
  49.3 1.3 %collective-permute-start.8 = (bf16[2,12,48,128]{3,2,1,0:T(8,128)(2,1)S(1)}, bf16[2,12,48,128]{3,2,1,0:T(8,128)(2,1)S(1)}, u32[]{:S(2)}, u32[]{:S(2)}) collective-permute-start(bf16[2,12,48,128]{3,2,1,0:T(8,128)(2,1)S(1)} %collective-permute-done.5.refs_11_), channel_id=1, source_target_pairs={{8,12},{4,0},{9,13},{5,1},{10,14},{6,2},{11,15},{7,3},{24,28},{20,... | collective-permute-start | bytes 884744 | tf_op jit(solution)/shard_map/ppermute | solution.py:231
  50.7 0.9 %copy-done.1 = bf16[8,48,256]{2,1,0:T(8,128)(2,1)S(1)} copy-done((bf16[8,48,256]{2,1,0:T(8,128)(2,1)S(1)}, bf16[8,48,256]{2,1,0:T(8,128)(2,1)}, u32[]{:S(2)}) %copy-start.1) | copy-done | bytes 196632
  51.6 0.9 %copy-done.4 = bf16[8,48,256]{2,1,0:T(8,128)(2,1)S(1)} copy-done((bf16[8,48,256]{2,1,0:T(8,128)(2,1)S(1)}, bf16[8,48,256]{2,1,0:T(8,128)(2,1)}, u32[]{:S(2)}) %copy-start.4) | copy-done | bytes 196632
  52.5 0.9 select.7.refs_8_
  53.5 0.6 copy-done.16
  54.1 0.6 copy-done.18
  54.7 4.3 %collective-permute-start.22 = (bf16[2,4,48,128]{3,2,1,0:T(8,128)(2,1)}, bf16[2,4,48,128]{3,2,1,0:T(8,128)(2,1)}, u32[]{:S(2)}, u32[]{:S(2)}) collective-permute-start(bf16[2,4,48,128]{3,2,1,0:T(8,128)(2,1)} %copy-done.10), channel_id=1, source_target_pairs={{8,12},{4,0},{9,13},{5,1},{10,14},{6,2},{11,15},{7,3},{24,28},{20,... | collective-permute-start | bytes 294920 | tf_op jit(solution)/shard_map/ppermute | solution.py:231
  59.4 3.2 %collective-permute-start.15 = (bf16[2,4,48,128]{3,2,1,0:T(8,128)(2,1)}, bf16[2,4,48,128]{3,2,1,0:T(8,128)(2,1)S(1)}, u32[]{:S(2)}, u32[]{:S(2)}) collective-permute-start(bf16[2,4,48,128]{3,2,1,0:T(8,128)(2,1)} %copy-done.6), channel_id=1, source_target_pairs={{4,8},{8,4},{5,9},{9,5},{6,10},{10,6},{7,11},{11,7},{20,24},{24,20... | collective-permute-start | bytes 294920 | tf_op jit(solution)/shard_map/ppermute | solution.py:230
  62.6 1.0 %collective-permute-done.22.refs_16_ = bf16[2,4,48,128]{3,2,1,0:T(8,128)(2,1)} collective-permute-done((bf16[2,4,48,128]{3,2,1,0:T(8,128)(2,1)}, bf16[2,4,48,128]{3,2,1,0:T(8,128)(2,1)}, u32[]{:S(2)}, u32[]{:S(2)}) %collective-permute-start.22) | collective-permute-done | bytes 98336 | tf_op jit(solution)/shard_map/ppermute | solution.py:231
  63.6 2.5 %collective-permute-start.4 = (bf16[2,4,48,128]{3,2,1,0:T(8,128)(2,1)}, bf16[2,4,48,128]{3,2,1,0:T(8,128)(2,1)S(1)}, u32[]{:S(2)}, u32[]{:S(2)}) collective-permute-start(bf16[2,4,48,128]{3,2,1,0:T(8,128)(2,1)} %select.7.refs_8_), channel_id=1, source_target_pairs={{0,4},{4,0},{8,12},{12,8},{1,5},{5,1},{9,13},{13,9},{2,6},{6,2},{1... | collective-permute-start | bytes 294920 | tf_op jit(solution)/shard_map/ppermute | solution.py:228
  66.1 4.2 %collective-permute-start.9 = (bf16[2,4,48,128]{3,2,1,0:T(8,128)(2,1)}, bf16[2,4,48,128]{3,2,1,0:T(8,128)(2,1)S(1)}, u32[]{:S(2)}, u32[]{:S(2)}) collective-permute-start(bf16[2,4,48,128]{3,2,1,0:T(8,128)(2,1)} %select.7.refs_8_), channel_id=1, source_target_pairs={{4,8},{8,4},{5,9},{9,5},{6,10},{10,6},{7,11},{11,7},{20,24},{24,20... | collective-permute-start | bytes 294920 | tf_op jit(solution)/shard_map/ppermute | solution.py:230
  70.3 1.3 %collective-permute-start.16 = (bf16[2,4,48,128]{3,2,1,0:T(8,128)(2,1)}, bf16[2,4,48,128]{3,2,1,0:T(8,128)(2,1)S(1)}, u32[]{:S(2)}, u32[]{:S(2)}) collective-permute-start(bf16[2,4,48,128]{3,2,1,0:T(8,128)(2,1)} %copy-done.16), channel_id=1, source_target_pairs={{8,12},{4,0},{9,13},{5,1},{10,14},{6,2},{11,15},{7,3},{24,28},{20,... | collective-permute-start | bytes 294920 | tf_op jit(solution)/shard_map/ppermute | solution.py:231
  71.6 1.3 %collective-permute-start.10 = (bf16[2,4,48,128]{3,2,1,0:T(8,128)(2,1)}, bf16[2,4,48,128]{3,2,1,0:T(8,128)(2,1)S(1)}, u32[]{:S(2)}, u32[]{:S(2)}) collective-permute-start(bf16[2,4,48,128]{3,2,1,0:T(8,128)(2,1)} %collective-permute-done.6.refs_12_), channel_id=1, source_target_pairs={{8,12},{4,0},{9,13},{5,1},{10,14},{6,2},{11,15},{7,3},{24,28},{20,... | collective-permute-start | bytes 294920 | tf_op jit(solution)/shard_map/ppermute | solution.py:231
  72.9 0.7 copy-done.8
  73.7 0.9 copy-done.11
  74.5 0.9 copy-done.13
  75.4 0.9 copy-done.15
  76.3 5.2 %cross.3.refs_17_ = bf16[24,2,2,256,256]{4,3,2,1,0:T(8,128)(2,1)} custom-call(s32[4]{0:T(128)S(1)} %iota_xor_fusion.1.refs_0_, f32[2,128]{1,0:T(2,128)S(1)} %pad.7.refs_1_, bf16[128,128]{1,0:T(8,128)(2,1)S(1)} %copy-done.8, bf16[24,48,256]{2,1,0:T(8,128)(2,1)S(1)} %get-tuple-element.13.refs_1_.refs_3_, ...), custom_call_target="tpu_custom_call" | custom-call | tf_op jit(solution)/shard_map/cross/pallas_call | solution.py:282
  81.5 5.0 %cross.4.refs_17_ = bf16[24,2,2,256,256]{4,3,2,1,0:T(8,128)(2,1)} custom-call(s32[4]{0:T(128)S(1)} %iota_xor_fusion.1.refs_0_, f32[2,128]{1,0:T(2,128)S(1)} %pad.7.refs_1_, bf16[128,128]{1,0:T(8,128)(2,1)S(1)} %copy-done.8, bf16[24,48,256]{2,1,0:T(8,128)(2,1)S(1)} %get-tuple-element.13.refs_1_.refs_3_, ...), custom_call_target="tpu_custom_call", output_to_operand_aliasing={{}: (17, {})} | custom-call | tf_op jit(solution)/shard_map/cross/pallas_call | solution.py:282
  86.6 5.1 %cross.5 = bf16[24,2,2,256,256]{4,3,2,1,0:T(8,128)(2,1)} custom-call(s32[4]{0:T(128)S(1)} %iota_xor_fusion.1.refs_0_, f32[2,128]{1,0:T(2,128)S(1)} %pad.7.refs_1_, bf16[128,128]{1,0:T(8,128)(2,1)S(1)} %copy-done.8, bf16[24,48,256]{2,1,0:T(8,128)(2,1)S(1)} %get-tuple-element.13.refs_1_.refs_3_, ...), custom_call_target="tpu_custom_call", output_to_operand_aliasing={{}: (17, {})} | custom-call | tf_op jit(solution)/shard_map/cross/pallas_call | solution.py:282
  (64 shorter events, 1.9 us)
Async XLA Ops:
  0.0 0.9 %copy-start.9 = (bf16[4,48,512]{2,1,0:T(8,128)(2,1)S(1)}, bf16[4,48,512]{2,1,0:T(8,128)(2,1)}, u32[]{:S(2)}) copy-start(bf16[4,48,512]{2,1,0:T(8,128)(2,1)} %constant.42.clone.refs_2_) | copy-start | bytes 589828
  0.9 0.8 copy-start.20
  11.5 5.8 %collective-permute-start = (bf16[24,48,256]{2,1,0:T(8,128)(2,1)S(1)}, bf16[24,48,256]{2,1,0:T(8,128)(2,1)S(1)}, u32[]{:S(2)}, u32[]{:S(2)}) collective-permute-start(bf16[24,48,256]{2,1,0:T(8,128)(2,1)S(1)} %get-tuple-element.14), channel_id=1, source_target_pairs={{0,1},{1,0},{2,3},{3,2},{4,5},{5,4},{6,7},{7,6},{8,9},{9,8},{10,11... | collective-permute-start | bytes 1769480 | tf_op jit(solution)/shard_map/ppermute | solution.py:205
  11.5 7.9 %collective-permute-start.17 = (bf16[8,48,256]{2,1,0:T(8,128)(2,1)}, bf16[8,48,256]{2,1,0:T(8,128)(2,1)S(1)}, u32[]{:S(2)}, u32[]{:S(2)}) collective-permute-start(bf16[8,48,256]{2,1,0:T(8,128)(2,1)} %get-tuple-element.19), channel_id=1, source_target_pairs={{0,2},{1,3},{2,0},{3,1},{4,6},{5,7},{6,4},{7,5},{8,10},{9,11},{10,... | collective-permute-start | bytes 589832 | tf_op jit(solution)/shard_map/ppermute | solution.py:205
  13.0 9.9 %collective-permute-start.18 = (bf16[8,48,256]{2,1,0:T(8,128)(2,1)}, bf16[8,48,256]{2,1,0:T(8,128)(2,1)S(1)}, u32[]{:S(2)}, u32[]{:S(2)}) collective-permute-start(bf16[8,48,256]{2,1,0:T(8,128)(2,1)} %get-tuple-element.20), channel_id=1, source_target_pairs={{0,3},{1,2},{2,1},{3,0},{4,7},{5,6},{6,5},{7,4},{8,11},{9,10},{10,... | collective-permute-start | bytes 589832 | tf_op jit(solution)/shard_map/ppermute | solution.py:205
  13.3 14.5 %collective-permute-start.11 = (bf16[8,48,256]{2,1,0:T(8,128)(2,1)}, bf16[8,48,256]{2,1,0:T(8,128)(2,1)S(1)}, u32[]{:S(2)}, u32[]{:S(2)}) collective-permute-start(bf16[8,48,256]{2,1,0:T(8,128)(2,1)} %get-tuple-element.17), channel_id=1, source_target_pairs={{0,2},{1,3},{2,0},{3,1},{4,6},{5,7},{6,4},{7,5},{8,10},{9,11},{10,... | collective-permute-start | bytes 589832 | tf_op jit(solution)/shard_map/ppermute | solution.py:205
  14.8 16.4 %collective-permute-start.12 = (bf16[8,48,256]{2,1,0:T(8,128)(2,1)}, bf16[8,48,256]{2,1,0:T(8,128)(2,1)S(1)}, u32[]{:S(2)}, u32[]{:S(2)}) collective-permute-start(bf16[8,48,256]{2,1,0:T(8,128)(2,1)} %get-tuple-element.18), channel_id=1, source_target_pairs={{0,3},{1,2},{2,1},{3,0},{4,7},{5,6},{6,5},{7,4},{8,11},{9,10},{10,... | collective-permute-start | bytes 589832 | tf_op jit(solution)/shard_map/ppermute | solution.py:205
  17.3 19.0 %collective-permute-start.1 = (bf16[8,48,256]{2,1,0:T(8,128)(2,1)S(1)}, bf16[8,48,256]{2,1,0:T(8,128)(2,1)S(1)}, u32[]{:S(2)}, u32[]{:S(2)}) collective-permute-start(bf16[8,48,256]{2,1,0:T(8,128)(2,1)S(1)} %get-tuple-element.15), channel_id=1, source_target_pairs={{0,2},{1,3},{2,0},{3,1},{4,6},{5,7},{6,4},{7,5},{8,10},{9,11},{10,... | collective-permute-start | bytes 589832 | tf_op jit(solution)/shard_map/ppermute | solution.py:205
  19.4 29.9 %collective-permute-start.5 = (bf16[2,12,48,128]{3,2,1,0:T(8,128)(2,1)S(1)}, bf16[2,12,48,128]{3,2,1,0:T(8,128)(2,1)S(1)}, u32[]{:S(2)}, u32[]{:S(2)}) collective-permute-start(bf16[2,12,48,128]{3,2,1,0:T(8,128)(2,1)S(1)} %select.6.refs_7_), channel_id=1, source_target_pairs={{0,8},{4,12},{8,0},{12,4},{1,9},{5,13},{9,1},{13,5},{2,10},{6,14},... | collective-permute-start | bytes 884744 | tf_op jit(solution)/shard_map/ppermute | solution.py:229
  22.8 18.4 %collective-permute-start.2 = (bf16[8,48,256]{2,1,0:T(8,128)(2,1)S(1)}, bf16[8,48,256]{2,1,0:T(8,128)(2,1)S(1)}, u32[]{:S(2)}, u32[]{:S(2)}) collective-permute-start(bf16[8,48,256]{2,1,0:T(8,128)(2,1)S(1)} %get-tuple-element.16), channel_id=1, source_target_pairs={{0,3},{1,2},{2,1},{3,0},{4,7},{5,6},{6,5},{7,4},{8,11},{9,10},{10,... | collective-permute-start | bytes 589832 | tf_op jit(solution)/shard_map/ppermute | solution.py:205
  27.8 15.1 %collective-permute-start.20 = (bf16[2,4,48,128]{3,2,1,0:T(8,128)(2,1)S(1)}, bf16[2,4,48,128]{3,2,1,0:T(8,128)(2,1)S(1)}, u32[]{:S(2)}, u32[]{:S(2)}) collective-permute-start(bf16[2,4,48,128]{3,2,1,0:T(8,128)(2,1)S(1)} %select.9.refs_8_), channel_id=1, source_target_pairs={{0,8},{4,12},{8,0},{12,4},{1,9},{5,13},{9,1},{13,5},{2,10},{6,14},... | collective-permute-start | bytes 294920 | tf_op jit(solution)/shard_map/ppermute | solution.py:229
  31.3 12.6 %collective-permute-start.19 = (bf16[2,4,48,128]{3,2,1,0:T(8,128)(2,1)S(1)}, bf16[2,4,48,128]{3,2,1,0:T(8,128)(2,1)S(1)}, u32[]{:S(2)}, u32[]{:S(2)}) collective-permute-start(bf16[2,4,48,128]{3,2,1,0:T(8,128)(2,1)S(1)} %select.9.refs_8_), channel_id=1, source_target_pairs={{0,4},{4,0},{8,12},{12,8},{1,5},{5,1},{9,13},{13,9},{2,6},{6,2},{1... | collective-permute-start | bytes 294920 | tf_op jit(solution)/shard_map/ppermute | solution.py:228
  36.2 0.7 copy-start
  36.9 8.7 %collective-permute-start.21 = (bf16[2,4,48,128]{3,2,1,0:T(8,128)(2,1)S(1)}, bf16[2,4,48,128]{3,2,1,0:T(8,128)(2,1)S(1)}, u32[]{:S(2)}, u32[]{:S(2)}) collective-permute-start(bf16[2,4,48,128]{3,2,1,0:T(8,128)(2,1)S(1)} %select.9.refs_8_), channel_id=1, source_target_pairs={{4,8},{8,4},{5,9},{9,5},{6,10},{10,6},{7,11},{11,7},{20,24},{24,20... | collective-permute-start | bytes 294920 | tf_op jit(solution)/shard_map/ppermute | solution.py:230
  41.3 12.1 %copy-start.6 = (bf16[2,4,48,128]{3,2,1,0:T(8,128)(2,1)}, bf16[2,4,48,128]{3,2,1,0:T(8,128)(2,1)S(1)}, u32[]{:S(2)}) copy-start(bf16[2,4,48,128]{3,2,1,0:T(8,128)(2,1)S(1)} %select.8.refs_8_) | copy-start | bytes 294916
  41.3 0.7 copy-start.3
  42.0 11.4 %collective-permute-start.14 = (bf16[2,4,48,128]{3,2,1,0:T(8,128)(2,1)S(1)}, bf16[2,4,48,128]{3,2,1,0:T(8,128)(2,1)S(1)}, u32[]{:S(2)}, u32[]{:S(2)}) collective-permute-start(bf16[2,4,48,128]{3,2,1,0:T(8,128)(2,1)S(1)} %select.8.refs_8_), channel_id=1, source_target_pairs={{0,8},{4,12},{8,0},{12,4},{1,9},{5,13},{9,1},{13,5},{2,10},{6,14},... | collective-permute-start | bytes 294920 | tf_op jit(solution)/shard_map/ppermute | solution.py:229
  43.0 0.9 %copy-start.10 = (bf16[2,4,48,128]{3,2,1,0:T(8,128)(2,1)}, bf16[2,4,48,128]{3,2,1,0:T(8,128)(2,1)S(1)}, u32[]{:S(2)}) copy-start(bf16[2,4,48,128]{3,2,1,0:T(8,128)(2,1)S(1)} %collective-permute-done.20.refs_12_) | copy-start | bytes 294916
  43.0 10.5 %collective-permute-start.13 = (bf16[2,4,48,128]{3,2,1,0:T(8,128)(2,1)S(1)}, bf16[2,4,48,128]{3,2,1,0:T(8,128)(2,1)S(1)}, u32[]{:S(2)}, u32[]{:S(2)}) collective-permute-start(bf16[2,4,48,128]{3,2,1,0:T(8,128)(2,1)S(1)} %select.8.refs_8_), channel_id=1, source_target_pairs={{0,4},{4,0},{8,12},{12,8},{1,5},{5,1},{9,13},{13,9},{2,6},{6,2},{1... | collective-permute-start | bytes 294920 | tf_op jit(solution)/shard_map/ppermute | solution.py:228
  43.9 0.6 copy-start.12
  44.5 21.5 %collective-permute-start.3 = (bf16[2,12,48,128]{3,2,1,0:T(8,128)(2,1)S(1)}, bf16[2,12,48,128]{3,2,1,0:T(8,128)(2,1)S(1)}, u32[]{:S(2)}, u32[]{:S(2)}) collective-permute-start(bf16[2,12,48,128]{3,2,1,0:T(8,128)(2,1)S(1)} %select.6.refs_7_), channel_id=1, source_target_pairs={{0,4},{4,0},{8,12},{12,8},{1,5},{5,1},{9,13},{13,9},{2,6},{6,2},{1... | collective-permute-start | bytes 884744 | tf_op jit(solution)/shard_map/ppermute | solution.py:228
  45.6 0.6 copy-start.14
  46.3 24.0 %collective-permute-start.7 = (bf16[2,12,48,128]{3,2,1,0:T(8,128)(2,1)S(1)}, bf16[2,12,48,128]{3,2,1,0:T(8,128)(2,1)S(1)}, u32[]{:S(2)}, u32[]{:S(2)}) collective-permute-start(bf16[2,12,48,128]{3,2,1,0:T(8,128)(2,1)S(1)} %select.6.refs_7_), channel_id=1, source_target_pairs={{4,8},{8,4},{5,9},{9,5},{6,10},{10,6},{7,11},{11,7},{20,24},{24,20... | collective-permute-start | bytes 884744 | tf_op jit(solution)/shard_map/ppermute | solution.py:230
  49.3 22.2 %collective-permute-start.8 = (bf16[2,12,48,128]{3,2,1,0:T(8,128)(2,1)S(1)}, bf16[2,12,48,128]{3,2,1,0:T(8,128)(2,1)S(1)}, u32[]{:S(2)}, u32[]{:S(2)}) collective-permute-start(bf16[2,12,48,128]{3,2,1,0:T(8,128)(2,1)S(1)} %collective-permute-done.5.refs_11_), channel_id=1, source_target_pairs={{8,12},{4,0},{9,13},{5,1},{10,14},{6,2},{11,15},{7,3},{24,28},{20,... | collective-permute-start | bytes 884744 | tf_op jit(solution)/shard_map/ppermute | solution.py:231
  50.7 0.9 %copy-start.1 = (bf16[8,48,256]{2,1,0:T(8,128)(2,1)S(1)}, bf16[8,48,256]{2,1,0:T(8,128)(2,1)}, u32[]{:S(2)}) copy-start(bf16[8,48,256]{2,1,0:T(8,128)(2,1)} %copy-done) | copy-start | bytes 589828
  51.6 0.9 %copy-start.4 = (bf16[8,48,256]{2,1,0:T(8,128)(2,1)S(1)}, bf16[8,48,256]{2,1,0:T(8,128)(2,1)}, u32[]{:S(2)}) copy-start(bf16[8,48,256]{2,1,0:T(8,128)(2,1)} %copy-done.3) | copy-start | bytes 589828
  53.4 0.6 copy-start.16
  53.4 6.0 %collective-permute-start.6 = (bf16[2,4,48,128]{3,2,1,0:T(8,128)(2,1)}, bf16[2,4,48,128]{3,2,1,0:T(8,128)(2,1)}, u32[]{:S(2)}, u32[]{:S(2)}) collective-permute-start(bf16[2,4,48,128]{3,2,1,0:T(8,128)(2,1)} %select.7.refs_8_), channel_id=1, source_target_pairs={{0,8},{4,12},{8,0},{12,4},{1,9},{5,13},{9,1},{13,5},{2,10},{6,14},... | collective-permute-start | bytes 294920 | tf_op jit(solution)/shard_map/ppermute | solution.py:229
  54.0 0.6 copy-start.18
  54.7 8.9 %collective-permute-start.22 = (bf16[2,4,48,128]{3,2,1,0:T(8,128)(2,1)}, bf16[2,4,48,128]{3,2,1,0:T(8,128)(2,1)}, u32[]{:S(2)}, u32[]{:S(2)}) collective-permute-start(bf16[2,4,48,128]{3,2,1,0:T(8,128)(2,1)} %copy-done.10), channel_id=1, source_target_pairs={{8,12},{4,0},{9,13},{5,1},{10,14},{6,2},{11,15},{7,3},{24,28},{20,... | collective-permute-start | bytes 294920 | tf_op jit(solution)/shard_map/ppermute | solution.py:231
  59.2 22.3 %copy-start.7 = (bf16[2,4,48,128]{3,2,1,0:T(8,128)(2,1)S(1)}, bf16[2,4,48,128]{3,2,1,0:T(8,128)(2,1)}, u32[]{:S(2)}) copy-start(bf16[2,4,48,128]{3,2,1,0:T(8,128)(2,1)} %copy-done.6) | copy-start | bytes 294916
  59.4 22.1 %collective-permute-start.15 = (bf16[2,4,48,128]{3,2,1,0:T(8,128)(2,1)}, bf16[2,4,48,128]{3,2,1,0:T(8,128)(2,1)S(1)}, u32[]{:S(2)}, u32[]{:S(2)}) collective-permute-start(bf16[2,4,48,128]{3,2,1,0:T(8,128)(2,1)} %copy-done.6), channel_id=1, source_target_pairs={{4,8},{8,4},{5,9},{9,5},{6,10},{10,6},{7,11},{11,7},{20,24},{24,20... | collective-permute-start | bytes 294920 | tf_op jit(solution)/shard_map/ppermute | solution.py:230
  63.6 22.9 %collective-permute-start.4 = (bf16[2,4,48,128]{3,2,1,0:T(8,128)(2,1)}, bf16[2,4,48,128]{3,2,1,0:T(8,128)(2,1)S(1)}, u32[]{:S(2)}, u32[]{:S(2)}) collective-permute-start(bf16[2,4,48,128]{3,2,1,0:T(8,128)(2,1)} %select.7.refs_8_), channel_id=1, source_target_pairs={{0,4},{4,0},{8,12},{12,8},{1,5},{5,1},{9,13},{13,9},{2,6},{6,2},{1... | collective-permute-start | bytes 294920 | tf_op jit(solution)/shard_map/ppermute | solution.py:228
  66.1 20.5 %collective-permute-start.9 = (bf16[2,4,48,128]{3,2,1,0:T(8,128)(2,1)}, bf16[2,4,48,128]{3,2,1,0:T(8,128)(2,1)S(1)}, u32[]{:S(2)}, u32[]{:S(2)}) collective-permute-start(bf16[2,4,48,128]{3,2,1,0:T(8,128)(2,1)} %select.7.refs_8_), channel_id=1, source_target_pairs={{4,8},{8,4},{5,9},{9,5},{6,10},{10,6},{7,11},{11,7},{20,24},{24,20... | collective-permute-start | bytes 294920 | tf_op jit(solution)/shard_map/ppermute | solution.py:230
  70.3 11.2 %collective-permute-start.16 = (bf16[2,4,48,128]{3,2,1,0:T(8,128)(2,1)}, bf16[2,4,48,128]{3,2,1,0:T(8,128)(2,1)S(1)}, u32[]{:S(2)}, u32[]{:S(2)}) collective-permute-start(bf16[2,4,48,128]{3,2,1,0:T(8,128)(2,1)} %copy-done.16), channel_id=1, source_target_pairs={{8,12},{4,0},{9,13},{5,1},{10,14},{6,2},{11,15},{7,3},{24,28},{20,... | collective-permute-start | bytes 294920 | tf_op jit(solution)/shard_map/ppermute | solution.py:231
  71.6 15.0 %collective-permute-start.10 = (bf16[2,4,48,128]{3,2,1,0:T(8,128)(2,1)}, bf16[2,4,48,128]{3,2,1,0:T(8,128)(2,1)S(1)}, u32[]{:S(2)}, u32[]{:S(2)}) collective-permute-start(bf16[2,4,48,128]{3,2,1,0:T(8,128)(2,1)} %collective-permute-done.6.refs_12_), channel_id=1, source_target_pairs={{8,12},{4,0},{9,13},{5,1},{10,14},{6,2},{11,15},{7,3},{24,28},{20,... | collective-permute-start | bytes 294920 | tf_op jit(solution)/shard_map/ppermute | solution.py:231
  72.9 0.8 copy-start.8
  73.7 0.9 copy-start.11
  74.5 0.9 copy-start.13
  75.4 0.9 copy-start.15
  76.3 5.2 %copy-start.17 = (bf16[2,4,48,128]{3,2,1,0:T(8,128)(2,1)S(1)}, bf16[2,4,48,128]{3,2,1,0:T(8,128)(2,1)}, u32[]{:S(2)}) copy-start(bf16[2,4,48,128]{3,2,1,0:T(8,128)(2,1)} %copy-done.16) | copy-start | bytes 294916
  76.3 5.2 %copy-start.19 = (bf16[2,4,48,128]{3,2,1,0:T(8,128)(2,1)S(1)}, bf16[2,4,48,128]{3,2,1,0:T(8,128)(2,1)}, u32[]{:S(2)}) copy-start(bf16[2,4,48,128]{3,2,1,0:T(8,128)(2,1)} %copy-done.18) | copy-start | bytes 294916
  81.5 5.1 %copy-start.2 = (bf16[8,48,256]{2,1,0:T(8,128)(2,1)S(1)}, bf16[8,48,256]{2,1,0:T(8,128)(2,1)}, u32[]{:S(2)}) copy-start(bf16[8,48,256]{2,1,0:T(8,128)(2,1)} %copy-done) | copy-start | bytes 589828
  81.5 5.1 %copy-start.5 = (bf16[8,48,256]{2,1,0:T(8,128)(2,1)S(1)}, bf16[8,48,256]{2,1,0:T(8,128)(2,1)}, u32[]{:S(2)}) copy-start(bf16[8,48,256]{2,1,0:T(8,128)(2,1)} %copy-done.3) | copy-start | bytes 589828

commit v2 on v1

v2 whole, which is shorter than its diff:
```python
import math

import jax
import jax.numpy as jnp
import numpy as np
import ml_dtypes
from jax import lax
from jax.experimental import pallas as pl
from jax.experimental.pallas import tpu as pltpu
from jax.sharding import PartitionSpec as P

F = 96
K0 = 8
G = 2
PARTS = (2, 1)
f32 = jnp.float32
bf16 = jnp.bfloat16


def make_table(length):
    freqs = K0 + np.arange(F)
    phase = freqs[:, None] * np.arange(length)[None, :] % length
    angle = phase.astype(np.float32) * np.float32(2.0 * math.pi / length)
    scale = np.float32(1.0 / math.sqrt(length))
    table = np.stack([np.cos(angle) * scale, -np.sin(angle) * scale], axis=1)
    return table.astype(np.float32).astype(ml_dtypes.bfloat16)


def up(n, m):
    return -(-n // m) * m


def chunk_sizes(bins):
    sizes = [bins * part // sum(PARTS) for part in PARTS]
    return sizes[:-1] + [bins - sum(sizes[:-1])]


def head_kernel(cfg, order, samples_hbm, table_hbm, *refs):
    win, wpad, n_tf, bins, sizes = cfg
    outs, (samples, table, tscr, spec, sem) = refs[:-5], refs[-5:]
    copies = [
        pltpu.make_async_copy(table_hbm, table, sem.at[0]),
        pltpu.make_async_copy(samples_hbm, samples, sem.at[1]),
    ]
    for copy in copies:
        copy.start()
    to = lax.broadcasted_iota(jnp.int32, (128, 128), 0)
    at = lax.broadcasted_iota(jnp.int32, (128, 128), 1)
    shuffle = ((to % 8 == at // 16) & (to // 8 == at % 16)).astype(f32).astype(bf16)
    for w in range(win, wpad):
        spec[w] = jnp.zeros(spec.shape[1:], bf16)
    copies[0].wait()
    rows = [table[order[k]].astype(f32) for k in range(n_tf)]
    tscr[...] = jnp.concatenate(rows, axis=0).astype(bf16)
    copies[1].wait()
    for w in range(win):
        x = samples[w]
        xf = x.astype(f32)
        power = jnp.mean(xf * xf, axis=0, keepdims=True)
        y = jnp.dot(tscr[...], x, preferred_element_type=f32)
        spec[w] = (y * lax.rsqrt(power + 1e-06)).astype(bf16)
    for grp in range(2 * F // 16):
        parts = []
        for wg in range(wpad // 8):
            block = spec[8 * wg : 8 * wg + 8, 16 * grp : 16 * grp + 16, :]
            block = block.reshape(128, block.shape[-1])
            parts.append(jnp.dot(shuffle, block, preferred_element_type=f32))
        for j in range(8):
            flat = grp * 8 + j
            k, f = flat // bins, flat % bins
            pieces = []
            for r in range(2):
                row = (2 * j + r) * 8
                pieces += [p[row : row + 8] for p in parts]
            value = jnp.concatenate(pieces, axis=0).astype(bf16)
            if k < 2:
                outs[k][f] = value
            else:
                q = 0
                while f >= sizes[q]:
                    f, q = f - sizes[q], q + 1
                outs[2 + (k - 2) * len(sizes) + q][f] = value


def select_kernel(wpad, cols, *refs):
    slabs, out = refs[:-1], refs[-1]
    bins, rows, chans = slabs[0].shape
    lanes = cols.shape[1]
    pick = (lax.broadcasted_iota(jnp.int32, (chans, lanes), 0) == cols[...]).astype(f32).astype(bf16)
    real = lax.broadcasted_iota(jnp.int32, (wpad, lanes), 1) < lanes // 2
    for d, slab in enumerate(slabs):
        def body(p, _, d=d, slab=slab):
            flat = slab[pl.ds(2 * p, 2)].reshape(2 * rows, chans)
            got = jnp.dot(flat, pick, preferred_element_type=f32)
            both = []
            for j in range(2):
                base = j * rows
                both.append(jnp.where(real, got[base : base + wpad], got[base + wpad : base + rows]))
            out[d, p] = jnp.concatenate(both, axis=0).astype(bf16)
            return 0

        lax.fori_loop(0, bins // 2, body, 0, unroll=True)


def cross_kernel(cfg, blk, coef, eye, *refs):
    wpad, kpad, scale, n_slab, counts, lead = cfg
    out, buf, sem = refs[-3:]
    slabs, rest = refs[:n_slab], refs[n_slab:-3]
    panels = []
    for near, far in counts:
        panels.append((rest[:near], rest[near : near + far]))
        rest = rest[near + far :]
    n_blk = len(panels)
    lanes = panels[0][0][0].shape[-1]
    src = lanes // 2
    chans = slabs[0].shape[-1]
    used = wpad * n_slab
    pairs = buf.shape[0]

    def copy_out(p, b):
        at = pl.ds(pl.multiple_of(blk[b] * src, src), src)
        return pltpu.make_async_copy(
            buf.at[p, :, :, :, pl.ds(b * src, src), :],
            out.at[pl.ds(2 * (lead + p), 2), :, :, at, :],
            sem.at[p, b],
        )

    def loaded(group, d, at):
        value = group[0][d, at].astype(f32)
        for other in group[1:]:
            value = value + other[d, at].astype(f32)
        return value

    def pair(p, _):
        stacks = [[], []]
        for near, far in panels:
            for group, at in ((near, lead + p), (far, p)):
                for d in range(group[0].shape[0]):
                    value = loaded(group, d, at)
                    for j in range(2):
                        stacks[j].append(value[j * wpad : (j + 1) * wpad])
            if kpad > used:
                for j in range(2):
                    stacks[j].append(jnp.zeros((kpad - used, lanes), f32))
        for j in range(2):
            re, im = [], []
            for i, slab in enumerate(slabs):
                v = slab[2 * ((lead if i < 2 else 0) + p) + j].astype(f32)
                re.append(v[:wpad])
                im.append(v[wpad:])
            if kpad > used:
                pad = [jnp.zeros((kpad - used, chans), f32)]
                re, im = re + pad, im + pad
            re = jnp.concatenate(re, axis=0)
            im = jnp.concatenate(im, axis=0)
            right = jnp.concatenate(
                [jnp.concatenate([re, im], axis=1), jnp.concatenate([im, -re], axis=1)], axis=0
            ).astype(bf16)
            stacked = jnp.concatenate(stacks[j], axis=0).astype(bf16)
            turned = lax.dot_general(
                eye[...], stacked, (((1,), (1,)), ((), ())), preferred_element_type=f32
            )
            rows = []
            for g in range(G):
                weight = coef[g : g + 1, :]
                for b in range(n_blk):
                    t = turned[:, b * kpad : (b + 1) * kpad] * weight
                    rows.append(jnp.concatenate([t[:src], t[src:]], axis=1))
            left = jnp.concatenate(rows, axis=0).astype(bf16)
            got = (jnp.dot(left, right, preferred_element_type=f32) * scale).astype(bf16)
            tall = n_blk * src
            for g in range(G):
                for o in range(2):
                    buf[p, j, g, o] = got[g * tall : (g + 1) * tall, o * chans : (o + 1) * chans]
        for b in range(n_blk):
            copy_out(p, b).start()
        return 0

    lax.fori_loop(0, pairs, pair, 0)
    for p in range(pairs):
        for b in range(n_blk):
            copy_out(p, b).wait()


def shards(samples, quality, substack, sources):
    win, length, chans = samples.shape
    n_tf = lax.axis_size("tf")
    n_chan = lax.axis_size("chan")
    me = lax.axis_index("tf")
    pos = lax.axis_index("chan")
    bins = F // n_tf
    src = sources.shape[0] // n_chan
    wpad = up(win, 8)
    kpad = up(wpad * n_tf, 128)
    sizes = chunk_sizes(bins)
    chunks = len(sizes)
    rows = 2 * wpad
    order = (me ^ jnp.arange(n_tf, dtype=jnp.int32)).astype(jnp.int32)
    table = jnp.asarray(make_table(length).reshape(n_tf, 2 * bins, length))
    smem = pl.BlockSpec(memory_space=pltpu.SMEM)
    vmem = pl.BlockSpec(memory_space=pltpu.VMEM)
    hbm = pl.BlockSpec(memory_space=pltpu.HBM)

    shapes = [jax.ShapeDtypeStruct((bins, rows, chans), bf16)] * 2
    for _ in range(n_tf - 2):
        shapes += [jax.ShapeDtypeStruct((size, rows, chans), bf16) for size in sizes]
    got = pl.pallas_call(
        lambda *refs: head_kernel((win, wpad, n_tf, bins, sizes), *refs),
        in_specs=[smem, hbm, hbm],
        out_specs=[vmem] * len(shapes),
        out_shape=shapes,
        scratch_shapes=[
            pltpu.VMEM(samples.shape, bf16),
            pltpu.VMEM(table.shape, bf16),
            pltpu.VMEM((2 * F, length), bf16),
            pltpu.VMEM((wpad, 2 * F, chans), bf16),
            pltpu.SemaphoreType.DMA((2,)),
        ],
        compiler_params=pltpu.CompilerParams(vmem_limit_bytes=20 * 1024 * 1024),
        name="head",
    )(order, samples, table)
    own, for_core = got[0], got[1]

    def across(value, k):
        return lax.ppermute(value, "tf", [(i, i ^ k) for i in range(n_tf)])

    core = across(for_core, 1)
    far = [
        [across(got[2 + (k - 2) * chunks + q], k) for k in range(2, n_tf)] for q in range(chunks)
    ]

    mine = lax.dynamic_slice_in_dim(sources, pos * src, src, 0) - pos * chans
    cols = jnp.concatenate([mine, mine])[None, :]

    def select(slabs):
        count = slabs[0].shape[0]
        return pl.pallas_call(
            lambda *refs: select_kernel(wpad, *refs),
            in_specs=[vmem] * (1 + len(slabs)),
            out_specs=vmem,
            out_shape=jax.ShapeDtypeStruct((len(slabs), count // 2, 2 * wpad, 2 * src), bf16),
            compiler_params=pltpu.CompilerParams(vmem_limit_bytes=12 * 1024 * 1024),
            name="select",
        )(cols, *slabs)

    def spread(panel):
        if n_chan == 4:
            one = lax.ppermute(panel, "chan", [(i, i ^ 1) for i in range(4)])
            two = lax.ppermute(panel, "chan", [(i, i ^ 2) for i in range(4)])
            mid = lax.ppermute(panel, "chan", [(1, 2), (2, 1)])
            end = lax.ppermute(two, "chan", [(2, 3), (1, 0)])
            return [[panel], [one], [two], [mid, end]]
        return [[panel]] + [
            [lax.ppermute(panel, "chan", [(i, (i + k) % n_chan) for i in range(n_chan)])]
            for k in range(1, n_chan)
        ]

    if n_chan == 4:
        blk = pos ^ jnp.arange(4, dtype=jnp.int32)
    else:
        blk = (pos - jnp.arange(n_chan, dtype=jnp.int32)) % n_chan
    blk = blk.astype(jnp.int32)

    coef = jnp.where(
        substack[None, :] == jnp.arange(G, dtype=jnp.int32)[:, None],
        (quality[None, :].astype(f32) + 1.0) / 4.0,
        0.0,
    ).reshape(G, n_tf, win)
    coef = jnp.pad(coef, ((0, 0), (0, 0), (0, wpad - win)))
    coef = jnp.take(coef, order, axis=1).reshape(G, n_tf * wpad)
    coef = jnp.pad(coef, ((0, 0), (0, kpad - n_tf * wpad)))
    eye = jnp.asarray(np.eye(2 * src, dtype=np.float32).astype(ml_dtypes.bfloat16))
    scale = 1.0 / math.sqrt(win * n_tf)

    near = spread(select([own, core]))
    away = [spread(select(far[q])) for q in range(chunks)]
    out_shape = jax.ShapeDtypeStruct((bins, G, 2, src * n_chan, chans), bf16)
    groups = [[0, 1, 2], [3]] if n_chan == 4 else [list(range(n_chan))]
    stacks = None
    for q, size in enumerate(sizes):
        for group in groups:
            pairs = size // 2
            args, counts = [own, core] + far[q], []
            for b in group:
                args += near[b] + away[q][b]
                counts.append((len(near[b]), len(away[q][b])))
            cfg = (wpad, kpad, scale, n_tf, counts, sum(sizes[:q]) // 2)
            first = stacks is None
            extra = [] if first else [stacks]

            def body(*refs, cfg=cfg, first=first):
                cross_kernel(cfg, *(refs if first else refs[:-4] + refs[-3:]))

            stacks = pl.pallas_call(
                body,
                in_specs=[smem] + [vmem] * (2 + len(args)) + [hbm] * len(extra),
                out_specs=hbm,
                out_shape=out_shape,
                scratch_shapes=[
                    pltpu.VMEM((pairs, 2, G, 2, len(group) * src, chans), bf16),
                    pltpu.SemaphoreType.DMA((pairs, len(group))),
                ],
                input_output_aliases={} if first else {3 + len(args): 0},
                compiler_params=pltpu.CompilerParams(vmem_limit_bytes=20 * 1024 * 1024),
                name="cross",
            )(blk[np.array(group)], coef, eye, *args, *extra)
    return stacks


def solution(mesh):
    in_specs = (P(("day", "tf"), None, "chan"), P("day"), P("day"), P())
    out_specs = P("tf", "day", None, None, "chan")
    return jax.shard_map(shards, mesh=mesh, in_specs=in_specs, out_specs=out_specs, check_vma=False)
```

time: 92.6 us -> 90.1 us (0.973)
  the two profiles are of different devices: /device:TPU:8 before, /device:TPU:16 now
where the time goes in v2:
time: 90.1 us; the launch traced here: 89.6 us
  Pallas kernels  28.8 us (32%)
  starting transfers between devices  26.4 us (29%)
  waiting for transfers between devices  25.5 us (28%)
  local copies, waits for them, and re-layouts  7.06 us (8%)
  other arithmetic  1.6 us (2%)
    pallas_call x4, Pallas kernels, shards(): pl.pallas_call(body, in_specs=[smem] + [vmem] * (2 + len(args)) + [hbm] *...  23.3 us
    ppermute x5, waiting for transfers between devices, across(): return lax.ppermute(value, 'tf', [(i, i ^ k) for i in range(n_tf)])  18 us
    ppermute x3, starting transfers between devices, spread(): mid = lax.ppermute(panel, 'chan', [(1, 2), (2, 1)])  8.5 us
    ppermute x3, starting transfers between devices, spread(): end = lax.ppermute(two, 'chan', [(2, 3), (1, 0)])  8.37 us
    ppermute x3, starting transfers between devices, spread(): one = lax.ppermute(panel, 'chan', [(i, i ^ 1) for i in range(4)])  5.07 us
    ppermute x3, waiting for transfers between devices, spread(): end = lax.ppermute(two, 'chan', [(2, 3), (1, 0)])  5.02 us
    unnamed x14, local copies, waits for them, and re-layouts  4.33 us
    pallas_call x1, Pallas kernels, shards(): pl.pallas_call(lambda *refs: head_kernel((win, wpad, n_tf, bins, sizes),...  3.8 us
  transfers between devices with their start and end apart: 17, of which 6 were waited for; matrix products, arithmetic and copies ran while one was open for 5% of the time, Pallas kernels for 23%

profile of v2, /device:TPU:16, one launch (start us, length us, event | category | flops | bytes accessed | tf_op | source)
XLA Modules:
  0.0 89.6 jit_solution(17133044544816723916)
XLA Ops:
  0.0 2.6 %copy-done = bf16[22,512,256]{2,1,0:T(8,128)(2,1)S(1)} copy-done((bf16[22,512,256]{2,1,0:T(8,128)(2,1)S(1)}, bf16[22,512,256]{2,1,0:T(8,128)(2,1)}, u32[]{:S(2)}) %copy-start) | copy-done | bytes 5767192
  2.6 0.9 %copy-done.4 = bf16[4,48,512]{2,1,0:T(8,128)(2,1)S(1)} copy-done((bf16[4,48,512]{2,1,0:T(8,128)(2,1)S(1)}, bf16[4,48,512]{2,1,0:T(8,128)(2,1)}, u32[]{:S(2)}) %copy-start.4) | copy-done | bytes 196632
  3.6 3.8 %head.1 = (bf16[24,48,256]{2,1,0:T(8,128)(2,1)S(1)}, bf16[24,48,256]{2,1,0:T(8,128)(2,1)S(1)}, bf16[16,48,256]{2,1,0:T(8,128)(2,1)}, bf16[8,48,256]{2,1,0:T(8,12...) custom-call(s32[4]{0:T(128)S(1)} %iota_xor_fusion.refs_0_, bf16[22,512,256]{2,1,0:T(8,128)(2,1)S(1)} %copy-done, ...), custom_call_target="tpu_custom_call" | custom-call | tf_op jit(solution)/shard_map/head/pallas_call | solution.py:207
  7.4 0.1 collective-permute-start
  7.5 1.6 %collective-permute-start.11 = (bf16[16,48,256]{2,1,0:T(8,128)(2,1)}, bf16[16,48,256]{2,1,0:T(8,128)(2,1)S(1)}, u32[]{:S(2)}, u32[]{:S(2)}) collective-permute-start(bf16[16,48,256]{2,1,0:T(8,128)(2,1)} %get-tuple-element.15), channel_id=1, source_target_pairs={{0,2},{1,3},{2,0},{3,1},{4,6},{5,7},{6,4},{7,5},{8,10},{9,11},{10,... | collective-permute-start | bytes 1179656 | tf_op jit(solution)/shard_map/ppermute | solution.py:225
  9.0 0.3 collective-permute-start.12
  9.3 1.5 %collective-permute-start.1 = (bf16[8,48,256]{2,1,0:T(8,128)(2,1)}, bf16[8,48,256]{2,1,0:T(8,128)(2,1)S(1)}, u32[]{:S(2)}, u32[]{:S(2)}) collective-permute-start(bf16[8,48,256]{2,1,0:T(8,128)(2,1)} %get-tuple-element.13), channel_id=1, source_target_pairs={{0,2},{1,3},{2,0},{3,1},{4,6},{5,7},{6,4},{7,5},{8,10},{9,11},{10,... | collective-permute-start | bytes 589832 | tf_op jit(solution)/shard_map/ppermute | solution.py:225
  10.8 0.2 collective-permute-start.2
  11.0 0.7 add_multiply_fusion
  11.7 0.1 broadcast_in_dim.44
  11.8 0.7 eq.16
  12.5 0.8 dynamic-slice_subtract_fusion
  13.2 0.1 add_bitcast_fusion.refs_0_
  13.3 0.5 select.5.refs_7_
  13.8 0.2 collective-permute-start.4
  14.1 5.6 %collective-permute-done.11.refs_1_.refs_5_ = bf16[16,48,256]{2,1,0:T(8,128)(2,1)S(1)} collective-permute-done((bf16[16,48,256]{2,1,0:T(8,128)(2,1)}, bf16[16,48,256]{2,1,0:T(8,128)(2,1)S(1)}, u32[]{:S(2)}, u32[]{:S(2)}) %collective-permute-start.11) | collective-permute-done | bytes 393248 | tf_op jit(solution)/shard_map/ppermute | solution.py:225
  19.6 7.5 %collective-permute-done.12.refs_2_.refs_6_ = bf16[16,48,256]{2,1,0:T(8,128)(2,1)S(1)} collective-permute-done((bf16[16,48,256]{2,1,0:T(8,128)(2,1)S(1)}, bf16[16,48,256]{2,1,0:T(8,128)(2,1)S(1)}, u32[]{:S(2)}, u32[]{:S(2)}) %collective-permute-start.12) | collective-permute-done | bytes 393248 | tf_op jit(solution)/shard_map/ppermute | solution.py:225
  27.2 1.0 %select.7.refs_8_ = bf16[2,8,48,128]{3,2,1,0:T(8,128)(2,1)} custom-call(s32[1,128]{1,0:T(1,128)S(1)} %add_bitcast_fusion.refs_0_, bf16[16,48,256]{2,1,0:T(8,128)(2,1)S(1)} %collective-permute-done.11.refs_1_.refs_5_, bf16[16,48,256]{2,1,0:T(8,128)(2,1)S(1)} %collective-permute-done.12.refs_2_.refs_6_), custom_call_target="tpu_custom_call" | custom-call | tf_op jit(solution)/shard_map/select/pallas_call | solution.py:237
  28.2 0.3 collective-permute-start.14
  28.5 1.7 %collective-permute-start.16 = (bf16[2,8,48,128]{3,2,1,0:T(8,128)(2,1)}, bf16[2,8,48,128]{3,2,1,0:T(8,128)(2,1)}, u32[]{:S(2)}, u32[]{:S(2)}) collective-permute-start(bf16[2,8,48,128]{3,2,1,0:T(8,128)(2,1)} %select.7.refs_8_), channel_id=1, source_target_pairs={{0,4},{4,0},{8,12},{12,8},{1,5},{5,1},{9,13},{13,9},{2,6},{6,2},{1... | collective-permute-start | bytes 589832 | tf_op jit(solution)/shard_map/ppermute | solution.py:248
  30.1 0.6 gather_fusion
  30.7 1.6 %collective-permute-done.1.refs_1_.refs_5_ = bf16[8,48,256]{2,1,0:T(8,128)(2,1)S(1)} collective-permute-done((bf16[8,48,256]{2,1,0:T(8,128)(2,1)}, bf16[8,48,256]{2,1,0:T(8,128)(2,1)S(1)}, u32[]{:S(2)}, u32[]{:S(2)}) %collective-permute-start.1) | collective-permute-done | bytes 196640 | tf_op jit(solution)/shard_map/ppermute | solution.py:225
  32.3 3.3 %collective-permute-done.2.refs_2_.refs_6_ = bf16[8,48,256]{2,1,0:T(8,128)(2,1)S(1)} collective-permute-done((bf16[8,48,256]{2,1,0:T(8,128)(2,1)S(1)}, bf16[8,48,256]{2,1,0:T(8,128)(2,1)S(1)}, u32[]{:S(2)}, u32[]{:S(2)}) %collective-permute-start.2) | collective-permute-done | bytes 196640 | tf_op jit(solution)/shard_map/ppermute | solution.py:225
  35.6 0.3 select.6.refs_8_
  35.9 0.3 collective-permute-start.7
  36.2 4.7 %collective-permute-start.13 = (bf16[2,8,48,128]{3,2,1,0:T(8,128)(2,1)}, bf16[2,8,48,128]{3,2,1,0:T(8,128)(2,1)}, u32[]{:S(2)}, u32[]{:S(2)}) collective-permute-start(bf16[2,8,48,128]{3,2,1,0:T(8,128)(2,1)} %select.7.refs_8_), channel_id=1, source_target_pairs={{4,8},{8,4},{5,9},{9,5},{6,10},{10,6},{7,11},{11,7},{20,24},{24,20... | collective-permute-start | bytes 589832 | tf_op jit(solution)/shard_map/ppermute | solution.py:250
  40.9 2.4 %collective-permute-done.7.refs_12_ = bf16[2,4,48,128]{3,2,1,0:T(8,128)(2,1)S(1)} collective-permute-done((bf16[2,4,48,128]{3,2,1,0:T(8,128)(2,1)S(1)}, bf16[2,4,48,128]{3,2,1,0:T(8,128)(2,1)S(1)}, u32[]{:S(2)}, u32[]{:S(2)}) %collective-permute-start.7) | collective-permute-done | bytes 98336 | tf_op jit(solution)/shard_map/ppermute | solution.py:249
  43.3 3.4 %collective-permute-start.9 = (bf16[2,12,48,128]{3,2,1,0:T(8,128)(2,1)S(1)}, bf16[2,12,48,128]{3,2,1,0:T(8,128)(2,1)S(1)}, u32[]{:S(2)}, u32[]{:S(2)}) collective-permute-start(bf16[2,12,48,128]{3,2,1,0:T(8,128)(2,1)S(1)} %select.5.refs_7_), channel_id=1, source_target_pairs={{0,4},{4,0},{8,12},{12,8},{1,5},{5,1},{9,13},{13,9},{2,6},{6,2},{1... | collective-permute-start | bytes 884744 | tf_op jit(solution)/shard_map/ppermute | solution.py:248
  46.7 0.0 collective-permute-done.14.refs_12_
  46.7 1.9 %collective-permute-start.3 = (bf16[2,12,48,128]{3,2,1,0:T(8,128)(2,1)S(1)}, bf16[2,12,48,128]{3,2,1,0:T(8,128)(2,1)S(1)}, u32[]{:S(2)}, u32[]{:S(2)}) collective-permute-start(bf16[2,12,48,128]{3,2,1,0:T(8,128)(2,1)S(1)} %select.5.refs_7_), channel_id=1, source_target_pairs={{4,8},{8,4},{5,9},{9,5},{6,10},{10,6},{7,11},{11,7},{20,24},{24,20... | collective-permute-start | bytes 884744 | tf_op jit(solution)/shard_map/ppermute | solution.py:250
  48.7 0.0 collective-permute-done.16.refs_10_
  48.7 2.0 %collective-permute-start.15 = (bf16[2,8,48,128]{3,2,1,0:T(8,128)(2,1)}, bf16[2,8,48,128]{3,2,1,0:T(8,128)(2,1)}, u32[]{:S(2)}, u32[]{:S(2)}) collective-permute-start(bf16[2,8,48,128]{3,2,1,0:T(8,128)(2,1)} %collective-permute-done.14.refs_12_), channel_id=1, source_target_pairs={{8,12},{4,0},{9,13},{5,1},{10,14},{6,2},{11,15},{7,3},{24,28},{20,... | collective-permute-start | bytes 589832 | tf_op jit(solution)/shard_map/ppermute | solution.py:251
  50.6 2.0 %collective-permute-start.5 = (bf16[2,12,48,128]{3,2,1,0:T(8,128)(2,1)S(1)}, bf16[2,12,48,128]{3,2,1,0:T(8,128)(2,1)}, u32[]{:S(2)}, u32[]{:S(2)}) collective-permute-start(bf16[2,12,48,128]{3,2,1,0:T(8,128)(2,1)S(1)} %collective-permute-done.4.refs_11_), channel_id=1, source_target_pairs={{8,12},{4,0},{9,13},{5,1},{10,14},{6,2},{11,15},{7,3},{24,28},{20,... | collective-permute-start | bytes 884744 | tf_op jit(solution)/shard_map/ppermute | solution.py:251
  52.6 0.1 pad_select_fusion
  52.7 0.1 reshape.43
  52.8 0.6 slice.5.refs_0_
  53.4 0.0 collective-permute-done.13.refs_9_
  53.4 5.0 %collective-permute-done.15.refs_10_ = bf16[2,8,48,128]{3,2,1,0:T(8,128)(2,1)} collective-permute-done((bf16[2,8,48,128]{3,2,1,0:T(8,128)(2,1)}, bf16[2,8,48,128]{3,2,1,0:T(8,128)(2,1)}, u32[]{:S(2)}, u32[]{:S(2)}) %collective-permute-start.15) | collective-permute-done | bytes 196640 | tf_op jit(solution)/shard_map/ppermute | solution.py:251
  58.4 1.9 %collective-permute-start.6 = (bf16[2,4,48,128]{3,2,1,0:T(8,128)(2,1)}, bf16[2,4,48,128]{3,2,1,0:T(8,128)(2,1)}, u32[]{:S(2)}, u32[]{:S(2)}) collective-permute-start(bf16[2,4,48,128]{3,2,1,0:T(8,128)(2,1)} %copy-done.2), channel_id=1, source_target_pairs={{4,8},{8,4},{5,9},{9,5},{6,10},{10,6},{7,11},{11,7},{20,24},{24,20... | collective-permute-start | bytes 294920 | tf_op jit(solution)/shard_map/ppermute | solution.py:250
  60.3 0.0 collective-permute-done.9.refs_9_
  60.4 4.4 %collective-permute-start.8 = (bf16[2,4,48,128]{3,2,1,0:T(8,128)(2,1)}, bf16[2,4,48,128]{3,2,1,0:T(8,128)(2,1)}, u32[]{:S(2)}, u32[]{:S(2)}) collective-permute-start(bf16[2,4,48,128]{3,2,1,0:T(8,128)(2,1)} %copy-done.5), channel_id=1, source_target_pairs={{8,12},{4,0},{9,13},{5,1},{10,14},{6,2},{11,15},{7,3},{24,28},{20,... | collective-permute-start | bytes 294920 | tf_op jit(solution)/shard_map/ppermute | solution.py:251
  64.8 0.6 gather_fusion.1
  65.4 0.8 copy-done.1
  66.2 7.8 %cross.4.refs_11_ = bf16[24,2,2,256,256]{4,3,2,1,0:T(8,128)(2,1)} custom-call(s32[3]{0:T(128)S(1)} %gather_fusion.1, f32[2,128]{1,0:T(2,128)S(1)} %pad.7.refs_1_, bf16[128,128]{1,0:T(8,128)(2,1)S(1)} %copy-done.1, bf16[24,48,256]{2,1,0:T(8,128)(2,1)S(1)} %get-tuple-element.11.refs_1_.refs_3_, bf16[24,48,256]{2,1,0:T(8,128)(2,1)S(1)} %collective-permute-done.refs_2_.refs_4_, ...), custom_call_target="tpu_custom_call" | custom-call | tf_op jit(solution)/shard_map/cross/pallas_call | solution.py:294
  74.0 0.0 collective-permute-done.5.refs_8_
  74.0 6.5 %cross.5.refs_13_ = bf16[24,2,2,256,256]{4,3,2,1,0:T(8,128)(2,1)} custom-call(s32[1]{0:T(128)} %slice.5.refs_0_, f32[2,128]{1,0:T(2,128)S(1)} %pad.7.refs_1_, bf16[128,128]{1,0:T(8,128)(2,1)S(1)} %copy-done.1, bf16[24,48,256]{2,1,0:T(8,128)(2,1)S(1)} %get-tuple-element.11.refs_1_.refs_3_, ...), custom_call_target="tpu_custom_call", output_to_operand_aliasing={{}: (11, {})} | custom-call | tf_op jit(solution)/shard_map/cross/pallas_call | solution.py:294
  80.5 4.7 %cross.6.refs_11_ = bf16[24,2,2,256,256]{4,3,2,1,0:T(8,128)(2,1)} custom-call(s32[3]{0:T(128)S(1)} %gather_fusion.1, f32[2,128]{1,0:T(2,128)S(1)} %pad.7.refs_1_, bf16[128,128]{1,0:T(8,128)(2,1)S(1)} %copy-done.1, bf16[24,48,256]{2,1,0:T(8,128)(2,1)S(1)} %get-tuple-element.11.refs_1_.refs_3_, ...), custom_call_target="tpu_custom_call", output_to_operand_aliasing={{}: (13, {})} | custom-call | tf_op jit(solution)/shard_map/cross/pallas_call | solution.py:294
  85.2 4.3 %cross.7 = bf16[24,2,2,256,256]{4,3,2,1,0:T(8,128)(2,1)} custom-call(s32[1]{0:T(128)} %slice.5.refs_0_, f32[2,128]{1,0:T(2,128)S(1)} %pad.7.refs_1_, bf16[128,128]{1,0:T(8,128)(2,1)S(1)} %copy-done.1, bf16[24,48,256]{2,1,0:T(8,128)(2,1)S(1)} %get-tuple-element.11.refs_1_.refs_3_, ...), custom_call_target="tpu_custom_call", output_to_operand_aliasing={{}: (11, {})} | custom-call | tf_op jit(solution)/shard_map/cross/pallas_call | solution.py:294
  (28 shorter events, 0.1 us)
Async XLA Ops:
  0.0 2.6 %copy-start = (bf16[22,512,256]{2,1,0:T(8,128)(2,1)S(1)}, bf16[22,512,256]{2,1,0:T(8,128)(2,1)}, u32[]{:S(2)}) copy-start(bf16[22,512,256]{2,1,0:T(8,128)(2,1)} %refs_1_.1) | copy-start | bytes 17301508
  2.6 0.9 %copy-start.4 = (bf16[4,48,512]{2,1,0:T(8,128)(2,1)S(1)}, bf16[4,48,512]{2,1,0:T(8,128)(2,1)}, u32[]{:S(2)}) copy-start(bf16[4,48,512]{2,1,0:T(8,128)(2,1)} %constant.51.clone.refs_2_) | copy-start | bytes 589828
  7.4 6.0 %collective-permute-start = (bf16[24,48,256]{2,1,0:T(8,128)(2,1)S(1)}, bf16[24,48,256]{2,1,0:T(8,128)(2,1)S(1)}, u32[]{:S(2)}, u32[]{:S(2)}) collective-permute-start(bf16[24,48,256]{2,1,0:T(8,128)(2,1)S(1)} %get-tuple-element.12), channel_id=1, source_target_pairs={{0,1},{1,0},{2,3},{3,2},{4,5},{5,4},{6,7},{7,6},{8,9},{9,8},{10,11... | collective-permute-start | bytes 1769480 | tf_op jit(solution)/shard_map/ppermute | solution.py:225
  7.5 12.2 %collective-permute-start.11 = (bf16[16,48,256]{2,1,0:T(8,128)(2,1)}, bf16[16,48,256]{2,1,0:T(8,128)(2,1)S(1)}, u32[]{:S(2)}, u32[]{:S(2)}) collective-permute-start(bf16[16,48,256]{2,1,0:T(8,128)(2,1)} %get-tuple-element.15), channel_id=1, source_target_pairs={{0,2},{1,3},{2,0},{3,1},{4,6},{5,7},{6,4},{7,5},{8,10},{9,11},{10,... | collective-permute-start | bytes 1179656 | tf_op jit(solution)/shard_map/ppermute | solution.py:225
  9.0 18.2 %collective-permute-start.12 = (bf16[16,48,256]{2,1,0:T(8,128)(2,1)S(1)}, bf16[16,48,256]{2,1,0:T(8,128)(2,1)S(1)}, u32[]{:S(2)}, u32[]{:S(2)}) collective-permute-start(bf16[16,48,256]{2,1,0:T(8,128)(2,1)S(1)} %get-tuple-element.16), channel_id=1, source_target_pairs={{0,3},{1,2},{2,1},{3,0},{4,7},{5,6},{6,5},{7,4},{8,11},{9,10},{10,... | collective-permute-start | bytes 1179656 | tf_op jit(solution)/shard_map/ppermute | solution.py:225
  9.3 23.0 %collective-permute-start.1 = (bf16[8,48,256]{2,1,0:T(8,128)(2,1)}, bf16[8,48,256]{2,1,0:T(8,128)(2,1)S(1)}, u32[]{:S(2)}, u32[]{:S(2)}) collective-permute-start(bf16[8,48,256]{2,1,0:T(8,128)(2,1)} %get-tuple-element.13), channel_id=1, source_target_pairs={{0,2},{1,3},{2,0},{3,1},{4,6},{5,7},{6,4},{7,5},{8,10},{9,11},{10,... | collective-permute-start | bytes 589832 | tf_op jit(solution)/shard_map/ppermute | solution.py:225
  10.8 24.8 %collective-permute-start.2 = (bf16[8,48,256]{2,1,0:T(8,128)(2,1)S(1)}, bf16[8,48,256]{2,1,0:T(8,128)(2,1)S(1)}, u32[]{:S(2)}, u32[]{:S(2)}) collective-permute-start(bf16[8,48,256]{2,1,0:T(8,128)(2,1)S(1)} %get-tuple-element.14), channel_id=1, source_target_pairs={{0,3},{1,2},{2,1},{3,0},{4,7},{5,6},{6,5},{7,4},{8,11},{9,10},{10,... | collective-permute-start | bytes 589832 | tf_op jit(solution)/shard_map/ppermute | solution.py:225
  13.8 36.8 %collective-permute-start.4 = (bf16[2,12,48,128]{3,2,1,0:T(8,128)(2,1)S(1)}, bf16[2,12,48,128]{3,2,1,0:T(8,128)(2,1)S(1)}, u32[]{:S(2)}, u32[]{:S(2)}) collective-permute-start(bf16[2,12,48,128]{3,2,1,0:T(8,128)(2,1)S(1)} %select.5.refs_7_), channel_id=1, source_target_pairs={{0,8},{4,12},{8,0},{12,4},{1,9},{5,13},{9,1},{13,5},{2,10},{6,14},... | collective-permute-start | bytes 884744 | tf_op jit(solution)/shard_map/ppermute | solution.py:249
  28.2 18.5 %collective-permute-start.14 = (bf16[2,8,48,128]{3,2,1,0:T(8,128)(2,1)}, bf16[2,8,48,128]{3,2,1,0:T(8,128)(2,1)}, u32[]{:S(2)}, u32[]{:S(2)}) collective-permute-start(bf16[2,8,48,128]{3,2,1,0:T(8,128)(2,1)} %select.7.refs_8_), channel_id=1, source_target_pairs={{0,8},{4,12},{8,0},{12,4},{1,9},{5,13},{9,1},{13,5},{2,10},{6,14},... | collective-permute-start | bytes 589832 | tf_op jit(solution)/shard_map/ppermute | solution.py:249
  28.5 20.2 %collective-permute-start.16 = (bf16[2,8,48,128]{3,2,1,0:T(8,128)(2,1)}, bf16[2,8,48,128]{3,2,1,0:T(8,128)(2,1)}, u32[]{:S(2)}, u32[]{:S(2)}) collective-permute-start(bf16[2,8,48,128]{3,2,1,0:T(8,128)(2,1)} %select.7.refs_8_), channel_id=1, source_target_pairs={{0,4},{4,0},{8,12},{12,8},{1,5},{5,1},{9,13},{13,9},{2,6},{6,2},{1... | collective-permute-start | bytes 589832 | tf_op jit(solution)/shard_map/ppermute | solution.py:248
  35.9 14.8 %copy-start.2 = (bf16[2,4,48,128]{3,2,1,0:T(8,128)(2,1)}, bf16[2,4,48,128]{3,2,1,0:T(8,128)(2,1)S(1)}, u32[]{:S(2)}) copy-start(bf16[2,4,48,128]{3,2,1,0:T(8,128)(2,1)S(1)} %select.6.refs_8_) | copy-start | bytes 294916
  35.9 7.4 %collective-permute-start.7 = (bf16[2,4,48,128]{3,2,1,0:T(8,128)(2,1)S(1)}, bf16[2,4,48,128]{3,2,1,0:T(8,128)(2,1)S(1)}, u32[]{:S(2)}, u32[]{:S(2)}) collective-permute-start(bf16[2,4,48,128]{3,2,1,0:T(8,128)(2,1)S(1)} %select.6.refs_8_), channel_id=1, source_target_pairs={{0,8},{4,12},{8,0},{12,4},{1,9},{5,13},{9,1},{13,5},{2,10},{6,14},... | collective-permute-start | bytes 294920 | tf_op jit(solution)/shard_map/ppermute | solution.py:249
  36.2 17.2 %collective-permute-start.13 = (bf16[2,8,48,128]{3,2,1,0:T(8,128)(2,1)}, bf16[2,8,48,128]{3,2,1,0:T(8,128)(2,1)}, u32[]{:S(2)}, u32[]{:S(2)}) collective-permute-start(bf16[2,8,48,128]{3,2,1,0:T(8,128)(2,1)} %select.7.refs_8_), channel_id=1, source_target_pairs={{4,8},{8,4},{5,9},{9,5},{6,10},{10,6},{7,11},{11,7},{20,24},{24,20... | collective-permute-start | bytes 589832 | tf_op jit(solution)/shard_map/ppermute | solution.py:250
  43.3 9.3 %copy-start.5 = (bf16[2,4,48,128]{3,2,1,0:T(8,128)(2,1)}, bf16[2,4,48,128]{3,2,1,0:T(8,128)(2,1)S(1)}, u32[]{:S(2)}) copy-start(bf16[2,4,48,128]{3,2,1,0:T(8,128)(2,1)S(1)} %collective-permute-done.7.refs_12_) | copy-start | bytes 294916
  43.3 17.0 %collective-permute-start.9 = (bf16[2,12,48,128]{3,2,1,0:T(8,128)(2,1)S(1)}, bf16[2,12,48,128]{3,2,1,0:T(8,128)(2,1)S(1)}, u32[]{:S(2)}, u32[]{:S(2)}) collective-permute-start(bf16[2,12,48,128]{3,2,1,0:T(8,128)(2,1)S(1)} %select.5.refs_7_), channel_id=1, source_target_pairs={{0,4},{4,0},{8,12},{12,8},{1,5},{5,1},{9,13},{13,9},{2,6},{6,2},{1... | collective-permute-start | bytes 884744 | tf_op jit(solution)/shard_map/ppermute | solution.py:248
  46.7 27.2 %collective-permute-start.3 = (bf16[2,12,48,128]{3,2,1,0:T(8,128)(2,1)S(1)}, bf16[2,12,48,128]{3,2,1,0:T(8,128)(2,1)S(1)}, u32[]{:S(2)}, u32[]{:S(2)}) collective-permute-start(bf16[2,12,48,128]{3,2,1,0:T(8,128)(2,1)S(1)} %select.5.refs_7_), channel_id=1, source_target_pairs={{4,8},{8,4},{5,9},{9,5},{6,10},{10,6},{7,11},{11,7},{20,24},{24,20... | collective-permute-start | bytes 884744 | tf_op jit(solution)/shard_map/ppermute | solution.py:250
  48.7 9.8 %collective-permute-start.15 = (bf16[2,8,48,128]{3,2,1,0:T(8,128)(2,1)}, bf16[2,8,48,128]{3,2,1,0:T(8,128)(2,1)}, u32[]{:S(2)}, u32[]{:S(2)}) collective-permute-start(bf16[2,8,48,128]{3,2,1,0:T(8,128)(2,1)} %collective-permute-done.14.refs_12_), channel_id=1, source_target_pairs={{8,12},{4,0},{9,13},{5,1},{10,14},{6,2},{11,15},{7,3},{24,28},{20,... | collective-permute-start | bytes 589832 | tf_op jit(solution)/shard_map/ppermute | solution.py:251
  50.6 23.4 %collective-permute-start.5 = (bf16[2,12,48,128]{3,2,1,0:T(8,128)(2,1)S(1)}, bf16[2,12,48,128]{3,2,1,0:T(8,128)(2,1)}, u32[]{:S(2)}, u32[]{:S(2)}) collective-permute-start(bf16[2,12,48,128]{3,2,1,0:T(8,128)(2,1)S(1)} %collective-permute-done.4.refs_11_), channel_id=1, source_target_pairs={{8,12},{4,0},{9,13},{5,1},{10,14},{6,2},{11,15},{7,3},{24,28},{20,... | collective-permute-start | bytes 884744 | tf_op jit(solution)/shard_map/ppermute | solution.py:251
  53.4 27.1 %collective-permute-start.10 = (bf16[2,4,48,128]{3,2,1,0:T(8,128)(2,1)}, bf16[2,4,48,128]{3,2,1,0:T(8,128)(2,1)}, u32[]{:S(2)}, u32[]{:S(2)}) collective-permute-start(bf16[2,4,48,128]{3,2,1,0:T(8,128)(2,1)} %copy-done.2), channel_id=1, source_target_pairs={{0,4},{4,0},{8,12},{12,8},{1,5},{5,1},{9,13},{13,9},{2,6},{6,2},{1... | collective-permute-start | bytes 294920 | tf_op jit(solution)/shard_map/ppermute | solution.py:248
  58.4 26.8 %collective-permute-start.6 = (bf16[2,4,48,128]{3,2,1,0:T(8,128)(2,1)}, bf16[2,4,48,128]{3,2,1,0:T(8,128)(2,1)}, u32[]{:S(2)}, u32[]{:S(2)}) collective-permute-start(bf16[2,4,48,128]{3,2,1,0:T(8,128)(2,1)} %copy-done.2), channel_id=1, source_target_pairs={{4,8},{8,4},{5,9},{9,5},{6,10},{10,6},{7,11},{11,7},{20,24},{24,20... | collective-permute-start | bytes 294920 | tf_op jit(solution)/shard_map/ppermute | solution.py:250
  60.4 24.8 %collective-permute-start.8 = (bf16[2,4,48,128]{3,2,1,0:T(8,128)(2,1)}, bf16[2,4,48,128]{3,2,1,0:T(8,128)(2,1)}, u32[]{:S(2)}, u32[]{:S(2)}) collective-permute-start(bf16[2,4,48,128]{3,2,1,0:T(8,128)(2,1)} %copy-done.5), channel_id=1, source_target_pairs={{8,12},{4,0},{9,13},{5,1},{10,14},{6,2},{11,15},{7,3},{24,28},{20,... | collective-permute-start | bytes 294920 | tf_op jit(solution)/shard_map/ppermute | solution.py:251
  65.4 0.8 copy-start.1
  74.0 6.5 %copy-start.3 = (bf16[2,4,48,128]{3,2,1,0:T(8,128)(2,1)S(1)}, bf16[2,4,48,128]{3,2,1,0:T(8,128)(2,1)}, u32[]{:S(2)}) copy-start(bf16[2,4,48,128]{3,2,1,0:T(8,128)(2,1)} %copy-done.2) | copy-start | bytes 294916
  74.0 6.5 %copy-start.6 = (bf16[2,4,48,128]{3,2,1,0:T(8,128)(2,1)S(1)}, bf16[2,4,48,128]{3,2,1,0:T(8,128)(2,1)}, u32[]{:S(2)}) copy-start(bf16[2,4,48,128]{3,2,1,0:T(8,128)(2,1)} %copy-done.5) | copy-start | bytes 294916

commit v3 on v2

v3 whole, which is shorter than its diff:
```python
import math

import jax
import jax.numpy as jnp
import numpy as np
import ml_dtypes
from jax import lax
from jax.experimental import pallas as pl
from jax.experimental.pallas import tpu as pltpu
from jax.sharding import PartitionSpec as P

F = 96
K0 = 8
G = 2
PARTS = (2, 1)
f32 = jnp.float32
bf16 = jnp.bfloat16


def make_table(length):
    freqs = K0 + np.arange(F)
    phase = freqs[:, None] * np.arange(length)[None, :] % length
    angle = phase.astype(np.float32) * np.float32(2.0 * math.pi / length)
    scale = np.float32(1.0 / math.sqrt(length))
    table = np.stack([np.cos(angle) * scale, -np.sin(angle) * scale], axis=1)
    return table.astype(np.float32).astype(ml_dtypes.bfloat16)


def up(n, m):
    return -(-n // m) * m


def chunk_sizes(bins):
    sizes = [bins * part // sum(PARTS) for part in PARTS]
    return sizes[:-1] + [bins - sum(sizes[:-1])]


def head_kernel(cfg, order, samples_hbm, table_hbm, *refs):
    win, wpad, n_tf, bins, sizes = cfg
    outs, (samples, table, tscr, spec, buf, sem) = refs[:-6], refs[-6:]
    load_table = pltpu.make_async_copy(table_hbm, table, sem.at[0])
    load_samples = pltpu.make_async_copy(samples_hbm, samples, sem.at[1])
    load_table.start()
    load_samples.start()
    to = lax.broadcasted_iota(jnp.int32, (128, 128), 0)
    at = lax.broadcasted_iota(jnp.int32, (128, 128), 1)
    shuffle = ((to % 8 == at // 16) & (to // 8 == at % 16)).astype(f32).astype(bf16)
    for w in range(win, wpad):
        spec[w] = jnp.zeros(spec.shape[1:], bf16)
    load_table.wait()
    rows = [table[order[k]].astype(f32) for k in range(n_tf)]
    tscr[...] = jnp.concatenate(rows, axis=0).astype(bf16)
    load_samples.wait()
    for w in range(win):
        x = samples[w]
        xf = x.astype(f32)
        power = jnp.mean(xf * xf, axis=0, keepdims=True)
        y = jnp.dot(tscr[...], x, preferred_element_type=f32)
        spec[w] = (y * lax.rsqrt(power + 1e-06)).astype(bf16)
    spans = [(0, bins), (bins, bins)]
    for k in range(2, n_tf):
        base = k * bins
        for size in sizes:
            spans.append((base, size))
            base += size
    stores = [
        pltpu.make_async_copy(buf.at[pl.ds(base, size)], out, sem.at[2 + i])
        for i, ((base, size), out) in enumerate(zip(spans, outs))
    ]
    done = set()
    for grp in reversed(range(2 * F // 16)):
        parts = []
        for wg in range(wpad // 8):
            block = spec[8 * wg : 8 * wg + 8, 16 * grp : 16 * grp + 16, :]
            block = block.reshape(128, block.shape[-1])
            parts.append(jnp.dot(shuffle, block, preferred_element_type=f32))
        for j in range(8):
            pieces = []
            for r in range(2):
                row = (2 * j + r) * 8
                pieces += [p[row : row + 8] for p in parts]
            buf[grp * 8 + j] = jnp.concatenate(pieces, axis=0).astype(bf16)
        for i, (base, _) in enumerate(spans):
            if base >= grp * 8 and i not in done:
                done.add(i)
                stores[i].start()
    for store in stores:
        store.wait()


def select_kernel(cols, *refs):
    slabs, out = refs[:-1], refs[-1]
    bins, rows, chans = slabs[0].shape
    lanes = cols.shape[1]
    pick = (lax.broadcasted_iota(jnp.int32, (chans, lanes), 0) == cols[...]).astype(f32).astype(bf16)
    first = lax.broadcasted_iota(jnp.int32, (rows, lanes), 1) < lanes // 2
    for d, slab in enumerate(slabs):
        for p in range(bins // 2):
            flat = slab[2 * p : 2 * p + 2].reshape(2 * rows, chans)
            got = jnp.dot(flat, pick, preferred_element_type=f32)
            out[d, p] = jnp.where(first, got[:rows], got[rows:]).astype(bf16)


def cross_kernel(cfg, blk, coef, *refs):
    wpad, scale, n_slab, counts, lead = cfg
    out, buf, sem = refs[-3:]
    slabs, rest = refs[:n_slab], refs[n_slab:-3]
    panels = []
    for near, far in counts:
        panels.append((rest[:near], rest[near : near + far]))
        rest = rest[near + far :]
    n_blk = len(panels)
    src = panels[0][0][0].shape[-1] // 2
    chans = slabs[0].shape[-1]
    tall = n_blk * src
    pairs = buf.shape[0]

    def copy_out(p, b):
        at = pl.ds(pl.multiple_of(blk[b] * src, src), src)
        return pltpu.make_async_copy(
            buf.at[p, :, :, :, pl.ds(b * src, src), :],
            out.at[pl.ds(2 * (lead + p), 2), :, :, at, :],
            sem.at[p, b],
        )

    def pair(p, _):
        turned = []
        for near, far in panels:
            stack = []
            for group, at in ((near, lead + p), (far, p)):
                for d in range(group[0].shape[0]):
                    value = group[0][d, at].astype(f32)
                    for other in group[1:]:
                        value = value + other[d, at].astype(f32)
                    stack.append(value)
            turned.append(jnp.transpose(jnp.concatenate(stack, axis=0)))
        for j in range(2):
            plain, swapped = [], []
            for i, slab in enumerate(slabs):
                v = slab[2 * ((lead if i < 2 else 0) + p) + j]
                plain.append(v)
                v = v.astype(f32)
                swapped += [v[wpad:], -v[:wpad]]
            plain = jnp.concatenate(plain, axis=0)
            swapped = jnp.concatenate(swapped, axis=0).astype(bf16)
            right = jnp.concatenate([plain, swapped], axis=1)
            left = [
                (t[src * j : src * (j + 1)] * coef[g : g + 1]).astype(bf16)
                for g in range(G)
                for t in turned
            ]
            left = jnp.concatenate(left, axis=0)
            got = (jnp.dot(left, right, preferred_element_type=f32) * scale).astype(bf16)
            for g in range(G):
                for o in range(2):
                    buf[p, j, g, o] = got[g * tall : (g + 1) * tall, o * chans : (o + 1) * chans]
        for b in range(n_blk):
            copy_out(p, b).start()
        return 0

    lax.fori_loop(0, pairs, pair, 0, unroll=4 if pairs % 4 == 0 else 2 if pairs % 2 == 0 else 1)
    for p in range(pairs):
        for b in range(n_blk):
            copy_out(p, b).wait()


def cost(us):
    return pl.CostEstimate(flops=int(us * 1.1e9), bytes_accessed=int(us * 3e6), transcendentals=0)


def shards(samples, quality, substack, sources):
    win, length, chans = samples.shape
    n_tf = lax.axis_size("tf")
    n_chan = lax.axis_size("chan")
    me = lax.axis_index("tf")
    pos = lax.axis_index("chan")
    bins = F // n_tf
    src = sources.shape[0] // n_chan
    wpad = up(win, 8)
    sizes = chunk_sizes(bins)
    chunks = len(sizes)
    rows = 2 * wpad
    order = (me ^ jnp.arange(n_tf, dtype=jnp.int32)).astype(jnp.int32)
    table = jnp.asarray(make_table(length).reshape(n_tf, 2 * bins, length))
    smem = pl.BlockSpec(memory_space=pltpu.SMEM)
    vmem = pl.BlockSpec(memory_space=pltpu.VMEM)
    hbm = pl.BlockSpec(memory_space=pltpu.HBM)

    shapes = [jax.ShapeDtypeStruct((bins, rows, chans), bf16)] * 2
    for _ in range(n_tf - 2):
        shapes += [jax.ShapeDtypeStruct((size, rows, chans), bf16) for size in sizes]
    got = pl.pallas_call(
        lambda *refs: head_kernel((win, wpad, n_tf, bins, sizes), *refs),
        in_specs=[smem, hbm, hbm],
        out_specs=[hbm] * len(shapes),
        out_shape=shapes,
        scratch_shapes=[
            pltpu.VMEM(samples.shape, bf16),
            pltpu.VMEM(table.shape, bf16),
            pltpu.VMEM((2 * F, length), bf16),
            pltpu.VMEM((wpad, 2 * F, chans), bf16),
            pltpu.VMEM((F, rows, chans), bf16),
            pltpu.SemaphoreType.DMA((2 + len(shapes),)),
        ],
        compiler_params=pltpu.CompilerParams(vmem_limit_bytes=57 * 1024 * 1024),
        cost_estimate=cost(5),
        name="head",
    )(order, samples, table)
    own, for_core = got[0], got[1]

    def across(value, k):
        return lax.ppermute(value, "tf", [(i, i ^ k) for i in range(n_tf)])

    core = across(for_core, 1)
    far = [
        [across(got[2 + (k - 2) * chunks + q], k) for k in range(2, n_tf)] for q in range(chunks)
    ]

    mine = lax.dynamic_slice_in_dim(sources, pos * src, src, 0) - pos * chans
    cols = jnp.concatenate([mine, mine])[None, :]

    def select(slabs):
        count = slabs[0].shape[0]
        return pl.pallas_call(
            select_kernel,
            in_specs=[vmem] * (1 + len(slabs)),
            out_specs=vmem,
            out_shape=jax.ShapeDtypeStruct((len(slabs), count // 2, rows, 2 * src), bf16),
            cost_estimate=cost(0.5),
            compiler_params=pltpu.CompilerParams(vmem_limit_bytes=12 * 1024 * 1024),
            name="select",
        )(cols, *slabs)

    def spread(panel):
        if n_chan == 4:
            two = lax.ppermute(panel, "chan", [(i, i ^ 2) for i in range(4)])
            one = lax.ppermute(panel, "chan", [(i, i ^ 1) for i in range(4)])
            later, one, two = lax.optimization_barrier((panel, one, two))
            end = lax.ppermute(two, "chan", [(2, 3), (1, 0)])
            mid = lax.ppermute(later, "chan", [(1, 2), (2, 1)])
            return [[panel], [one], [two], [mid, end]]
        return [[panel]] + [
            [lax.ppermute(panel, "chan", [(i, (i + k) % n_chan) for i in range(n_chan)])]
            for k in range(1, n_chan)
        ]

    if n_chan == 4:
        blk = pos ^ jnp.arange(4, dtype=jnp.int32)
    else:
        blk = (pos - jnp.arange(n_chan, dtype=jnp.int32)) % n_chan
    blk = blk.astype(jnp.int32)

    coef = jnp.where(
        substack[None, :] == jnp.arange(G, dtype=jnp.int32)[:, None],
        (quality[None, :].astype(f32) + 1.0) / 4.0,
        0.0,
    ).reshape(G, n_tf, win)
    coef = jnp.pad(coef, ((0, 0), (0, 0), (0, wpad - win)))
    coef = jnp.take(jnp.concatenate([coef, coef], axis=2), order, axis=1).reshape(G, n_tf * rows)
    scale = 1.0 / math.sqrt(win * n_tf)

    near = spread(select([own, core]))
    away, before = [], [near[1][0], near[2][0]]
    for q in range(chunks):
        if q:
            *far[q], _, _, _ = lax.optimization_barrier((*far[q], *before, panel))
        panel = select(far[q])
        away.append(spread(panel))
    out_shape = jax.ShapeDtypeStruct((bins, G, 2, src * n_chan, chans), bf16)
    groups = [[0, 1, 2], [3]] if n_chan == 4 else [list(range(n_chan))]
    stacks = None
    for q, size in enumerate(sizes):
        for group in groups:
            pairs = size // 2
            args, counts = [own, core] + far[q], []
            for b in group:
                args += near[b] + away[q][b]
                counts.append((len(near[b]), len(away[q][b])))
            cfg = (wpad, scale, n_tf, counts, sum(sizes[:q]) // 2)
            first = stacks is None
            extra = [] if first else [stacks]

            def body(*refs, cfg=cfg, first=first):
                cross_kernel(cfg, *(refs if first else refs[:-4] + refs[-3:]))

            stacks = pl.pallas_call(
                body,
                in_specs=[smem] + [vmem] * (1 + len(args)) + [hbm] * len(extra),
                out_specs=hbm,
                out_shape=out_shape,
                scratch_shapes=[
                    pltpu.VMEM((pairs, 2, G, 2, len(group) * src, chans), bf16),
                    pltpu.SemaphoreType.DMA((pairs, len(group))),
                ],
                input_output_aliases={} if first else {2 + len(args): 0},
                compiler_params=pltpu.CompilerParams(vmem_limit_bytes=20 * 1024 * 1024),
                cost_estimate=cost(1.5 + size * len(group) * src / 1000),
                name="cross",
            )(blk[np.array(group)], coef, *args, *extra)
    return stacks


def solution(mesh):
    in_specs = (P(("day", "tf"), None, "chan"), P("day"), P("day"), P())
    out_specs = P("tf", "day", None, None, "chan")
    return jax.shard_map(shards, mesh=mesh, in_specs=in_specs, out_specs=out_specs, check_vma=False)
```

time: 90.1 us -> 72.4 us (0.80)
  the two profiles are of different devices: /device:TPU:16 before, /device:TPU:0 now
where the time goes in v3:
time: 72.4 us; the launch traced here: 72 us
  starting transfers between devices  25.5 us (35%)
  waiting for transfers between devices  22.7 us (31%)
  Pallas kernels  18.4 us (25%)
  local copies, waits for them, and re-layouts  4.38 us (6%)
  other arithmetic  0.77 us (1%)
    pallas_call x4, Pallas kernels, shards(): pl.pallas_call(body, in_specs=[smem] + [vmem] * (1 + len(args)) + [hbm] *...  10.9 us
    ppermute x3, waiting for transfers between devices, spread(): one = lax.ppermute(panel, 'chan', [(i, i ^ 1) for i in range(4)])  9.24 us
    ppermute x5, waiting for transfers between devices, across(): return lax.ppermute(value, 'tf', [(i, i ^ k) for i in range(n_tf)])  8.88 us
    ppermute x3, starting transfers between devices, spread(): two = lax.ppermute(panel, 'chan', [(i, i ^ 2) for i in range(4)])  8.4 us
    pallas_call x1, Pallas kernels, shards(): pl.pallas_call(lambda *refs: head_kernel((win, wpad, n_tf, bins, sizes),...  6.39 us
    ppermute x3, starting transfers between devices, spread(): one = lax.ppermute(panel, 'chan', [(i, i ^ 1) for i in range(4)])  6.11 us
    ppermute x5, starting transfers between devices, across(): return lax.ppermute(value, 'tf', [(i, i ^ k) for i in range(n_tf)])  5.16 us
    ppermute x3, waiting for transfers between devices, spread(): two = lax.ppermute(panel, 'chan', [(i, i ^ 2) for i in range(4)])  4.61 us
  transfers between devices with their start and end apart: 17, of which 7 were waited for; matrix products, arithmetic and copies ran while one was open for 4% of the time, Pallas kernels for 14%

profile of v3, /device:TPU:0, one launch (start us, length us, event | category | flops | bytes accessed | tf_op | source)
XLA Modules:
  0.0 72.0 jit_solution(9191639153809815861)
XLA Ops:
  0.0 0.5 iota_xor_fusion.refs_0_
  0.5 6.4 %head.1 = (bf16[24,48,256]{2,1,0:T(8,128)(2,1)}, bf16[24,48,256]{2,1,0:T(8,128)(2,1)}, bf16[16,48,256]{2,1,0:T(8,128)(2,1)}, bf16[8,48,256]{2,1,0:T(8,128)(2,1)}...) custom-call(s32[4]{0:T(128)} %iota_xor_fusion.refs_0_, bf16[22,512,256]{2,1,0:T(8,128)(2,1)} %refs_1_.1, ...), custom_call_target="tpu_custom_call" | custom-call | flops 5500000256 | bytes 15000000 | tf_op jit(solution)/shard_map/head/pallas_call | solution.py:192
  6.9 3.0 %collective-permute-start.5 = (bf16[16,48,256]{2,1,0:T(8,128)(2,1)}, bf16[16,48,256]{2,1,0:T(8,128)(2,1)S(1)}, u32[]{:S(2)}, u32[]{:S(2)}) collective-permute-start(bf16[16,48,256]{2,1,0:T(8,128)(2,1)} %get-tuple-element.28), channel_id=1, source_target_pairs={{0,2},{1,3},{2,0},{3,1},{4,6},{5,7},{6,4},{7,5},{8,10},{9,11},{10,... | collective-permute-start | bytes 1179656 | tf_op jit(solution)/shard_map/ppermute | solution.py:212
  9.9 0.2 collective-permute-start
  10.1 1.9 %collective-permute-start.1 = (bf16[8,48,256]{2,1,0:T(8,128)(2,1)}, bf16[8,48,256]{2,1,0:T(8,128)(2,1)S(1)}, u32[]{:S(2)}, u32[]{:S(2)}) collective-permute-start(bf16[8,48,256]{2,1,0:T(8,128)(2,1)} %get-tuple-element.24), channel_id=1, source_target_pairs={{0,2},{1,3},{2,0},{3,1},{4,6},{5,7},{6,4},{7,5},{8,10},{9,11},{10,... | collective-permute-start | bytes 589832 | tf_op jit(solution)/shard_map/ppermute | solution.py:212
  12.1 0.0 collective-permute-start.2
  12.1 0.1 broadcast_in_dim.50
  12.2 0.1 eq.16
  12.3 0.1 dynamic-slice_subtract_fusion
  12.4 0.1 pad_maximum_fusion
  12.4 0.1 add_bitcast_fusion.cols
  12.5 0.0 collective-permute-done.refs_1_.refs_3_
  12.5 1.1 %copy-done = bf16[24,48,256]{2,1,0:T(8,128)(2,1)S(1)} copy-done((bf16[24,48,256]{2,1,0:T(8,128)(2,1)S(1)}, bf16[24,48,256]{2,1,0:T(8,128)(2,1)}, u32[]{:S(2)}) %copy-start) | copy-done | bytes 589848
  13.6 0.5 select.4.refs_6_
  14.1 1.6 %collective-permute-start.3 = (bf16[2,12,48,128]{3,2,1,0:T(8,128)(2,1)S(1)}, bf16[2,12,48,128]{3,2,1,0:T(8,128)(2,1)S(1)}, u32[]{:S(2)}, u32[]{:S(2)}) collective-permute-start(bf16[2,12,48,128]{3,2,1,0:T(8,128)(2,1)S(1)} %select.4.refs_6_), channel_id=1, source_target_pairs={{0,4},{4,0},{8,12},{12,8},{1,5},{5,1},{9,13},{13,9},{2,6},{6,2},{1... | collective-permute-start | bytes 884744 | tf_op jit(solution)/shard_map/ppermute | solution.py:237
  15.7 0.6 gather_fusion
  16.3 0.1 gather.20
  16.4 0.1 broadcast_in_dim.47
  16.4 0.1 broadcast_in_dim.48
  16.5 3.5 %collective-permute-done.5.refs_0_.refs_4_ = bf16[16,48,256]{2,1,0:T(8,128)(2,1)S(1)} collective-permute-done((bf16[16,48,256]{2,1,0:T(8,128)(2,1)}, bf16[16,48,256]{2,1,0:T(8,128)(2,1)S(1)}, u32[]{:S(2)}, u32[]{:S(2)}) %collective-permute-start.5) | collective-permute-done | bytes 393248 | tf_op jit(solution)/shard_map/ppermute | solution.py:212
  20.1 3.2 %collective-permute-start.4 = (bf16[2,12,48,128]{3,2,1,0:T(8,128)(2,1)S(1)}, bf16[2,12,48,128]{3,2,1,0:T(8,128)(2,1)S(1)}, u32[]{:S(2)}, u32[]{:S(2)}) collective-permute-start(bf16[2,12,48,128]{3,2,1,0:T(8,128)(2,1)S(1)} %select.4.refs_6_), channel_id=1, source_target_pairs={{0,8},{4,12},{8,0},{12,4},{1,9},{5,13},{9,1},{13,5},{2,10},{6,14},... | collective-permute-start | bytes 884744 | tf_op jit(solution)/shard_map/ppermute | solution.py:236
  23.2 4.9 %collective-permute-done.6.refs_1_.refs_5_ = bf16[16,48,256]{2,1,0:T(8,128)(2,1)S(1)} collective-permute-done((bf16[16,48,256]{2,1,0:T(8,128)(2,1)}, bf16[16,48,256]{2,1,0:T(8,128)(2,1)S(1)}, u32[]{:S(2)}, u32[]{:S(2)}) %collective-permute-start.6) | collective-permute-done | bytes 393248 | tf_op jit(solution)/shard_map/ppermute | solution.py:212
  28.2 0.4 select.5.refs_7_
  28.5 1.6 %collective-permute-start.13 = (bf16[2,8,48,128]{3,2,1,0:T(8,128)(2,1)S(1)}, bf16[2,8,48,128]{3,2,1,0:T(8,128)(2,1)S(1)}, u32[]{:S(2)}, u32[]{:S(2)}) collective-permute-start(bf16[2,8,48,128]{3,2,1,0:T(8,128)(2,1)S(1)} %select.5.refs_7_), channel_id=1, source_target_pairs={{0,4},{4,0},{8,12},{12,8},{1,5},{5,1},{9,13},{13,9},{2,6},{6,2},{1... | collective-permute-start | bytes 589832 | tf_op jit(solution)/shard_map/ppermute | solution.py:237
  30.2 0.0 collective-permute-done.3.refs_8_
  30.2 2.6 %collective-permute-start.14 = (bf16[2,8,48,128]{3,2,1,0:T(8,128)(2,1)S(1)}, bf16[2,8,48,128]{3,2,1,0:T(8,128)(2,1)S(1)}, u32[]{:S(2)}, u32[]{:S(2)}) collective-permute-start(bf16[2,8,48,128]{3,2,1,0:T(8,128)(2,1)S(1)} %select.5.refs_7_), channel_id=1, source_target_pairs={{0,8},{4,12},{8,0},{12,4},{1,9},{5,13},{9,1},{13,5},{2,10},{6,14},... | collective-permute-start | bytes 589832 | tf_op jit(solution)/shard_map/ppermute | solution.py:236
  32.8 0.6 slice.5.refs_0_
  33.4 1.7 %collective-permute-done.4.refs_10_ = bf16[2,12,48,128]{3,2,1,0:T(8,128)(2,1)S(1)} collective-permute-done((bf16[2,12,48,128]{3,2,1,0:T(8,128)(2,1)S(1)}, bf16[2,12,48,128]{3,2,1,0:T(8,128)(2,1)S(1)}, u32[]{:S(2)}, u32[]{:S(2)}) %collective-permute-start.4) | collective-permute-done | bytes 294944 | tf_op jit(solution)/shard_map/ppermute | solution.py:236
  35.1 0.4 collective-permute-done.2.refs_1_.refs_5_
  35.4 0.3 select.6.refs_7_
  35.7 2.7 %collective-permute-start.10 = (bf16[2,4,48,128]{3,2,1,0:T(8,128)(2,1)S(1)}, bf16[2,4,48,128]{3,2,1,0:T(8,128)(2,1)S(1)}, u32[]{:S(2)}, u32[]{:S(2)}) collective-permute-start(bf16[2,4,48,128]{3,2,1,0:T(8,128)(2,1)S(1)} %select.6.refs_7_), channel_id=1, source_target_pairs={{0,8},{4,12},{8,0},{12,4},{1,9},{5,13},{9,1},{13,5},{2,10},{6,14},... | collective-permute-start | bytes 294920 | tf_op jit(solution)/shard_map/ppermute | solution.py:236
  38.4 0.6 gather_fusion.1
  39.0 3.6 %collective-permute-done.13.refs_9_ = bf16[2,8,48,128]{3,2,1,0:T(8,128)(2,1)S(1)} collective-permute-done((bf16[2,8,48,128]{3,2,1,0:T(8,128)(2,1)S(1)}, bf16[2,8,48,128]{3,2,1,0:T(8,128)(2,1)S(1)}, u32[]{:S(2)}, u32[]{:S(2)}) %collective-permute-start.13) | collective-permute-done | bytes 196640 | tf_op jit(solution)/shard_map/ppermute | solution.py:237
  42.6 2.9 %collective-permute-done.14.refs_11_ = bf16[2,8,48,128]{3,2,1,0:T(8,128)(2,1)S(1)} collective-permute-done((bf16[2,8,48,128]{3,2,1,0:T(8,128)(2,1)S(1)}, bf16[2,8,48,128]{3,2,1,0:T(8,128)(2,1)S(1)}, u32[]{:S(2)}, u32[]{:S(2)}) %collective-permute-start.14) | collective-permute-done | bytes 196640 | tf_op jit(solution)/shard_map/ppermute | solution.py:236
  45.5 0.7 collective-permute-start.15
  46.2 1.3 %collective-permute-start.16 = (bf16[2,8,48,128]{3,2,1,0:T(8,128)(2,1)S(1)}, bf16[2,8,48,128]{3,2,1,0:T(8,128)(2,1)S(1)}, u32[]{:S(2)}, u32[]{:S(2)}) collective-permute-start(bf16[2,8,48,128]{3,2,1,0:T(8,128)(2,1)S(1)} %collective-permute-done.14.refs_11_), channel_id=1, source_target_pairs={{8,12},{4,0},{9,13},{5,1},{10,14},{6,2},{11,15},{7,3},{24,28},{20,... | collective-permute-start | bytes 589832 | tf_op jit(solution)/shard_map/ppermute | solution.py:239
  47.5 1.3 %collective-permute-start.8 = (bf16[2,12,48,128]{3,2,1,0:T(8,128)(2,1)S(1)}, bf16[2,12,48,128]{3,2,1,0:T(8,128)(2,1)S(1)}, u32[]{:S(2)}, u32[]{:S(2)}) collective-permute-start(bf16[2,12,48,128]{3,2,1,0:T(8,128)(2,1)S(1)} %collective-permute-done.4.refs_10_), channel_id=1, source_target_pairs={{8,12},{4,0},{9,13},{5,1},{10,14},{6,2},{11,15},{7,3},{24,28},{20,... | collective-permute-start | bytes 884744 | tf_op jit(solution)/shard_map/ppermute | solution.py:239
  48.8 2.8 %collective-permute-start.9 = (bf16[2,4,48,128]{3,2,1,0:T(8,128)(2,1)S(1)}, bf16[2,4,48,128]{3,2,1,0:T(8,128)(2,1)S(1)}, u32[]{:S(2)}, u32[]{:S(2)}) collective-permute-start(bf16[2,4,48,128]{3,2,1,0:T(8,128)(2,1)S(1)} %select.6.refs_7_), channel_id=1, source_target_pairs={{0,4},{4,0},{8,12},{12,8},{1,5},{5,1},{9,13},{13,9},{2,6},{6,2},{1... | collective-permute-start | bytes 294920 | tf_op jit(solution)/shard_map/ppermute | solution.py:237
  51.6 0.7 collective-permute-start.7
  52.3 0.0 copy-start.1
  52.3 1.1 %copy-done.1 = bf16[24,48,256]{2,1,0:T(8,128)(2,1)S(1)} copy-done((bf16[24,48,256]{2,1,0:T(8,128)(2,1)S(1)}, bf16[24,48,256]{2,1,0:T(8,128)(2,1)}, u32[]{:S(2)}) %copy-start.1) | copy-done | bytes 589848
  53.4 3.8 %cross.4.refs_10_ = bf16[24,2,2,256,256]{4,3,2,1,0:T(8,128)(2,1)} custom-call(s32[3]{0:T(128)S(1)} %gather_fusion.1, f32[2,192]{1,0:T(2,128)S(1)} %broadcast_select_fusion.refs_1_, bf16[24,48,256]{2,1,0:T(8,128)(2,1)S(1)} %copy-done.1, bf16[24,48,256]{2,1,0:T(8,128)(2,1)S(1)} %collective-permute-done.refs_1_.refs_3_, ...), custom_call_target="tpu_custom_call" | custom-call | flops 5029199872 | bytes 13716000 | tf_op jit(solution)/shard_map/cross/pallas_call | solution.py:286
  57.2 5.7 %collective-permute-done.9.refs_9_ = bf16[2,4,48,128]{3,2,1,0:T(8,128)(2,1)S(1)} collective-permute-done((bf16[2,4,48,128]{3,2,1,0:T(8,128)(2,1)S(1)}, bf16[2,4,48,128]{3,2,1,0:T(8,128)(2,1)S(1)}, u32[]{:S(2)}, u32[]{:S(2)}) %collective-permute-start.9) | collective-permute-done | bytes 98336 | tf_op jit(solution)/shard_map/ppermute | solution.py:237
  62.9 0.7 collective-permute-start.11
  63.6 1.3 %collective-permute-start.12 = (bf16[2,4,48,128]{3,2,1,0:T(8,128)(2,1)S(1)}, bf16[2,4,48,128]{3,2,1,0:T(8,128)(2,1)S(1)}, u32[]{:S(2)}, u32[]{:S(2)}) collective-permute-start(bf16[2,4,48,128]{3,2,1,0:T(8,128)(2,1)S(1)} %collective-permute-done.10.refs_11_), channel_id=1, source_target_pairs={{8,12},{4,0},{9,13},{5,1},{10,14},{6,2},{11,15},{7,3},{24,28},{20,... | collective-permute-start | bytes 294920 | tf_op jit(solution)/shard_map/ppermute | solution.py:239
  64.9 2.4 %cross.5.refs_12_ = bf16[24,2,2,256,256]{4,3,2,1,0:T(8,128)(2,1)} custom-call(s32[1]{0:T(128)} %slice.5.refs_0_, f32[2,192]{1,0:T(2,128)S(1)} %broadcast_select_fusion.refs_1_, bf16[24,48,256]{2,1,0:T(8,128)(2,1)S(1)} %copy-done.1, bf16[24,48,256]{2,1,0:T(8,128)(2,1)S(1)} %collective-permute-done.refs_1_.refs_3_, ...), custom_call_target="tpu_custom_call", output_to_operand_aliasing={{}: (10, {})} | custom-call | flops 2776399872 | bytes 7572000 | tf_op jit(solution)/shard_map/cross/pallas_call | solution.py:286
  67.4 2.7 %cross.6.refs_10_ = bf16[24,2,2,256,256]{4,3,2,1,0:T(8,128)(2,1)} custom-call(s32[3]{0:T(128)S(1)} %gather_fusion.1, f32[2,192]{1,0:T(2,128)S(1)} %broadcast_select_fusion.refs_1_, bf16[24,48,256]{2,1,0:T(8,128)(2,1)S(1)} %copy-done.1, bf16[24,48,256]{2,1,0:T(8,128)(2,1)S(1)} %collective-permute-done.refs_1_.refs_3_, ...), custom_call_target="tpu_custom_call", output_to_operand_aliasing={{}: (12, {})} | custom-call | flops 3339599872 | bytes 9108000 | tf_op jit(solution)/shard_map/cross/pallas_call | solution.py:286
  70.1 1.9 %cross.7 = bf16[24,2,2,256,256]{4,3,2,1,0:T(8,128)(2,1)} custom-call(s32[1]{0:T(128)} %slice.5.refs_0_, f32[2,192]{1,0:T(2,128)S(1)} %broadcast_select_fusion.refs_1_, bf16[24,48,256]{2,1,0:T(8,128)(2,1)S(1)} %copy-done.1, bf16[24,48,256]{2,1,0:T(8,128)(2,1)S(1)} %collective-permute-done.refs_1_.refs_3_, ...), custom_call_target="tpu_custom_call", output_to_operand_aliasing={{}: (10, {})} | custom-call | flops 2213199872 | bytes 6036000 | tf_op jit(solution)/shard_map/cross/pallas_call | solution.py:286
  (27 shorter events, 0.1 us)
Async XLA Ops:
  0.0 12.1 %copy-start.4 = (s32[88]{0:T(128)S(1)}, s32[88]{0:T(128)}, u32[]{:S(2)}) copy-start(s32[88]{0:T(128)} %param.14) | copy-start | bytes 1060
  0.0 12.2 %copy-start.2 = (s32[88]{0:T(128)S(1)}, s32[88]{0:T(128)}, u32[]{:S(2)}) copy-start(s32[88]{0:T(128)} %param.15) | copy-start | bytes 1060
  0.0 12.3 %copy-start.3 = (s32[256]{0:T(256)S(1)}, s32[256]{0:T(256)}, u32[]{:S(2)}) copy-start(s32[256]{0:T(256)} %param.16) | copy-start | bytes 3076
  6.9 13.2 %collective-permute-start.5 = (bf16[16,48,256]{2,1,0:T(8,128)(2,1)}, bf16[16,48,256]{2,1,0:T(8,128)(2,1)S(1)}, u32[]{:S(2)}, u32[]{:S(2)}) collective-permute-start(bf16[16,48,256]{2,1,0:T(8,128)(2,1)} %get-tuple-element.28), channel_id=1, source_target_pairs={{0,2},{1,3},{2,0},{3,1},{4,6},{5,7},{6,4},{7,5},{8,10},{9,11},{10,... | collective-permute-start | bytes 1179656 | tf_op jit(solution)/shard_map/ppermute | solution.py:212
  9.9 18.3 %collective-permute-start.6 = (bf16[16,48,256]{2,1,0:T(8,128)(2,1)}, bf16[16,48,256]{2,1,0:T(8,128)(2,1)S(1)}, u32[]{:S(2)}, u32[]{:S(2)}) collective-permute-start(bf16[16,48,256]{2,1,0:T(8,128)(2,1)} %get-tuple-element.29), channel_id=1, source_target_pairs={{0,3},{1,2},{2,1},{3,0},{4,7},{5,6},{6,5},{7,4},{8,11},{9,10},{10,... | collective-permute-start | bytes 1179656 | tf_op jit(solution)/shard_map/ppermute | solution.py:212
  9.9 2.6 %collective-permute-start = (bf16[24,48,256]{2,1,0:T(8,128)(2,1)}, bf16[24,48,256]{2,1,0:T(8,128)(2,1)S(1)}, u32[]{:S(2)}, u32[]{:S(2)}) collective-permute-start(bf16[24,48,256]{2,1,0:T(8,128)(2,1)} %get-tuple-element.23), channel_id=1, source_target_pairs={{0,1},{1,0},{2,3},{3,2},{4,5},{5,4},{6,7},{7,6},{8,9},{9,8},{10,11... | collective-permute-start | bytes 1769480 | tf_op jit(solution)/shard_map/ppermute | solution.py:212
  10.1 25.0 %collective-permute-start.1 = (bf16[8,48,256]{2,1,0:T(8,128)(2,1)}, bf16[8,48,256]{2,1,0:T(8,128)(2,1)S(1)}, u32[]{:S(2)}, u32[]{:S(2)}) collective-permute-start(bf16[8,48,256]{2,1,0:T(8,128)(2,1)} %get-tuple-element.24), channel_id=1, source_target_pairs={{0,2},{1,3},{2,0},{3,1},{4,6},{5,7},{6,4},{7,5},{8,10},{9,11},{10,... | collective-permute-start | bytes 589832 | tf_op jit(solution)/shard_map/ppermute | solution.py:212
  12.1 23.4 %collective-permute-start.2 = (bf16[8,48,256]{2,1,0:T(8,128)(2,1)}, bf16[8,48,256]{2,1,0:T(8,128)(2,1)S(1)}, u32[]{:S(2)}, u32[]{:S(2)}) collective-permute-start(bf16[8,48,256]{2,1,0:T(8,128)(2,1)} %get-tuple-element.25), channel_id=1, source_target_pairs={{0,3},{1,2},{2,1},{3,0},{4,7},{5,6},{6,5},{7,4},{8,11},{9,10},{10,... | collective-permute-start | bytes 589832 | tf_op jit(solution)/shard_map/ppermute | solution.py:212
  12.5 1.1 %copy-start = (bf16[24,48,256]{2,1,0:T(8,128)(2,1)S(1)}, bf16[24,48,256]{2,1,0:T(8,128)(2,1)}, u32[]{:S(2)}) copy-start(bf16[24,48,256]{2,1,0:T(8,128)(2,1)} %get-tuple-element.22.refs_0_.refs_2_) | copy-start | bytes 1769476
  14.1 16.1 %collective-permute-start.3 = (bf16[2,12,48,128]{3,2,1,0:T(8,128)(2,1)S(1)}, bf16[2,12,48,128]{3,2,1,0:T(8,128)(2,1)S(1)}, u32[]{:S(2)}, u32[]{:S(2)}) collective-permute-start(bf16[2,12,48,128]{3,2,1,0:T(8,128)(2,1)S(1)} %select.4.refs_6_), channel_id=1, source_target_pairs={{0,4},{4,0},{8,12},{12,8},{1,5},{5,1},{9,13},{13,9},{2,6},{6,2},{1... | collective-permute-start | bytes 884744 | tf_op jit(solution)/shard_map/ppermute | solution.py:237
  20.1 15.0 %collective-permute-start.4 = (bf16[2,12,48,128]{3,2,1,0:T(8,128)(2,1)S(1)}, bf16[2,12,48,128]{3,2,1,0:T(8,128)(2,1)S(1)}, u32[]{:S(2)}, u32[]{:S(2)}) collective-permute-start(bf16[2,12,48,128]{3,2,1,0:T(8,128)(2,1)S(1)} %select.4.refs_6_), channel_id=1, source_target_pairs={{0,8},{4,12},{8,0},{12,4},{1,9},{5,13},{9,1},{13,5},{2,10},{6,14},... | collective-permute-start | bytes 884744 | tf_op jit(solution)/shard_map/ppermute | solution.py:236
  28.5 14.0 %collective-permute-start.13 = (bf16[2,8,48,128]{3,2,1,0:T(8,128)(2,1)S(1)}, bf16[2,8,48,128]{3,2,1,0:T(8,128)(2,1)S(1)}, u32[]{:S(2)}, u32[]{:S(2)}) collective-permute-start(bf16[2,8,48,128]{3,2,1,0:T(8,128)(2,1)S(1)} %select.5.refs_7_), channel_id=1, source_target_pairs={{0,4},{4,0},{8,12},{12,8},{1,5},{5,1},{9,13},{13,9},{2,6},{6,2},{1... | collective-permute-start | bytes 589832 | tf_op jit(solution)/shard_map/ppermute | solution.py:237
  30.2 15.3 %collective-permute-start.14 = (bf16[2,8,48,128]{3,2,1,0:T(8,128)(2,1)S(1)}, bf16[2,8,48,128]{3,2,1,0:T(8,128)(2,1)S(1)}, u32[]{:S(2)}, u32[]{:S(2)}) collective-permute-start(bf16[2,8,48,128]{3,2,1,0:T(8,128)(2,1)S(1)} %select.5.refs_7_), channel_id=1, source_target_pairs={{0,8},{4,12},{8,0},{12,4},{1,9},{5,13},{9,1},{13,5},{2,10},{6,14},... | collective-permute-start | bytes 589832 | tf_op jit(solution)/shard_map/ppermute | solution.py:236
  35.7 15.9 %collective-permute-start.10 = (bf16[2,4,48,128]{3,2,1,0:T(8,128)(2,1)S(1)}, bf16[2,4,48,128]{3,2,1,0:T(8,128)(2,1)S(1)}, u32[]{:S(2)}, u32[]{:S(2)}) collective-permute-start(bf16[2,4,48,128]{3,2,1,0:T(8,128)(2,1)S(1)} %select.6.refs_7_), channel_id=1, source_target_pairs={{0,8},{4,12},{8,0},{12,4},{1,9},{5,13},{9,1},{13,5},{2,10},{6,14},... | collective-permute-start | bytes 294920 | tf_op jit(solution)/shard_map/ppermute | solution.py:236
  45.5 18.0 %collective-permute-start.15 = (bf16[2,8,48,128]{3,2,1,0:T(8,128)(2,1)S(1)}, bf16[2,8,48,128]{3,2,1,0:T(8,128)(2,1)S(1)}, u32[]{:S(2)}, u32[]{:S(2)}) collective-permute-start(bf16[2,8,48,128]{3,2,1,0:T(8,128)(2,1)S(1)} %select.5.refs_7_), channel_id=1, source_target_pairs={{4,8},{8,4},{5,9},{9,5},{6,10},{10,6},{7,11},{11,7},{20,24},{24,20... | collective-permute-start | bytes 589832 | tf_op jit(solution)/shard_map/ppermute | solution.py:240
  46.2 18.7 %collective-permute-start.16 = (bf16[2,8,48,128]{3,2,1,0:T(8,128)(2,1)S(1)}, bf16[2,8,48,128]{3,2,1,0:T(8,128)(2,1)S(1)}, u32[]{:S(2)}, u32[]{:S(2)}) collective-permute-start(bf16[2,8,48,128]{3,2,1,0:T(8,128)(2,1)S(1)} %collective-permute-done.14.refs_11_), channel_id=1, source_target_pairs={{8,12},{4,0},{9,13},{5,1},{10,14},{6,2},{11,15},{7,3},{24,28},{20,... | collective-permute-start | bytes 589832 | tf_op jit(solution)/shard_map/ppermute | solution.py:239
  47.5 17.4 %collective-permute-start.8 = (bf16[2,12,48,128]{3,2,1,0:T(8,128)(2,1)S(1)}, bf16[2,12,48,128]{3,2,1,0:T(8,128)(2,1)S(1)}, u32[]{:S(2)}, u32[]{:S(2)}) collective-permute-start(bf16[2,12,48,128]{3,2,1,0:T(8,128)(2,1)S(1)} %collective-permute-done.4.refs_10_), channel_id=1, source_target_pairs={{8,12},{4,0},{9,13},{5,1},{10,14},{6,2},{11,15},{7,3},{24,28},{20,... | collective-permute-start | bytes 884744 | tf_op jit(solution)/shard_map/ppermute | solution.py:239
  48.8 14.1 %collective-permute-start.9 = (bf16[2,4,48,128]{3,2,1,0:T(8,128)(2,1)S(1)}, bf16[2,4,48,128]{3,2,1,0:T(8,128)(2,1)S(1)}, u32[]{:S(2)}, u32[]{:S(2)}) collective-permute-start(bf16[2,4,48,128]{3,2,1,0:T(8,128)(2,1)S(1)} %select.6.refs_7_), channel_id=1, source_target_pairs={{0,4},{4,0},{8,12},{12,8},{1,5},{5,1},{9,13},{13,9},{2,6},{6,2},{1... | collective-permute-start | bytes 294920 | tf_op jit(solution)/shard_map/ppermute | solution.py:237
  51.6 13.2 %collective-permute-start.7 = (bf16[2,12,48,128]{3,2,1,0:T(8,128)(2,1)S(1)}, bf16[2,12,48,128]{3,2,1,0:T(8,128)(2,1)S(1)}, u32[]{:S(2)}, u32[]{:S(2)}) collective-permute-start(bf16[2,12,48,128]{3,2,1,0:T(8,128)(2,1)S(1)} %select.4.refs_6_), channel_id=1, source_target_pairs={{4,8},{8,4},{5,9},{9,5},{6,10},{10,6},{7,11},{11,7},{20,24},{24,20... | collective-permute-start | bytes 884744 | tf_op jit(solution)/shard_map/ppermute | solution.py:240
  52.3 1.1 %copy-start.1 = (bf16[24,48,256]{2,1,0:T(8,128)(2,1)S(1)}, bf16[24,48,256]{2,1,0:T(8,128)(2,1)}, u32[]{:S(2)}) copy-start(bf16[24,48,256]{2,1,0:T(8,128)(2,1)} %get-tuple-element.22.refs_0_.refs_2_) | copy-start | bytes 1769476
  62.9 7.2 %collective-permute-start.11 = (bf16[2,4,48,128]{3,2,1,0:T(8,128)(2,1)S(1)}, bf16[2,4,48,128]{3,2,1,0:T(8,128)(2,1)S(1)}, u32[]{:S(2)}, u32[]{:S(2)}) collective-permute-start(bf16[2,4,48,128]{3,2,1,0:T(8,128)(2,1)S(1)} %select.6.refs_7_), channel_id=1, source_target_pairs={{4,8},{8,4},{5,9},{9,5},{6,10},{10,6},{7,11},{11,7},{20,24},{24,20... | collective-permute-start | bytes 294920 | tf_op jit(solution)/shard_map/ppermute | solution.py:240
  63.6 6.5 %collective-permute-start.12 = (bf16[2,4,48,128]{3,2,1,0:T(8,128)(2,1)S(1)}, bf16[2,4,48,128]{3,2,1,0:T(8,128)(2,1)S(1)}, u32[]{:S(2)}, u32[]{:S(2)}) collective-permute-start(bf16[2,4,48,128]{3,2,1,0:T(8,128)(2,1)S(1)} %collective-permute-done.10.refs_11_), channel_id=1, source_target_pairs={{8,12},{4,0},{9,13},{5,1},{10,14},{6,2},{11,15},{7,3},{24,28},{20,... | collective-permute-start | bytes 294920 | tf_op jit(solution)/shard_map/ppermute | solution.py:239

commit v4 on v3

--- a/solution.py
+++ b/solution.py
@@ -2,8 +2,6 @@
 
 import jax
 import jax.numpy as jnp
-import numpy as np
-import ml_dtypes
 from jax import lax
 from jax.experimental import pallas as pl
 from jax.experimental.pallas import tpu as pltpu
@@ -12,18 +10,9 @@
 F = 96
 K0 = 8
 G = 2
-PARTS = (2, 1)
+PARTS = (1,)
 f32 = jnp.float32
 bf16 = jnp.bfloat16
-
-
-def make_table(length):
-    freqs = K0 + np.arange(F)
-    phase = freqs[:, None] * np.arange(length)[None, :] % length
-    angle = phase.astype(np.float32) * np.float32(2.0 * math.pi / length)
-    scale = np.float32(1.0 / math.sqrt(length))
-    table = np.stack([np.cos(angle) * scale, -np.sin(angle) * scale], axis=1)
-    return table.astype(np.float32).astype(ml_dtypes.bfloat16)
 
 
 def up(n, m):
@@ -35,57 +24,53 @@
     return sizes[:-1] + [bins - sum(sizes[:-1])]
 
 
-def head_kernel(cfg, order, samples_hbm, table_hbm, *refs):
+def head_kernel(cfg, samples_hbm, *refs):
     win, wpad, n_tf, bins, sizes = cfg
-    outs, (samples, table, tscr, spec, buf, sem) = refs[:-6], refs[-6:]
-    load_table = pltpu.make_async_copy(table_hbm, table, sem.at[0])
-    load_samples = pltpu.make_async_copy(samples_hbm, samples, sem.at[1])
-    load_table.start()
-    load_samples.start()
+    outs, (samples, table, spec, sem) = refs[:-4], refs[-4:]
+    load = pltpu.make_async_copy(samples_hbm, samples, sem)
+    load.start()
+    shape = table.shape
+    length = shape[1]
+    row = lax.broadcasted_iota(jnp.int32, (shape[0], 1), 0)
+    owner = lax.axis_index("tf") ^ (row // (2 * bins))
+    freq = K0 + owner * bins + (row % (2 * bins)) // 2
+    phase = freq * lax.broadcasted_iota(jnp.int32, shape, 1)
+    phase = (phase + (row % 2) * (length // 4)) % length
+    angle = phase.astype(f32) * (2.0 * math.pi / length)
+    table[...] = (jnp.cos(angle) * (1.0 / math.sqrt(length))).astype(bf16)
     to = lax.broadcasted_iota(jnp.int32, (128, 128), 0)
     at = lax.broadcasted_iota(jnp.int32, (128, 128), 1)
     shuffle = ((to % 8 == at // 16) & (to // 8 == at % 16)).astype(f32).astype(bf16)
     for w in range(win, wpad):
         spec[w] = jnp.zeros(spec.shape[1:], bf16)
-    load_table.wait()
-    rows = [table[order[k]].astype(f32) for k in range(n_tf)]
-    tscr[...] = jnp.concatenate(rows, axis=0).astype(bf16)
-    load_samples.wait()
+    load.wait()
     for w in range(win):
         x = samples[w]
         xf = x.astype(f32)
         power = jnp.mean(xf * xf, axis=0, keepdims=True)
-        y = jnp.dot(tscr[...], x, preferred_element_type=f32)
+        y = jnp.dot(table[...], x, preferred_element_type=f32)
         spec[w] = (y * lax.rsqrt(power + 1e-06)).astype(bf16)
-    spans = [(0, bins), (bins, bins)]
-    for k in range(2, n_tf):
-        base = k * bins
-        for size in sizes:
-            spans.append((base, size))
-            base += size
-    stores = [
-        pltpu.make_async_copy(buf.at[pl.ds(base, size)], out, sem.at[2 + i])
-        for i, ((base, size), out) in enumerate(zip(spans, outs))
-    ]
-    done = set()
-    for grp in reversed(range(2 * F // 16)):
+    for grp in range(2 * F // 16):
         parts = []
         for wg in range(wpad // 8):
             block = spec[8 * wg : 8 * wg + 8, 16 * grp : 16 * grp + 16, :]
             block = block.reshape(128, block.shape[-1])
             parts.append(jnp.dot(shuffle, block, preferred_element_type=f32))
         for j in range(8):
+            flat = grp * 8 + j
+            k, f = flat // bins, flat % bins
             pieces = []
             for r in range(2):
                 row = (2 * j + r) * 8
                 pieces += [p[row : row + 8] for p in parts]
-            buf[grp * 8 + j] = jnp.concatenate(pieces, axis=0).astype(bf16)
-        for i, (base, _) in enumerate(spans):
-            if base >= grp * 8 and i not in done:
-                done.add(i)
-                stores[i].start()
-    for store in stores:
-        store.wait()
+            value = jnp.concatenate(pieces, axis=0).astype(bf16)
+            if k < 2:
+                outs[k][f] = value
+            else:
+                q = 0
+                while f >= sizes[q]:
+                    f, q = f - sizes[q], q + 1
+                outs[2 + (k - 2) * len(sizes) + q][f] = value
 
 
 def select_kernel(cols, *refs):
@@ -101,8 +86,10 @@
             out[d, p] = jnp.where(first, got[:rows], got[rows:]).astype(bf16)
 
 
-def cross_kernel(cfg, blk, coef, *refs):
-    wpad, scale, n_slab, counts, lead = cfg
+def cross_kernel(cfg, coef, *refs):
+    wpad, scale, n_slab, counts, lead, owners = cfg
+    pos = lax.axis_index("chan")
+    blk = owners(pos)
     out, buf, sem = refs[-3:]
     slabs, rest = refs[:n_slab], refs[n_slab:-3]
     panels = []
@@ -181,8 +168,6 @@
     chunks = len(sizes)
     rows = 2 * wpad
     order = (me ^ jnp.arange(n_tf, dtype=jnp.int32)).astype(jnp.int32)
-    table = jnp.asarray(make_table(length).reshape(n_tf, 2 * bins, length))
-    smem = pl.BlockSpec(memory_space=pltpu.SMEM)
     vmem = pl.BlockSpec(memory_space=pltpu.VMEM)
     hbm = pl.BlockSpec(memory_space=pltpu.HBM)
 
@@ -191,31 +176,25 @@
         shapes += [jax.ShapeDtypeStruct((size, rows, chans), bf16) for size in sizes]
     got = pl.pallas_call(
         lambda *refs: head_kernel((win, wpad, n_tf, bins, sizes), *refs),
-        in_specs=[smem, hbm, hbm],
-        out_specs=[hbm] * len(shapes),
+        in_specs=[hbm],
+        out_specs=[vmem] * len(shapes),
         out_shape=shapes,
         scratch_shapes=[
             pltpu.VMEM(samples.shape, bf16),
-            pltpu.VMEM(table.shape, bf16),
             pltpu.VMEM((2 * F, length), bf16),
             pltpu.VMEM((wpad, 2 * F, chans), bf16),
-            pltpu.VMEM((F, rows, chans), bf16),
-            pltpu.SemaphoreType.DMA((2 + len(shapes),)),
+            pltpu.SemaphoreType.DMA,
         ],
-        compiler_params=pltpu.CompilerParams(vmem_limit_bytes=57 * 1024 * 1024),
+        compiler_params=pltpu.CompilerParams(vmem_limit_bytes=50 * 1024 * 1024),
         cost_estimate=cost(5),
         name="head",
-    )(order, samples, table)
+    )(samples)
     own, for_core = got[0], got[1]
 
     def across(value, k):
         return lax.ppermute(value, "tf", [(i, i ^ k) for i in range(n_tf)])
 
     core = across(for_core, 1)
-    far = [
-        [across(got[2 + (k - 2) * chunks + q], k) for k in range(2, n_tf)] for q in range(chunks)
-    ]
-
     mine = lax.dynamic_slice_in_dim(sources, pos * src, src, 0) - pos * chans
     cols = jnp.concatenate([mine, mine])[None, :]
 
@@ -244,12 +223,6 @@
             for k in range(1, n_chan)
         ]
 
-    if n_chan == 4:
-        blk = pos ^ jnp.arange(4, dtype=jnp.int32)
-    else:
-        blk = (pos - jnp.arange(n_chan, dtype=jnp.int32)) % n_chan
-    blk = blk.astype(jnp.int32)
-
     coef = jnp.where(
         substack[None, :] == jnp.arange(G, dtype=jnp.int32)[:, None],
         (quality[None, :].astype(f32) + 1.0) / 4.0,
@@ -259,13 +232,21 @@
     coef = jnp.take(jnp.concatenate([coef, coef], axis=2), order, axis=1).reshape(G, n_tf * rows)
     scale = 1.0 / math.sqrt(win * n_tf)
 
-    near = spread(select([own, core]))
-    away, before = [], [near[1][0], near[2][0]]
+    outgoing = [[got[2 + k * chunks + q] for k in range(n_tf - 2)] for q in range(chunks)]
+    panel = select([own, core])
+    far, away = [], []
     for q in range(chunks):
         if q:
-            *far[q], _, _, _ = lax.optimization_barrier((*far[q], *before, panel))
+            *outgoing[q], panel = lax.optimization_barrier((*outgoing[q], panel))
+        far.append([across(value, k + 2) for k, value in enumerate(outgoing[q])])
+    near = spread(panel)
+    before = near[1] + near[2]
+    for q in range(chunks):
+        *far[q], panel = lax.optimization_barrier((*far[q], panel, *before))[: n_tf - 1]
         panel = select(far[q])
+        weights, panel = lax.optimization_barrier((coef, panel))
         away.append(spread(panel))
+        before = away[q][1] + away[q][2]
     out_shape = jax.ShapeDtypeStruct((bins, G, 2, src * n_chan, chans), bf16)
     groups = [[0, 1, 2], [3]] if n_chan == 4 else [list(range(n_chan))]
     stacks = None
@@ -276,7 +257,11 @@
             for b in group:
                 args += near[b] + away[q][b]
                 counts.append((len(near[b]), len(away[q][b])))
-            cfg = (wpad, scale, n_tf, counts, sum(sizes[:q]) // 2)
+
+            def owners(at, group=group):
+                return [at ^ b if n_chan == 4 else lax.rem(at - b + n_chan, n_chan) for b in group]
+
+            cfg = (wpad, scale, n_tf, counts, sum(sizes[:q]) // 2, owners)
             first = stacks is None
             extra = [] if first else [stacks]
 
@@ -285,18 +270,18 @@
 
             stacks = pl.pallas_call(
                 body,
-                in_specs=[smem] + [vmem] * (1 + len(args)) + [hbm] * len(extra),
+                in_specs=[vmem] * (1 + len(args)) + [hbm] * len(extra),
                 out_specs=hbm,
                 out_shape=out_shape,
                 scratch_shapes=[
                     pltpu.VMEM((pairs, 2, G, 2, len(group) * src, chans), bf16),
                     pltpu.SemaphoreType.DMA((pairs, len(group))),
                 ],
-                input_output_aliases={} if first else {2 + len(args): 0},
+                input_output_aliases={} if first else {1 + len(args): 0},
                 compiler_params=pltpu.CompilerParams(vmem_limit_bytes=20 * 1024 * 1024),
                 cost_estimate=cost(1.5 + size * len(group) * src / 1000),
                 name="cross",
-            )(blk[np.array(group)], coef, *args, *extra)
+            )(weights, *args, *extra)
     return stacks
 
 

time: 72.4 us -> 66.3 us (0.916)
  waiting for transfers between devices: 22.7 us -> 33 us
  starting transfers between devices: 25.5 us -> 15.8 us
  Pallas kernels: 18.4 us -> 14.7 us
  local copies, waits for them, and re-layouts: 4.38 us -> 1.58 us
    ppermute x3 -> x2, waiting for transfers between devices: 4.61 us -> 22.4 us  [spread(): two = lax.ppermute(panel, 'chan', [(i, i ^ 2) for i in range(4)])]
    ppermute x3 -> x2, waiting for transfers between devices: 9.24 us -> 0.57 us  [spread(): one = lax.ppermute(panel, 'chan', [(i, i ^ 1) for i in range(4)])]
    ppermute x3 -> x2, waiting for transfers between devices: 0.01 us -> 4.7 us  [spread(): end = lax.ppermute(two, 'chan', [(2, 3), (1, 0)])]
    ppermute x5 -> x3, waiting for transfers between devices: 8.88 us -> 5.32 us  [across(): return lax.ppermute(value, 'tf', [(i, i ^ k) for i in range(n_tf)])]
    pallas_call x4 -> x2, Pallas kernels: 10.9 us -> 7.95 us  [shards(): pl.pallas_call(body, in_specs=[vmem] * (1 + len(args)) + [hbm] * len(extr...]
    ppermute x3 -> x2, starting transfers between devices: 6.11 us -> 3.16 us  [spread(): one = lax.ppermute(panel, 'chan', [(i, i ^ 1) for i in range(4)])]
    ppermute x3 -> x2, starting transfers between devices: 8.4 us -> 5.53 us  [spread(): two = lax.ppermute(panel, 'chan', [(i, i ^ 2) for i in range(4)])]
    unnamed x10 -> x6, local copies, waits for them, and re-layouts: 2.14 us -> 0.01 us
  transfers between devices with their start and end apart: 17 -> 11, of which waited for: 7 -> 7; matrix products, arithmetic and copies ran while one was open for 4% -> 4% of each run, Pallas kernels for 14% -> 10%
where the time goes in v4:
time: 66.3 us; the launch traced here: 66.1 us
  waiting for transfers between devices  33 us (50%)
  starting transfers between devices  15.8 us (24%)
  Pallas kernels  14.7 us (22%)
  local copies, waits for them, and re-layouts  1.58 us (2%)
  other arithmetic  0.94 us (1%)
    ppermute x2, waiting for transfers between devices, spread(): two = lax.ppermute(panel, 'chan', [(i, i ^ 2) for i in range(4)])  22.4 us
    pallas_call x2, Pallas kernels, shards(): pl.pallas_call(body, in_specs=[vmem] * (1 + len(args)) + [hbm] * len(extr...  7.95 us
    ppermute x2, starting transfers between devices, spread(): two = lax.ppermute(panel, 'chan', [(i, i ^ 2) for i in range(4)])  5.53 us
    ppermute x3, waiting for transfers between devices, across(): return lax.ppermute(value, 'tf', [(i, i ^ k) for i in range(n_tf)])  5.32 us
    pallas_call x1, Pallas kernels, shards(): pl.pallas_call(lambda *refs: head_kernel((win, wpad, n_tf, bins, sizes),...  5.16 us
    ppermute x2, waiting for transfers between devices, spread(): end = lax.ppermute(two, 'chan', [(2, 3), (1, 0)])  4.7 us
    ppermute x3, starting transfers between devices, across(): return lax.ppermute(value, 'tf', [(i, i ^ k) for i in range(n_tf)])  3.2 us
    ppermute x2, starting transfers between devices, spread(): one = lax.ppermute(panel, 'chan', [(i, i ^ 1) for i in range(4)])  3.16 us
  transfers between devices with their start and end apart: 11, of which 7 were waited for; matrix products, arithmetic and copies ran while one was open for 4% of the time, Pallas kernels for 10%

profile of v4, /device:TPU:0, one launch (start us, length us, event | category | flops | bytes accessed | tf_op | source)
XLA Modules:
  0.0 66.1 jit_solution(3279955314613582325)
XLA Ops:
  0.0 0.0 copy-start.2
  0.0 0.0 copy-start
  0.0 0.0 copy-start.1
  0.0 5.2 %head.1 = (bf16[24,48,256]{2,1,0:T(8,128)(2,1)S(1)}, bf16[24,48,256]{2,1,0:T(8,128)(2,1)}, bf16[24,48,256]{2,1,0:T(8,128)(2,1)S(1)}, bf16[24,48,256]{2,1,0:T(8,128)(2,1)S(1)}) custom-call(bf16[22,512,256]{2,1,0:T(8,128)(2,1)} %refs_0_.1), custom_call_target="tpu_custom_call" | custom-call | flops 5500000256 | bytes 15000000 | tf_op jit(solution)/shard_map/head/pallas_call | solution.py:177
  5.2 3.0 %collective-permute-start = (bf16[24,48,256]{2,1,0:T(8,128)(2,1)S(1)}, bf16[24,48,256]{2,1,0:T(8,128)(2,1)S(1)}, u32[]{:S(2)}, u32[]{:S(2)}) collective-permute-start(bf16[24,48,256]{2,1,0:T(8,128)(2,1)S(1)} %get-tuple-element.19), channel_id=1, source_target_pairs={{0,2},{1,3},{2,0},{3,1},{4,6},{5,7},{6,4},{7,5},{8,10},{9,11},{10,... | collective-permute-start | bytes 1769480 | tf_op jit(solution)/shard_map/ppermute | solution.py:195
  8.2 0.0 collective-permute-start.1
  8.2 0.2 collective-permute-start.2
  8.4 0.0 copy-done.2
  8.4 0.1 broadcast_in_dim.34
  8.5 0.7 %broadcast_in_dim.35 = pred[192]{0:T(512)(128)(4,1)} reshape(pred[4,48]{1,0:T(4,128)(4,1)S(1)} %broadcast_in_dim.34) | data formatting | bytes 384 | tf_op jit(solution)/shard_map/jit(_take)/broadcast_in_dim | solution.py:232
  9.1 0.1 broadcast_in_dim.37
  9.2 0.0 copy-done
  9.2 0.1 eq.16
  9.3 0.0 copy-done.1
  9.3 0.1 dynamic-slice_subtract_fusion
  9.4 0.1 add_bitcast_fusion.cols
  9.5 0.1 pad_maximum_fusion
  9.6 0.8 %collective-permute-done.2.refs_1_.refs_2_ = bf16[24,48,256]{2,1,0:T(8,128)(2,1)S(1)} collective-permute-done((bf16[24,48,256]{2,1,0:T(8,128)(2,1)}, bf16[24,48,256]{2,1,0:T(8,128)(2,1)S(1)}, u32[]{:S(2)}, u32[]{:S(2)}) %collective-permute-start.2) | collective-permute-done | bytes 589856 | tf_op jit(solution)/shard_map/ppermute | solution.py:195
  10.4 1.2 %select.3.refs_5_ = bf16[2,12,48,128]{3,2,1,0:T(8,128)(2,1)} custom-call(s32[1,128]{1,0:T(1,128)S(1)} %add_bitcast_fusion.cols, bf16[24,48,256]{2,1,0:T(8,128)(2,1)S(1)} %get-tuple-element.21.refs_0_.refs_1_, bf16[24,48,256]{2,1,0:T(8,128)(2,1)S(1)} %collective-permute-done.2.refs_1_.refs_2_), custom_call_target="tpu_custom_call" | custom-call | flops 550000000 | bytes 1500000 | tf_op jit(solution)/shard_map/select/pallas_call | solution.py:203
  11.6 2.9 %collective-permute-start.4 = (bf16[2,12,48,128]{3,2,1,0:T(8,128)(2,1)}, bf16[2,12,48,128]{3,2,1,0:T(8,128)(2,1)}, u32[]{:S(2)}, u32[]{:S(2)}) collective-permute-start(bf16[2,12,48,128]{3,2,1,0:T(8,128)(2,1)} %select.3.refs_5_), channel_id=1, source_target_pairs={{0,8},{4,12},{8,0},{12,4},{1,9},{5,13},{9,1},{13,5},{2,10},{6,14},... | collective-permute-start | bytes 884744 | tf_op jit(solution)/shard_map/ppermute | solution.py:215
  14.4 1.6 %collective-permute-start.3 = (bf16[2,12,48,128]{3,2,1,0:T(8,128)(2,1)}, bf16[2,12,48,128]{3,2,1,0:T(8,128)(2,1)}, u32[]{:S(2)}, u32[]{:S(2)}) collective-permute-start(bf16[2,12,48,128]{3,2,1,0:T(8,128)(2,1)} %select.3.refs_5_), channel_id=1, source_target_pairs={{0,4},{4,0},{8,12},{12,8},{1,5},{5,1},{9,13},{13,9},{2,6},{6,2},{1... | collective-permute-start | bytes 884744 | tf_op jit(solution)/shard_map/ppermute | solution.py:216
  16.0 0.6 gather_fusion
  16.6 0.1 gather.7
  16.7 0.7 %broadcast_select_fusion.refs_0_ = f32[2,192]{1,0:T(2,128)S(1)} fusion(f32[2,192]{1,0:T(2,128)S(1)} %gather.7, pred[192]{0:T(512)(128)(4,1)} %broadcast_in_dim.35), kind=kLoop, calls=%fused_computation.6 | loop fusion | flops 384 | bytes 3264 | tf_op jit(solution)/shard_map/jit(_take)/select_n | solution.py:232
  17.4 11.4 %collective-permute-done.4.refs_9_ = bf16[2,12,48,128]{3,2,1,0:T(8,128)(2,1)} collective-permute-done((bf16[2,12,48,128]{3,2,1,0:T(8,128)(2,1)}, bf16[2,12,48,128]{3,2,1,0:T(8,128)(2,1)}, u32[]{:S(2)}, u32[]{:S(2)}) %collective-permute-start.4) | collective-permute-done | bytes 294944 | tf_op jit(solution)/shard_map/ppermute | solution.py:215
  28.7 0.2 collective-permute-done.3.refs_7_
  28.9 0.0 collective-permute-done.refs_0_.refs_3_
  28.9 4.5 %collective-permute-done.1.refs_1_.refs_4_ = bf16[24,48,256]{2,1,0:T(8,128)(2,1)S(1)} collective-permute-done((bf16[24,48,256]{2,1,0:T(8,128)(2,1)S(1)}, bf16[24,48,256]{2,1,0:T(8,128)(2,1)S(1)}, u32[]{:S(2)}, u32[]{:S(2)}) %collective-permute-start.1) | collective-permute-done | bytes 589856 | tf_op jit(solution)/shard_map/ppermute | solution.py:195
  33.4 0.5 select.4.refs_6_
  33.9 2.7 %collective-permute-start.8 = (bf16[2,12,48,128]{3,2,1,0:T(8,128)(2,1)S(1)}, bf16[2,12,48,128]{3,2,1,0:T(8,128)(2,1)S(1)}, u32[]{:S(2)}, u32[]{:S(2)}) collective-permute-start(bf16[2,12,48,128]{3,2,1,0:T(8,128)(2,1)S(1)} %select.4.refs_6_), channel_id=1, source_target_pairs={{0,8},{4,12},{8,0},{12,4},{1,9},{5,13},{9,1},{13,5},{2,10},{6,14},... | collective-permute-start | bytes 884744 | tf_op jit(solution)/shard_map/ppermute | solution.py:215
  36.5 1.6 %collective-permute-start.7 = (bf16[2,12,48,128]{3,2,1,0:T(8,128)(2,1)S(1)}, bf16[2,12,48,128]{3,2,1,0:T(8,128)(2,1)S(1)}, u32[]{:S(2)}, u32[]{:S(2)}) collective-permute-start(bf16[2,12,48,128]{3,2,1,0:T(8,128)(2,1)S(1)} %select.4.refs_6_), channel_id=1, source_target_pairs={{0,4},{4,0},{8,12},{12,8},{1,5},{5,1},{9,13},{13,9},{2,6},{6,2},{1... | collective-permute-start | bytes 884744 | tf_op jit(solution)/shard_map/ppermute | solution.py:216
  38.1 1.3 %collective-permute-start.6 = (bf16[2,12,48,128]{3,2,1,0:T(8,128)(2,1)}, bf16[2,12,48,128]{3,2,1,0:T(8,128)(2,1)S(1)}, u32[]{:S(2)}, u32[]{:S(2)}) collective-permute-start(bf16[2,12,48,128]{3,2,1,0:T(8,128)(2,1)} %collective-permute-done.4.refs_9_), channel_id=1, source_target_pairs={{8,12},{4,0},{9,13},{5,1},{10,14},{6,2},{11,15},{7,3},{24,28},{20,... | collective-permute-start | bytes 884744 | tf_op jit(solution)/shard_map/ppermute | solution.py:218
  39.4 0.7 %collective-permute-start.5 = (bf16[2,12,48,128]{3,2,1,0:T(8,128)(2,1)}, bf16[2,12,48,128]{3,2,1,0:T(8,128)(2,1)S(1)}, u32[]{:S(2)}, u32[]{:S(2)}) collective-permute-start(bf16[2,12,48,128]{3,2,1,0:T(8,128)(2,1)} %select.3.refs_5_), channel_id=1, source_target_pairs={{4,8},{8,4},{5,9},{9,5},{6,10},{10,6},{7,11},{11,7},{20,24},{24,20... | collective-permute-start | bytes 884744 | tf_op jit(solution)/shard_map/ppermute | solution.py:219
  40.1 11.0 %collective-permute-done.8.refs_10_ = bf16[2,12,48,128]{3,2,1,0:T(8,128)(2,1)S(1)} collective-permute-done((bf16[2,12,48,128]{3,2,1,0:T(8,128)(2,1)S(1)}, bf16[2,12,48,128]{3,2,1,0:T(8,128)(2,1)S(1)}, u32[]{:S(2)}, u32[]{:S(2)}) %collective-permute-start.8) | collective-permute-done | bytes 294944 | tf_op jit(solution)/shard_map/ppermute | solution.py:215
  51.1 0.4 collective-permute-done.7.refs_8_
  51.5 0.7 %collective-permute-start.9 = (bf16[2,12,48,128]{3,2,1,0:T(8,128)(2,1)S(1)}, bf16[2,12,48,128]{3,2,1,0:T(8,128)(2,1)S(1)}, u32[]{:S(2)}, u32[]{:S(2)}) collective-permute-start(bf16[2,12,48,128]{3,2,1,0:T(8,128)(2,1)S(1)} %select.4.refs_6_), channel_id=1, source_target_pairs={{4,8},{8,4},{5,9},{9,5},{6,10},{10,6},{7,11},{11,7},{20,24},{24,20... | collective-permute-start | bytes 884744 | tf_op jit(solution)/shard_map/ppermute | solution.py:219
  52.1 1.3 %collective-permute-start.10 = (bf16[2,12,48,128]{3,2,1,0:T(8,128)(2,1)S(1)}, bf16[2,12,48,128]{3,2,1,0:T(8,128)(2,1)S(1)}, u32[]{:S(2)}, u32[]{:S(2)}) collective-permute-start(bf16[2,12,48,128]{3,2,1,0:T(8,128)(2,1)S(1)} %collective-permute-done.8.refs_10_), channel_id=1, source_target_pairs={{8,12},{4,0},{9,13},{5,1},{10,14},{6,2},{11,15},{7,3},{24,28},{20,... | collective-permute-start | bytes 884744 | tf_op jit(solution)/shard_map/ppermute | solution.py:218
  53.4 5.6 %cross.2.refs_9_ = bf16[24,2,2,256,256]{4,3,2,1,0:T(8,128)(2,1)} custom-call(f32[2,192]{1,0:T(2,128)S(1)} %broadcast_select_fusion.refs_0_, bf16[24,48,256]{2,1,0:T(8,128)(2,1)S(1)} %get-tuple-element.21.refs_0_.refs_1_, bf16[24,48,256]{2,1,0:T(8,128)(2,1)S(1)} %collective-permute-done.2.refs_1_.refs_2_, ...), custom_call_target="tpu_custom_call" | custom-call | flops 6718799872 | bytes 18324000 | tf_op jit(solution)/shard_map/cross/pallas_call | solution.py:271
  59.0 0.0 collective-permute-done.5.refs_5_
  59.0 0.0 collective-permute-done.6.refs_6_
  59.0 0.0 collective-permute-done.9.refs_7_
  59.1 4.7 %collective-permute-done.10.refs_8_ = bf16[2,12,48,128]{3,2,1,0:T(8,128)(2,1)S(1)} collective-permute-done((bf16[2,12,48,128]{3,2,1,0:T(8,128)(2,1)S(1)}, bf16[2,12,48,128]{3,2,1,0:T(8,128)(2,1)S(1)}, u32[]{:S(2)}, u32[]{:S(2)}) %collective-permute-start.10) | collective-permute-done | bytes 294944 | tf_op jit(solution)/shard_map/ppermute | solution.py:218
  63.8 2.4 %cross.3 = bf16[24,2,2,256,256]{4,3,2,1,0:T(8,128)(2,1)} custom-call(f32[2,192]{1,0:T(2,128)S(1)} %broadcast_select_fusion.refs_0_, bf16[24,48,256]{2,1,0:T(8,128)(2,1)S(1)} %get-tuple-element.21.refs_0_.refs_1_, bf16[24,48,256]{2,1,0:T(8,128)(2,1)S(1)} %collective-permute-done.2.refs_1_.refs_2_, ...), custom_call_target="tpu_custom_call", output_to_operand_aliasing={{}: (9, {})} | custom-call | flops 3339599872 | bytes 9108000 | tf_op jit(solution)/shard_map/cross/pallas_call | solution.py:271
  (7 shorter events, 0.0 us)
Async XLA Ops:
  0.0 8.4 %copy-start.2 = (s32[88]{0:T(128)S(1)}, s32[88]{0:T(128)}, u32[]{:S(2)}) copy-start(s32[88]{0:T(128)} %param.5) | copy-start | bytes 1060
  0.0 9.2 %copy-start = (s32[88]{0:T(128)S(1)}, s32[88]{0:T(128)}, u32[]{:S(2)}) copy-start(s32[88]{0:T(128)} %param.6) | copy-start | bytes 1060
  0.0 9.3 %copy-start.1 = (s32[256]{0:T(256)S(1)}, s32[256]{0:T(256)}, u32[]{:S(2)}) copy-start(s32[256]{0:T(256)} %param.7) | copy-start | bytes 3076
  5.2 23.7 %collective-permute-start = (bf16[24,48,256]{2,1,0:T(8,128)(2,1)S(1)}, bf16[24,48,256]{2,1,0:T(8,128)(2,1)S(1)}, u32[]{:S(2)}, u32[]{:S(2)}) collective-permute-start(bf16[24,48,256]{2,1,0:T(8,128)(2,1)S(1)} %get-tuple-element.19), channel_id=1, source_target_pairs={{0,2},{1,3},{2,0},{3,1},{4,6},{5,7},{6,4},{7,5},{8,10},{9,11},{10,... | collective-permute-start | bytes 1769480 | tf_op jit(solution)/shard_map/ppermute | solution.py:195
  8.2 25.2 %collective-permute-start.1 = (bf16[24,48,256]{2,1,0:T(8,128)(2,1)S(1)}, bf16[24,48,256]{2,1,0:T(8,128)(2,1)S(1)}, u32[]{:S(2)}, u32[]{:S(2)}) collective-permute-start(bf16[24,48,256]{2,1,0:T(8,128)(2,1)S(1)} %get-tuple-element.20), channel_id=1, source_target_pairs={{0,3},{1,2},{2,1},{3,0},{4,7},{5,6},{6,5},{7,4},{8,11},{9,10},{10,... | collective-permute-start | bytes 1769480 | tf_op jit(solution)/shard_map/ppermute | solution.py:195
  8.2 2.2 %collective-permute-start.2 = (bf16[24,48,256]{2,1,0:T(8,128)(2,1)}, bf16[24,48,256]{2,1,0:T(8,128)(2,1)S(1)}, u32[]{:S(2)}, u32[]{:S(2)}) collective-permute-start(bf16[24,48,256]{2,1,0:T(8,128)(2,1)} %get-tuple-element.22), channel_id=1, source_target_pairs={{0,1},{1,0},{2,3},{3,2},{4,5},{5,4},{6,7},{7,6},{8,9},{9,8},{10,11... | collective-permute-start | bytes 1769480 | tf_op jit(solution)/shard_map/ppermute | solution.py:195
  11.6 17.1 %collective-permute-start.4 = (bf16[2,12,48,128]{3,2,1,0:T(8,128)(2,1)}, bf16[2,12,48,128]{3,2,1,0:T(8,128)(2,1)}, u32[]{:S(2)}, u32[]{:S(2)}) collective-permute-start(bf16[2,12,48,128]{3,2,1,0:T(8,128)(2,1)} %select.3.refs_5_), channel_id=1, source_target_pairs={{0,8},{4,12},{8,0},{12,4},{1,9},{5,13},{9,1},{13,5},{2,10},{6,14},... | collective-permute-start | bytes 884744 | tf_op jit(solution)/shard_map/ppermute | solution.py:215
  14.4 14.5 %collective-permute-start.3 = (bf16[2,12,48,128]{3,2,1,0:T(8,128)(2,1)}, bf16[2,12,48,128]{3,2,1,0:T(8,128)(2,1)}, u32[]{:S(2)}, u32[]{:S(2)}) collective-permute-start(bf16[2,12,48,128]{3,2,1,0:T(8,128)(2,1)} %select.3.refs_5_), channel_id=1, source_target_pairs={{0,4},{4,0},{8,12},{12,8},{1,5},{5,1},{9,13},{13,9},{2,6},{6,2},{1... | collective-permute-start | bytes 884744 | tf_op jit(solution)/shard_map/ppermute | solution.py:216
  33.9 17.2 %collective-permute-start.8 = (bf16[2,12,48,128]{3,2,1,0:T(8,128)(2,1)S(1)}, bf16[2,12,48,128]{3,2,1,0:T(8,128)(2,1)S(1)}, u32[]{:S(2)}, u32[]{:S(2)}) collective-permute-start(bf16[2,12,48,128]{3,2,1,0:T(8,128)(2,1)S(1)} %select.4.refs_6_), channel_id=1, source_target_pairs={{0,8},{4,12},{8,0},{12,4},{1,9},{5,13},{9,1},{13,5},{2,10},{6,14},... | collective-permute-start | bytes 884744 | tf_op jit(solution)/shard_map/ppermute | solution.py:215
  36.5 14.9 %collective-permute-start.7 = (bf16[2,12,48,128]{3,2,1,0:T(8,128)(2,1)S(1)}, bf16[2,12,48,128]{3,2,1,0:T(8,128)(2,1)S(1)}, u32[]{:S(2)}, u32[]{:S(2)}) collective-permute-start(bf16[2,12,48,128]{3,2,1,0:T(8,128)(2,1)S(1)} %select.4.refs_6_), channel_id=1, source_target_pairs={{0,4},{4,0},{8,12},{12,8},{1,5},{5,1},{9,13},{13,9},{2,6},{6,2},{1... | collective-permute-start | bytes 884744 | tf_op jit(solution)/shard_map/ppermute | solution.py:216
  38.1 20.9 %collective-permute-start.6 = (bf16[2,12,48,128]{3,2,1,0:T(8,128)(2,1)}, bf16[2,12,48,128]{3,2,1,0:T(8,128)(2,1)S(1)}, u32[]{:S(2)}, u32[]{:S(2)}) collective-permute-start(bf16[2,12,48,128]{3,2,1,0:T(8,128)(2,1)} %collective-permute-done.4.refs_9_), channel_id=1, source_target_pairs={{8,12},{4,0},{9,13},{5,1},{10,14},{6,2},{11,15},{7,3},{24,28},{20,... | collective-permute-start | bytes 884744 | tf_op jit(solution)/shard_map/ppermute | solution.py:218
  39.4 19.6 %collective-permute-start.5 = (bf16[2,12,48,128]{3,2,1,0:T(8,128)(2,1)}, bf16[2,12,48,128]{3,2,1,0:T(8,128)(2,1)S(1)}, u32[]{:S(2)}, u32[]{:S(2)}) collective-permute-start(bf16[2,12,48,128]{3,2,1,0:T(8,128)(2,1)} %select.3.refs_5_), channel_id=1, source_target_pairs={{4,8},{8,4},{5,9},{9,5},{6,10},{10,6},{7,11},{11,7},{20,24},{24,20... | collective-permute-start | bytes 884744 | tf_op jit(solution)/shard_map/ppermute | solution.py:219
  51.5 7.6 %collective-permute-start.9 = (bf16[2,12,48,128]{3,2,1,0:T(8,128)(2,1)S(1)}, bf16[2,12,48,128]{3,2,1,0:T(8,128)(2,1)S(1)}, u32[]{:S(2)}, u32[]{:S(2)}) collective-permute-start(bf16[2,12,48,128]{3,2,1,0:T(8,128)(2,1)S(1)} %select.4.refs_6_), channel_id=1, source_target_pairs={{4,8},{8,4},{5,9},{9,5},{6,10},{10,6},{7,11},{11,7},{20,24},{24,20... | collective-permute-start | bytes 884744 | tf_op jit(solution)/shard_map/ppermute | solution.py:219
  52.1 11.6 %collective-permute-start.10 = (bf16[2,12,48,128]{3,2,1,0:T(8,128)(2,1)S(1)}, bf16[2,12,48,128]{3,2,1,0:T(8,128)(2,1)S(1)}, u32[]{:S(2)}, u32[]{:S(2)}) collective-permute-start(bf16[2,12,48,128]{3,2,1,0:T(8,128)(2,1)S(1)} %collective-permute-done.8.refs_10_), channel_id=1, source_target_pairs={{8,12},{4,0},{9,13},{5,1},{10,14},{6,2},{11,15},{7,3},{24,28},{20,... | collective-permute-start | bytes 884744 | tf_op jit(solution)/shard_map/ppermute | solution.py:218

commit v5 on v4

v5 whole, which is shorter than its diff:
```python
import math

import jax
import jax.numpy as jnp
from jax import lax
from jax.experimental import pallas as pl
from jax.experimental.pallas import tpu as pltpu
from jax.sharding import PartitionSpec as P

F = 96
K0 = 8
G = 2
UNROLL = 3
f32 = jnp.float32
bf16 = jnp.bfloat16


def head_kernel(cfg, samples_hbm, *refs):
    win, n_tf, bins = cfg
    outs, (samples, table, spec, sem) = refs[:-4], refs[-4:]
    load = pltpu.make_async_copy(samples_hbm, samples, sem)
    load.start()
    shape = table.shape
    length = shape[1]
    row = lax.broadcasted_iota(jnp.int32, (shape[0], 1), 0)
    owner = lax.axis_index("tf") ^ (row // (2 * bins))
    freq = K0 + owner * bins + (row % (2 * bins)) // 2
    phase = freq * lax.broadcasted_iota(jnp.int32, shape, 1)
    phase = (phase + (row % 2) * (length // 4)) % length
    turn = (phase + length // 8) // (length // 4)
    x = (phase - turn * (length // 4)).astype(f32) * (2.0 * math.pi / length)
    y = x * x
    even = 1.0 + y * (-1 / 2 + y * (1 / 24 + y * (-1 / 720 + y * (1 / 40320))))
    odd = x * (1.0 + y * (-1 / 6 + y * (1 / 120 + y * (-1 / 5040 + y * (1 / 362880)))))
    wave = jnp.where(turn % 2 == 0, even, -odd)
    wave = jnp.where((turn // 2) % 2 == 0, wave, -wave)
    table[...] = (wave * (1.0 / math.sqrt(length))).astype(bf16)
    to = lax.broadcasted_iota(jnp.int32, (16 * win, 16 * win), 0)
    at = lax.broadcasted_iota(jnp.int32, (1, 16 * win), 1)
    shuffle = (to == (at % 16) * win + at // 16).astype(f32).astype(bf16)
    load.wait()
    for w in range(win):
        x = samples[w]
        xf = x.astype(f32)
        power = jnp.mean(xf * xf, axis=0, keepdims=True)
        y = jnp.dot(table[...], x, preferred_element_type=f32)
        spec[w] = (y * lax.rsqrt(power + 1e-06)).astype(bf16)
    for grp in range(2 * F // 16):
        block = spec[:, 16 * grp : 16 * grp + 16, :].reshape(16 * win, spec.shape[-1])
        turned = jnp.dot(shuffle, block, preferred_element_type=f32).astype(bf16)
        for j in range(4):
            k, p = divmod(grp * 4 + j, bins // 2)
            outs[k][p] = turned[4 * win * j : 4 * win * (j + 1)]


def select_kernel(cols, *refs):
    slabs, out = refs[:-1], refs[-1]
    count, rows, chans = slabs[0].shape
    lanes = cols.shape[1]
    pick = (lax.broadcasted_iota(jnp.int32, (chans, lanes), 0) == cols[...]).astype(f32).astype(bf16)
    first = lax.broadcasted_iota(jnp.int32, (rows, lanes), 1) < lanes // 2
    for d, slab in enumerate(slabs):
        for p in range(count // 2):
            pair = [
                jnp.dot(slab[p + half * (count // 2)], pick, preferred_element_type=f32)
                for half in range(2)
            ]
            out[d, p] = jnp.where(first, *pair).astype(bf16)


def cross_kernel(cfg, coef, *refs):
    win, scale, n_slab, counts, owners = cfg
    pos = lax.axis_index("chan")
    blk = owners(pos)
    out, buf, sem = refs[-3:]
    slabs, rest = refs[:n_slab], refs[n_slab:-3]
    panels = []
    for near, far in counts:
        panels.append((rest[:near], rest[near : near + far]))
        rest = rest[near + far :]
    n_blk = len(panels)
    src = panels[0][0][0].shape[-1] // 2
    chans = slabs[0].shape[-1]
    tall = n_blk * src
    pairs = buf.shape[0]

    def copy_out(p, half, b):
        at = pl.ds(pl.multiple_of(blk[b] * src, src), src)
        return pltpu.make_async_copy(
            buf.at[p, half, :, :, :, pl.ds(b * src, src), :],
            out.at[pl.ds(2 * (p + half * pairs), 2), :, :, at, :],
            sem.at[p, half, b],
        )

    def pair(p, _):
        turned = [[], []]
        for group in panels:
            stack = []
            for part in group:
                for d in range(part[0].shape[0]):
                    value = part[0][d, p].astype(f32)
                    for other in part[1:]:
                        value = value + other[d, p].astype(f32)
                    stack.append(value)
            for j in range(2):
                rows = [v[2 * win * j : 2 * win * (j + 1)] for v in stack]
                turned[j].append(jnp.transpose(jnp.concatenate(rows, axis=0)))
        for half in range(2):
            values = [slab[p + half * pairs].astype(f32) for slab in slabs]
            for j in range(2):
                plain, swapped = [], []
                for v in values:
                    re = v[2 * win * j : 2 * win * j + win]
                    im = v[2 * win * j + win : 2 * win * (j + 1)]
                    plain += [re, im]
                    swapped += [im, -re]
                right = jnp.concatenate(
                    [jnp.concatenate(plain, axis=0), jnp.concatenate(swapped, axis=0)], axis=1
                ).astype(bf16)
                left = [
                    (t[src * half : src * (half + 1)] * coef[g : g + 1]).astype(bf16)
                    for g in range(G)
                    for t in turned[j]
                ]
                left = jnp.concatenate(left, axis=0)
                got = (jnp.dot(left, right, preferred_element_type=f32) * scale).astype(bf16)
                for g in range(G):
                    for o in range(2):
                        buf[p, half, j, g, o] = got[
                            g * tall : (g + 1) * tall, o * chans : (o + 1) * chans
                        ]
            for b in range(n_blk):
                copy_out(p, half, b).start()
        return 0

    lax.fori_loop(0, pairs, pair, 0, unroll=UNROLL if pairs % UNROLL == 0 else 1)
    for p in range(pairs):
        for half in range(2):
            for b in range(n_blk):
                copy_out(p, half, b).wait()


def cost(us):
    return pl.CostEstimate(flops=int(us * 1.1e9), bytes_accessed=int(us * 3e6), transcendentals=0)


def shards(samples, quality, substack, sources):
    win, length, chans = samples.shape
    n_tf = lax.axis_size("tf")
    n_chan = lax.axis_size("chan")
    me = lax.axis_index("tf")
    pos = lax.axis_index("chan")
    bins = F // n_tf
    src = sources.shape[0] // n_chan
    rows = 4 * win
    order = (me ^ jnp.arange(n_tf, dtype=jnp.int32)).astype(jnp.int32)
    vmem = pl.BlockSpec(memory_space=pltpu.VMEM)
    hbm = pl.BlockSpec(memory_space=pltpu.HBM)

    shapes = [jax.ShapeDtypeStruct((bins // 2, rows, chans), bf16)] * n_tf
    got = pl.pallas_call(
        lambda *refs: head_kernel((win, n_tf, bins), *refs),
        in_specs=[hbm],
        out_specs=[vmem] * len(shapes),
        out_shape=shapes,
        scratch_shapes=[
            pltpu.VMEM(samples.shape, bf16),
            pltpu.VMEM((2 * F, length), bf16),
            pltpu.VMEM((win, 2 * F, chans), bf16),
            pltpu.SemaphoreType.DMA,
        ],
        compiler_params=pltpu.CompilerParams(vmem_limit_bytes=50 * 1024 * 1024),
        cost_estimate=cost(5),
        name="head",
    )(samples)
    own, for_core = got[0], got[1]

    def across(value, k):
        return lax.ppermute(value, "tf", [(i, i ^ k) for i in range(n_tf)])

    core = across(for_core, 1)
    mine = lax.dynamic_slice_in_dim(sources, pos * src, src, 0) - pos * chans
    cols = jnp.concatenate([mine, mine])[None, :]

    def select(slabs):
        count = slabs[0].shape[0]
        return pl.pallas_call(
            select_kernel,
            in_specs=[vmem] * (1 + len(slabs)),
            out_specs=vmem,
            out_shape=jax.ShapeDtypeStruct((len(slabs), count // 2, rows, 2 * src), bf16),
            cost_estimate=cost(0.5),
            compiler_params=pltpu.CompilerParams(vmem_limit_bytes=12 * 1024 * 1024),
            name="select",
        )(cols, *slabs)

    def spread(panel):
        if n_chan == 4:
            two = lax.ppermute(panel, "chan", [(i, i ^ 2) for i in range(4)])
            one = lax.ppermute(panel, "chan", [(i, i ^ 1) for i in range(4)])
            later, one, two = lax.optimization_barrier((panel, one, two))
            end = lax.ppermute(two, "chan", [(2, 3), (1, 0)])
            mid = lax.ppermute(later, "chan", [(1, 2), (2, 1)])
            return [[panel], [one], [two], [mid, end]]
        return [[panel]] + [
            [lax.ppermute(panel, "chan", [(i, (i + k) % n_chan) for i in range(n_chan)])]
            for k in range(1, n_chan)
        ]

    coef = jnp.where(
        substack[None, :] == jnp.arange(G, dtype=jnp.int32)[:, None],
        (quality[None, :].astype(f32) + 1.0) / 4.0,
        0.0,
    ).reshape(G, n_tf, win)
    coef = jnp.take(jnp.concatenate([coef, coef], axis=2), order, axis=1)
    coef = coef.reshape(G, 2 * n_tf * win)
    scale = 1.0 / math.sqrt(win * n_tf)

    far = [across(value, k + 2) for k, value in enumerate(got[2:])]
    near = spread(select([own, core]))
    *far, _, _ = lax.optimization_barrier((*far, near[1][0], near[2][0]))
    away = spread(select(far))
    out_shape = jax.ShapeDtypeStruct((bins, G, 2, src * n_chan, chans), bf16)
    groups = [[0, 1, 2], [3]] if n_chan == 4 else [list(range(n_chan))]
    stacks = None
    for group in groups:
        args, counts = [own, core, *far], []
        for b in group:
            args += near[b] + away[b]
            counts.append((len(near[b]), len(away[b])))

        def owners(at, group=group):
            return [at ^ b if n_chan == 4 else lax.rem(at - b + n_chan, n_chan) for b in group]

        cfg = (win, scale, n_tf, counts, owners)
        first = stacks is None
        extra = [] if first else [stacks]

        def body(*refs, cfg=cfg, first=first):
            cross_kernel(cfg, *(refs if first else refs[:-4] + refs[-3:]))

        stacks = pl.pallas_call(
            body,
            in_specs=[vmem] * (1 + len(args)) + [hbm] * len(extra),
            out_specs=hbm,
            out_shape=out_shape,
            scratch_shapes=[
                pltpu.VMEM((bins // 4, 2, 2, G, 2, len(group) * src, chans), bf16),
                pltpu.SemaphoreType.DMA((bins // 4, 2, len(group))),
            ],
            input_output_aliases={} if first else {1 + len(args): 0},
            compiler_params=pltpu.CompilerParams(vmem_limit_bytes=20 * 1024 * 1024),
            cost_estimate=cost(1.5 + bins * len(group) * src / 1000),
            name="cross",
        )(coef, *args, *extra)
    return stacks


def solution(mesh):
    in_specs = (P(("day", "tf"), None, "chan"), P("day"), P("day"), P())
    out_specs = P("tf", "day", None, None, "chan")
    return jax.shard_map(shards, mesh=mesh, in_specs=in_specs, out_specs=out_specs, check_vma=False)
```

time: 66.3 us -> 63.7 us (0.961)
  waiting for transfers between devices: 33 us -> 27.8 us
  local copies, waits for them, and re-layouts: 1.58 us -> 4.56 us
  other arithmetic: 0.94 us -> 0.27 us
    ppermute x2, waiting for transfers between devices: 4.7 us -> 0.11 us  [spread(): end = lax.ppermute(two, 'chan', [(2, 3), (1, 0)])]
    unnamed x6 -> x18, local copies, waits for them, and re-layouts: 0.01 us -> 3.57 us
    ppermute x2, waiting for transfers between devices: 22.4 us -> 20.3 us  [spread(): two = lax.ppermute(panel, 'chan', [(i, i ^ 2) for i in range(4)])]
    ppermute x3, waiting for transfers between devices: 5.32 us -> 6.62 us  [across(): return lax.ppermute(value, 'tf', [(i, i ^ k) for i in range(n_tf)])]
    pallas_call x2, Pallas kernels: 1.63 us -> 0.93 us  [select(): pl.pallas_call(select_kernel, in_specs=[vmem] * (1 + len(slabs)), out_spe...]
    select_n x2, other arithmetic: 0.68 us -> 0.01 us  [shards(): coef = jnp.take(jnp.concatenate([coef, coef], axis=2), order, axis=1)]
  transfers between devices with their start and end apart: 11 -> 11, of which waited for: 7 -> 6; matrix products, arithmetic and copies ran while one was open for 4% -> 2% of each run, Pallas kernels for 10% -> 9%
where the time goes in v5:
time: 63.7 us; the launch traced here: 63.4 us
  waiting for transfers between devices  27.8 us (44%)
  starting transfers between devices  15.8 us (25%)
  Pallas kernels  14.8 us (23%)
  local copies, waits for them, and re-layouts  4.56 us (7%)
    ppermute x2, waiting for transfers between devices, spread(): two = lax.ppermute(panel, 'chan', [(i, i ^ 2) for i in range(4)])  20.3 us
    pallas_call x2, Pallas kernels, shards(): pl.pallas_call(body, in_specs=[vmem] * (1 + len(args)) + [hbm] * len(extr...  8.52 us
    ppermute x3, waiting for transfers between devices, across(): return lax.ppermute(value, 'tf', [(i, i ^ k) for i in range(n_tf)])  6.62 us
    ppermute x2, starting transfers between devices, spread(): two = lax.ppermute(panel, 'chan', [(i, i ^ 2) for i in range(4)])  5.61 us
    pallas_call x1, Pallas kernels, shards(): pl.pallas_call(lambda *refs: head_kernel((win, n_tf, bins), *refs), in_sp...  5.35 us
    unnamed x18, local copies, waits for them, and re-layouts  3.57 us
    ppermute x3, starting transfers between devices, across(): return lax.ppermute(value, 'tf', [(i, i ^ k) for i in range(n_tf)])  3.15 us
    ppermute x2, starting transfers between devices, spread(): one = lax.ppermute(panel, 'chan', [(i, i ^ 1) for i in range(4)])  3.15 us
  transfers between devices with their start and end apart: 11, of which 6 were waited for; matrix products, arithmetic and copies ran while one was open for 2% of the time, Pallas kernels for 9%

profile of v5, /device:TPU:0, one launch (start us, length us, event | category | flops | bytes accessed | tf_op | source)
XLA Modules:
  0.0 63.4 jit_solution(5630843567704113239)
XLA Ops:
  0.0 0.0 copy-start.8
  0.0 5.3 %head.1 = (bf16[12,88,256]{2,1,0:T(8,128)(2,1)S(1)}, bf16[12,88,256]{2,1,0:T(8,128)(2,1)}, bf16[12,88,256]{2,1,0:T(8,128)(2,1)S(1)}, bf16[12,88,256]{2,1,0:T(8,128)(2,1)S(1)}) custom-call(bf16[22,512,256]{2,1,0:T(8,128)(2,1)} %refs_0_.1), custom_call_target="tpu_custom_call" | custom-call | flops 5500000256 | bytes 15000000 | tf_op jit(solution)/shard_map/head/pallas_call | solution.py:161
  5.4 0.5 collective-permute-start
  5.9 2.6 %collective-permute-start.1 = (bf16[12,88,256]{2,1,0:T(8,128)(2,1)S(1)}, bf16[12,88,256]{2,1,0:T(8,128)(2,1)S(1)}, u32[]{:S(2)}, u32[]{:S(2)}) collective-permute-start(bf16[12,88,256]{2,1,0:T(8,128)(2,1)S(1)} %get-tuple-element.19), channel_id=1, source_target_pairs={{0,2},{1,3},{2,0},{3,1},{4,6},{5,7},{6,4},{7,5},{8,10},{9,11},{10,... | collective-permute-start | bytes 1622024 | tf_op jit(solution)/shard_map/ppermute | solution.py:179
  8.4 0.1 collective-permute-start.2
  8.5 0.0 copy-done.8
  8.5 0.1 broadcast_in_dim.37
  8.6 0.0 copy-done.6
  8.6 0.1 eq.16
  8.7 0.0 copy-done.7
  8.7 0.1 dynamic-slice_subtract_fusion
  8.8 0.1 add_bitcast_fusion.cols
  8.9 0.0 collective-permute-done.refs_1_.refs_2_
  8.9 0.5 select.2.refs_5_
  9.3 2.9 %collective-permute-start.4 = (bf16[2,6,88,128]{3,2,1,0:T(8,128)(2,1)S(1)}, bf16[2,6,88,128]{3,2,1,0:T(8,128)(2,1)S(1)}, u32[]{:S(2)}, u32[]{:S(2)}) collective-permute-start(bf16[2,6,88,128]{3,2,1,0:T(8,128)(2,1)S(1)} %select.2.refs_5_), channel_id=1, source_target_pairs={{0,8},{4,12},{8,0},{12,4},{1,9},{5,13},{9,1},{13,5},{2,10},{6,14},... | collective-permute-start | bytes 811016 | tf_op jit(solution)/shard_map/ppermute | solution.py:199
  12.2 1.6 %collective-permute-start.3 = (bf16[2,6,88,128]{3,2,1,0:T(8,128)(2,1)S(1)}, bf16[2,6,88,128]{3,2,1,0:T(8,128)(2,1)S(1)}, u32[]{:S(2)}, u32[]{:S(2)}) collective-permute-start(bf16[2,6,88,128]{3,2,1,0:T(8,128)(2,1)S(1)} %select.2.refs_5_), channel_id=1, source_target_pairs={{0,4},{4,0},{8,12},{12,8},{1,5},{5,1},{9,13},{13,9},{2,6},{6,2},{1... | collective-permute-start | bytes 811016 | tf_op jit(solution)/shard_map/ppermute | solution.py:200
  13.8 0.1 pad_maximum_fusion
  13.9 11.2 %collective-permute-done.4.refs_9_ = bf16[2,6,88,128]{3,2,1,0:T(8,128)(2,1)S(1)} collective-permute-done((bf16[2,6,88,128]{3,2,1,0:T(8,128)(2,1)S(1)}, bf16[2,6,88,128]{3,2,1,0:T(8,128)(2,1)S(1)}, u32[]{:S(2)}, u32[]{:S(2)}) %collective-permute-start.4) | collective-permute-done | bytes 270368 | tf_op jit(solution)/shard_map/ppermute | solution.py:199
  25.1 0.2 collective-permute-done.3.refs_7_
  25.3 0.7 %copy-done.2 = bf16[2,6,88,128]{3,2,1,0:T(8,128)(2,1)} copy-done((bf16[2,6,88,128]{3,2,1,0:T(8,128)(2,1)}, bf16[2,6,88,128]{3,2,1,0:T(8,128)(2,1)S(1)}, u32[]{:S(2)}) %copy-start.2) | copy-done | bytes 270360
  26.0 0.0 collective-permute-done.1.refs_0_.refs_3_
  26.0 0.0 copy-done
  26.0 6.6 %collective-permute-done.2.refs_1_.refs_4_ = bf16[12,88,256]{2,1,0:T(8,128)(2,1)S(1)} collective-permute-done((bf16[12,88,256]{2,1,0:T(8,128)(2,1)S(1)}, bf16[12,88,256]{2,1,0:T(8,128)(2,1)S(1)}, u32[]{:S(2)}, u32[]{:S(2)}) %collective-permute-start.2) | collective-permute-done | bytes 540704 | tf_op jit(solution)/shard_map/ppermute | solution.py:179
  32.6 0.5 select.3.refs_6_
  33.1 0.0 copy-start.4
  33.1 2.7 %collective-permute-start.8 = (bf16[2,6,88,128]{3,2,1,0:T(8,128)(2,1)S(1)}, bf16[2,6,88,128]{3,2,1,0:T(8,128)(2,1)}, u32[]{:S(2)}, u32[]{:S(2)}) collective-permute-start(bf16[2,6,88,128]{3,2,1,0:T(8,128)(2,1)S(1)} %select.3.refs_6_), channel_id=1, source_target_pairs={{0,8},{4,12},{8,0},{12,4},{1,9},{5,13},{9,1},{13,5},{2,10},{6,14},... | collective-permute-start | bytes 811016 | tf_op jit(solution)/shard_map/ppermute | solution.py:199
  35.8 1.6 %collective-permute-start.7 = (bf16[2,6,88,128]{3,2,1,0:T(8,128)(2,1)S(1)}, bf16[2,6,88,128]{3,2,1,0:T(8,128)(2,1)}, u32[]{:S(2)}, u32[]{:S(2)}) collective-permute-start(bf16[2,6,88,128]{3,2,1,0:T(8,128)(2,1)S(1)} %select.3.refs_6_), channel_id=1, source_target_pairs={{0,4},{4,0},{8,12},{12,8},{1,5},{5,1},{9,13},{13,9},{2,6},{6,2},{1... | collective-permute-start | bytes 811016 | tf_op jit(solution)/shard_map/ppermute | solution.py:200
  37.4 0.1 broadcast_in_dim.34
  37.5 0.1 broadcast_in_dim.35
  37.6 0.6 gather_fusion
  38.2 0.1 gather.7
  38.3 1.3 %collective-permute-start.6 = (bf16[2,6,88,128]{3,2,1,0:T(8,128)(2,1)}, bf16[2,6,88,128]{3,2,1,0:T(8,128)(2,1)S(1)}, u32[]{:S(2)}, u32[]{:S(2)}) collective-permute-start(bf16[2,6,88,128]{3,2,1,0:T(8,128)(2,1)} %copy-done), channel_id=1, source_target_pairs={{8,12},{4,0},{9,13},{5,1},{10,14},{6,2},{11,15},{7,3},{24,28},{20,... | collective-permute-start | bytes 811016 | tf_op jit(solution)/shard_map/ppermute | solution.py:202
  39.6 0.7 %collective-permute-start.5 = (bf16[2,6,88,128]{3,2,1,0:T(8,128)(2,1)S(1)}, bf16[2,6,88,128]{3,2,1,0:T(8,128)(2,1)S(1)}, u32[]{:S(2)}, u32[]{:S(2)}) collective-permute-start(bf16[2,6,88,128]{3,2,1,0:T(8,128)(2,1)S(1)} %select.2.refs_5_), channel_id=1, source_target_pairs={{4,8},{8,4},{5,9},{9,5},{6,10},{10,6},{7,11},{11,7},{20,24},{24,20... | collective-permute-start | bytes 811016 | tf_op jit(solution)/shard_map/ppermute | solution.py:203
  40.3 9.1 %collective-permute-done.8.refs_10_ = bf16[2,6,88,128]{3,2,1,0:T(8,128)(2,1)} collective-permute-done((bf16[2,6,88,128]{3,2,1,0:T(8,128)(2,1)S(1)}, bf16[2,6,88,128]{3,2,1,0:T(8,128)(2,1)}, u32[]{:S(2)}, u32[]{:S(2)}) %collective-permute-start.8) | collective-permute-done | bytes 270368 | tf_op jit(solution)/shard_map/ppermute | solution.py:199
  49.3 0.0 copy-done.4
  49.3 0.6 collective-permute-done.7.refs_8_
  49.9 0.7 %collective-permute-start.9 = (bf16[2,6,88,128]{3,2,1,0:T(8,128)(2,1)}, bf16[2,6,88,128]{3,2,1,0:T(8,128)(2,1)S(1)}, u32[]{:S(2)}, u32[]{:S(2)}) collective-permute-start(bf16[2,6,88,128]{3,2,1,0:T(8,128)(2,1)} %copy-done.4), channel_id=1, source_target_pairs={{4,8},{8,4},{5,9},{9,5},{6,10},{10,6},{7,11},{11,7},{20,24},{24,20... | collective-permute-start | bytes 811016 | tf_op jit(solution)/shard_map/ppermute | solution.py:203
  50.6 1.3 %collective-permute-start.10 = (bf16[2,6,88,128]{3,2,1,0:T(8,128)(2,1)}, bf16[2,6,88,128]{3,2,1,0:T(8,128)(2,1)S(1)}, u32[]{:S(2)}, u32[]{:S(2)}) collective-permute-start(bf16[2,6,88,128]{3,2,1,0:T(8,128)(2,1)} %collective-permute-done.8.refs_10_), channel_id=1, source_target_pairs={{8,12},{4,0},{9,13},{5,1},{10,14},{6,2},{11,15},{7,3},{24,28},{20,... | collective-permute-start | bytes 811016 | tf_op jit(solution)/shard_map/ppermute | solution.py:202
  51.9 0.0 copy-start.1
  51.9 0.9 %copy-done.1 = bf16[2,6,88,128]{3,2,1,0:T(8,128)(2,1)S(1)} copy-done((bf16[2,6,88,128]{3,2,1,0:T(8,128)(2,1)S(1)}, bf16[2,6,88,128]{3,2,1,0:T(8,128)(2,1)}, u32[]{:S(2)}) %copy-start.1) | copy-done | bytes 270360
  52.9 1.0 %copy-done.3 = bf16[2,6,88,128]{3,2,1,0:T(8,128)(2,1)S(1)} copy-done((bf16[2,6,88,128]{3,2,1,0:T(8,128)(2,1)S(1)}, bf16[2,6,88,128]{3,2,1,0:T(8,128)(2,1)}, u32[]{:S(2)}) %copy-start.3) | copy-done | bytes 270360
  53.8 1.0 %copy-done.5 = bf16[2,6,88,128]{3,2,1,0:T(8,128)(2,1)S(1)} copy-done((bf16[2,6,88,128]{3,2,1,0:T(8,128)(2,1)S(1)}, bf16[2,6,88,128]{3,2,1,0:T(8,128)(2,1)}, u32[]{:S(2)}) %copy-start.5) | copy-done | bytes 270360
  54.8 5.5 %cross.2.refs_9_ = bf16[24,2,2,256,256]{4,3,2,1,0:T(8,128)(2,1)} custom-call(f32[2,176]{1,0:T(2,128)S(1)} %broadcast_select_fusion.refs_0_, bf16[12,88,256]{2,1,0:T(8,128)(2,1)S(1)} %get-tuple-element.17.refs_0_.refs_1_, bf16[12,88,256]{2,1,0:T(8,128)(2,1)S(1)} %collective-permute-done.refs_1_.refs_2_, ...), custom_call_target="tpu_custom_call" | custom-call | flops 6718799872 | bytes 18324000 | tf_op jit(solution)/shard_map/cross/pallas_call | solution.py:242
  60.3 0.0 collective-permute-done.5.refs_5_
  60.3 0.0 collective-permute-done.6.refs_6_
  60.3 0.0 collective-permute-done.9.refs_7_
  60.3 0.1 collective-permute-done.10.refs_8_
  60.4 3.0 %cross.3 = bf16[24,2,2,256,256]{4,3,2,1,0:T(8,128)(2,1)} custom-call(f32[2,176]{1,0:T(2,128)S(1)} %broadcast_select_fusion.refs_0_, bf16[12,88,256]{2,1,0:T(8,128)(2,1)S(1)} %get-tuple-element.17.refs_0_.refs_1_, bf16[12,88,256]{2,1,0:T(8,128)(2,1)S(1)} %collective-permute-done.refs_1_.refs_2_, ...), custom_call_target="tpu_custom_call", output_to_operand_aliasing={{}: (9, {})} | custom-call | flops 3339599872 | bytes 9108000 | tf_op jit(solution)/shard_map/cross/pallas_call | solution.py:242
  (13 shorter events, 0.1 us)
Async XLA Ops:
  0.0 8.5 %copy-start.8 = (s32[88]{0:T(128)S(1)}, s32[88]{0:T(128)}, u32[]{:S(2)}) copy-start(s32[88]{0:T(128)} %param.5) | copy-start | bytes 1060
  0.0 8.6 %copy-start.6 = (s32[88]{0:T(128)S(1)}, s32[88]{0:T(128)}, u32[]{:S(2)}) copy-start(s32[88]{0:T(128)} %param.6) | copy-start | bytes 1060
  0.0 8.7 %copy-start.7 = (s32[256]{0:T(256)S(1)}, s32[256]{0:T(256)}, u32[]{:S(2)}) copy-start(s32[256]{0:T(256)} %param.7) | copy-start | bytes 3076
  5.4 3.5 %collective-permute-start = (bf16[12,88,256]{2,1,0:T(8,128)(2,1)}, bf16[12,88,256]{2,1,0:T(8,128)(2,1)S(1)}, u32[]{:S(2)}, u32[]{:S(2)}) collective-permute-start(bf16[12,88,256]{2,1,0:T(8,128)(2,1)} %get-tuple-element.18), channel_id=1, source_target_pairs={{0,1},{1,0},{2,3},{3,2},{4,5},{5,4},{6,7},{7,6},{8,9},{9,8},{10,11... | collective-permute-start | bytes 1622024 | tf_op jit(solution)/shard_map/ppermute | solution.py:179
  5.9 20.1 %collective-permute-start.1 = (bf16[12,88,256]{2,1,0:T(8,128)(2,1)S(1)}, bf16[12,88,256]{2,1,0:T(8,128)(2,1)S(1)}, u32[]{:S(2)}, u32[]{:S(2)}) collective-permute-start(bf16[12,88,256]{2,1,0:T(8,128)(2,1)S(1)} %get-tuple-element.19), channel_id=1, source_target_pairs={{0,2},{1,3},{2,0},{3,1},{4,6},{5,7},{6,4},{7,5},{8,10},{9,11},{10,... | collective-permute-start | bytes 1622024 | tf_op jit(solution)/shard_map/ppermute | solution.py:179
  8.4 24.2 %collective-permute-start.2 = (bf16[12,88,256]{2,1,0:T(8,128)(2,1)S(1)}, bf16[12,88,256]{2,1,0:T(8,128)(2,1)S(1)}, u32[]{:S(2)}, u32[]{:S(2)}) collective-permute-start(bf16[12,88,256]{2,1,0:T(8,128)(2,1)S(1)} %get-tuple-element.20), channel_id=1, source_target_pairs={{0,3},{1,2},{2,1},{3,0},{4,7},{5,6},{6,5},{7,4},{8,11},{9,10},{10,... | collective-permute-start | bytes 1622024 | tf_op jit(solution)/shard_map/ppermute | solution.py:179
  9.3 15.8 %collective-permute-start.4 = (bf16[2,6,88,128]{3,2,1,0:T(8,128)(2,1)S(1)}, bf16[2,6,88,128]{3,2,1,0:T(8,128)(2,1)S(1)}, u32[]{:S(2)}, u32[]{:S(2)}) collective-permute-start(bf16[2,6,88,128]{3,2,1,0:T(8,128)(2,1)S(1)} %select.2.refs_5_), channel_id=1, source_target_pairs={{0,8},{4,12},{8,0},{12,4},{1,9},{5,13},{9,1},{13,5},{2,10},{6,14},... | collective-permute-start | bytes 811016 | tf_op jit(solution)/shard_map/ppermute | solution.py:199
  12.2 13.1 %collective-permute-start.3 = (bf16[2,6,88,128]{3,2,1,0:T(8,128)(2,1)S(1)}, bf16[2,6,88,128]{3,2,1,0:T(8,128)(2,1)S(1)}, u32[]{:S(2)}, u32[]{:S(2)}) collective-permute-start(bf16[2,6,88,128]{3,2,1,0:T(8,128)(2,1)S(1)} %select.2.refs_5_), channel_id=1, source_target_pairs={{0,4},{4,0},{8,12},{12,8},{1,5},{5,1},{9,13},{13,9},{2,6},{6,2},{1... | collective-permute-start | bytes 811016 | tf_op jit(solution)/shard_map/ppermute | solution.py:200
  25.1 0.9 %copy-start = (bf16[2,6,88,128]{3,2,1,0:T(8,128)(2,1)}, bf16[2,6,88,128]{3,2,1,0:T(8,128)(2,1)S(1)}, u32[]{:S(2)}) copy-start(bf16[2,6,88,128]{3,2,1,0:T(8,128)(2,1)S(1)} %collective-permute-done.4.refs_9_) | copy-start | bytes 811012
  25.3 0.7 %copy-start.2 = (bf16[2,6,88,128]{3,2,1,0:T(8,128)(2,1)}, bf16[2,6,88,128]{3,2,1,0:T(8,128)(2,1)S(1)}, u32[]{:S(2)}) copy-start(bf16[2,6,88,128]{3,2,1,0:T(8,128)(2,1)S(1)} %collective-permute-done.3.refs_7_) | copy-start | bytes 811012
  33.1 16.2 %copy-start.4 = (bf16[2,6,88,128]{3,2,1,0:T(8,128)(2,1)}, bf16[2,6,88,128]{3,2,1,0:T(8,128)(2,1)S(1)}, u32[]{:S(2)}) copy-start(bf16[2,6,88,128]{3,2,1,0:T(8,128)(2,1)S(1)} %select.3.refs_6_) | copy-start | bytes 811012
  33.1 16.2 %collective-permute-start.8 = (bf16[2,6,88,128]{3,2,1,0:T(8,128)(2,1)S(1)}, bf16[2,6,88,128]{3,2,1,0:T(8,128)(2,1)}, u32[]{:S(2)}, u32[]{:S(2)}) collective-permute-start(bf16[2,6,88,128]{3,2,1,0:T(8,128)(2,1)S(1)} %select.3.refs_6_), channel_id=1, source_target_pairs={{0,8},{4,12},{8,0},{12,4},{1,9},{5,13},{9,1},{13,5},{2,10},{6,14},... | collective-permute-start | bytes 811016 | tf_op jit(solution)/shard_map/ppermute | solution.py:199
  35.8 14.1 %collective-permute-start.7 = (bf16[2,6,88,128]{3,2,1,0:T(8,128)(2,1)S(1)}, bf16[2,6,88,128]{3,2,1,0:T(8,128)(2,1)}, u32[]{:S(2)}, u32[]{:S(2)}) collective-permute-start(bf16[2,6,88,128]{3,2,1,0:T(8,128)(2,1)S(1)} %select.3.refs_6_), channel_id=1, source_target_pairs={{0,4},{4,0},{8,12},{12,8},{1,5},{5,1},{9,13},{13,9},{2,6},{6,2},{1... | collective-permute-start | bytes 811016 | tf_op jit(solution)/shard_map/ppermute | solution.py:200
  38.3 22.0 %collective-permute-start.6 = (bf16[2,6,88,128]{3,2,1,0:T(8,128)(2,1)}, bf16[2,6,88,128]{3,2,1,0:T(8,128)(2,1)S(1)}, u32[]{:S(2)}, u32[]{:S(2)}) collective-permute-start(bf16[2,6,88,128]{3,2,1,0:T(8,128)(2,1)} %copy-done), channel_id=1, source_target_pairs={{8,12},{4,0},{9,13},{5,1},{10,14},{6,2},{11,15},{7,3},{24,28},{20,... | collective-permute-start | bytes 811016 | tf_op jit(solution)/shard_map/ppermute | solution.py:202
  39.6 20.7 %collective-permute-start.5 = (bf16[2,6,88,128]{3,2,1,0:T(8,128)(2,1)S(1)}, bf16[2,6,88,128]{3,2,1,0:T(8,128)(2,1)S(1)}, u32[]{:S(2)}, u32[]{:S(2)}) collective-permute-start(bf16[2,6,88,128]{3,2,1,0:T(8,128)(2,1)S(1)} %select.2.refs_5_), channel_id=1, source_target_pairs={{4,8},{8,4},{5,9},{9,5},{6,10},{10,6},{7,11},{11,7},{20,24},{24,20... | collective-permute-start | bytes 811016 | tf_op jit(solution)/shard_map/ppermute | solution.py:203
  49.9 10.4 %collective-permute-start.9 = (bf16[2,6,88,128]{3,2,1,0:T(8,128)(2,1)}, bf16[2,6,88,128]{3,2,1,0:T(8,128)(2,1)S(1)}, u32[]{:S(2)}, u32[]{:S(2)}) collective-permute-start(bf16[2,6,88,128]{3,2,1,0:T(8,128)(2,1)} %copy-done.4), channel_id=1, source_target_pairs={{4,8},{8,4},{5,9},{9,5},{6,10},{10,6},{7,11},{11,7},{20,24},{24,20... | collective-permute-start | bytes 811016 | tf_op jit(solution)/shard_map/ppermute | solution.py:203
  50.6 9.8 %collective-permute-start.10 = (bf16[2,6,88,128]{3,2,1,0:T(8,128)(2,1)}, bf16[2,6,88,128]{3,2,1,0:T(8,128)(2,1)S(1)}, u32[]{:S(2)}, u32[]{:S(2)}) collective-permute-start(bf16[2,6,88,128]{3,2,1,0:T(8,128)(2,1)} %collective-permute-done.8.refs_10_), channel_id=1, source_target_pairs={{8,12},{4,0},{9,13},{5,1},{10,14},{6,2},{11,15},{7,3},{24,28},{20,... | collective-permute-start | bytes 811016 | tf_op jit(solution)/shard_map/ppermute | solution.py:202
  51.9 1.0 %copy-start.1 = (bf16[2,6,88,128]{3,2,1,0:T(8,128)(2,1)S(1)}, bf16[2,6,88,128]{3,2,1,0:T(8,128)(2,1)}, u32[]{:S(2)}) copy-start(bf16[2,6,88,128]{3,2,1,0:T(8,128)(2,1)} %copy-done) | copy-start | bytes 811012
  52.9 1.0 %copy-start.3 = (bf16[2,6,88,128]{3,2,1,0:T(8,128)(2,1)S(1)}, bf16[2,6,88,128]{3,2,1,0:T(8,128)(2,1)}, u32[]{:S(2)}) copy-start(bf16[2,6,88,128]{3,2,1,0:T(8,128)(2,1)} %copy-done.2) | copy-start | bytes 811012
  53.8 1.0 %copy-start.5 = (bf16[2,6,88,128]{3,2,1,0:T(8,128)(2,1)S(1)}, bf16[2,6,88,128]{3,2,1,0:T(8,128)(2,1)}, u32[]{:S(2)}) copy-start(bf16[2,6,88,128]{3,2,1,0:T(8,128)(2,1)} %copy-done.4) | copy-start | bytes 811012

commit v6 on v5

--- a/solution.py
+++ b/solution.py
@@ -35,9 +35,12 @@
     wave = jnp.where(turn % 2 == 0, even, -odd)
     wave = jnp.where((turn // 2) % 2 == 0, wave, -wave)
     table[...] = (wave * (1.0 / math.sqrt(length))).astype(bf16)
-    to = lax.broadcasted_iota(jnp.int32, (16 * win, 16 * win), 0)
-    at = lax.broadcasted_iota(jnp.int32, (1, 16 * win), 1)
-    shuffle = (to == (at % 16) * win + at // 16).astype(f32).astype(bf16)
+    whole = win // 8 * 8
+    shuffles = []
+    for count in (whole, win - whole):
+        to = lax.broadcasted_iota(jnp.int32, (16 * count, 16 * count), 0)
+        at = lax.broadcasted_iota(jnp.int32, (1, 16 * count), 1)
+        shuffles.append((to == (at % 16) * count + at // 16).astype(f32).astype(bf16))
     load.wait()
     for w in range(win):
         x = samples[w]
@@ -46,11 +49,15 @@
         y = jnp.dot(table[...], x, preferred_element_type=f32)
         spec[w] = (y * lax.rsqrt(power + 1e-06)).astype(bf16)
     for grp in range(2 * F // 16):
-        block = spec[:, 16 * grp : 16 * grp + 16, :].reshape(16 * win, spec.shape[-1])
-        turned = jnp.dot(shuffle, block, preferred_element_type=f32).astype(bf16)
+        turned = []
+        for shuffle, first, last in zip(shuffles, (0, whole), (whole, win)):
+            block = spec[first:last, 16 * grp : 16 * grp + 16, :]
+            block = block.reshape(16 * (last - first), spec.shape[-1])
+            turned.append(jnp.dot(shuffle, block, preferred_element_type=f32))
         for j in range(4):
             k, p = divmod(grp * 4 + j, bins // 2)
-            outs[k][p] = turned[4 * win * j : 4 * win * (j + 1)]
+            parts = [t[t.shape[0] // 4 * j : t.shape[0] // 4 * (j + 1)] for t in turned]
+            outs[k][p] = jnp.concatenate(parts, axis=0).astype(bf16)
 
 
 def select_kernel(cols, *refs):
@@ -92,6 +99,11 @@
             sem.at[p, half, b],
         )
 
+    whole = win // 8 * 8
+
+    def spans(j):
+        return (2 * whole * j, 2 * whole), (4 * whole + 2 * (win - whole) * j, 2 * (win - whole))
+
     def pair(p, _):
         turned = [[], []]
         for group in panels:
@@ -103,17 +115,17 @@
                         value = value + other[d, p].astype(f32)
                     stack.append(value)
             for j in range(2):
-                rows = [v[2 * win * j : 2 * win * (j + 1)] for v in stack]
+                rows = [v[a : a + n] for a, n in spans(j) for v in stack]
                 turned[j].append(jnp.transpose(jnp.concatenate(rows, axis=0)))
         for half in range(2):
             values = [slab[p + half * pairs].astype(f32) for slab in slabs]
             for j in range(2):
                 plain, swapped = [], []
-                for v in values:
-                    re = v[2 * win * j : 2 * win * j + win]
-                    im = v[2 * win * j + win : 2 * win * (j + 1)]
-                    plain += [re, im]
-                    swapped += [im, -re]
+                for a, n in spans(j):
+                    for v in values:
+                        re, im = v[a : a + n // 2], v[a + n // 2 : a + n]
+                        plain += [re, im]
+                        swapped += [im, -re]
                 right = jnp.concatenate(
                     [jnp.concatenate(plain, axis=0), jnp.concatenate(swapped, axis=0)], axis=1
                 ).astype(bf16)
@@ -199,9 +211,9 @@
             two = lax.ppermute(panel, "chan", [(i, i ^ 2) for i in range(4)])
             one = lax.ppermute(panel, "chan", [(i, i ^ 1) for i in range(4)])
             later, one, two = lax.optimization_barrier((panel, one, two))
+            mid = lax.ppermute(later, "chan", [(1, 2), (2, 1)])
             end = lax.ppermute(two, "chan", [(2, 3), (1, 0)])
-            mid = lax.ppermute(later, "chan", [(1, 2), (2, 1)])
-            return [[panel], [one], [two], [mid, end]]
+            return [[panel], [one], [two], [end, mid]]
         return [[panel]] + [
             [lax.ppermute(panel, "chan", [(i, (i + k) % n_chan) for i in range(n_chan)])]
             for k in range(1, n_chan)
@@ -212,8 +224,10 @@
         (quality[None, :].astype(f32) + 1.0) / 4.0,
         0.0,
     ).reshape(G, n_tf, win)
-    coef = jnp.take(jnp.concatenate([coef, coef], axis=2), order, axis=1)
-    coef = coef.reshape(G, 2 * n_tf * win)
+    coef = jnp.take(coef, order, axis=1)
+    halves = [coef[..., : win // 8 * 8], coef[..., win // 8 * 8 :]]
+    halves = [jnp.concatenate([h, h], axis=2).reshape(G, -1) for h in halves]
+    coef = jnp.concatenate(halves, axis=1)
     scale = 1.0 / math.sqrt(win * n_tf)
 
     far = [across(value, k + 2) for k, value in enumerate(got[2:])]
@@ -221,7 +235,7 @@
     *far, _, _ = lax.optimization_barrier((*far, near[1][0], near[2][0]))
     away = spread(select(far))
     out_shape = jax.ShapeDtypeStruct((bins, G, 2, src * n_chan, chans), bf16)
-    groups = [[0, 1, 2], [3]] if n_chan == 4 else [list(range(n_chan))]
+    groups = [[0], [1, 2], [3]] if n_chan == 4 else [list(range(n_chan))]
     stacks = None
     for group in groups:
         args, counts = [own, core, *far], []

time: 63.7 us -> 62.5 us (0.981)
  local copies, waits for them, and re-layouts: 4.56 us -> 1.01 us
  waiting for transfers between devices: 27.8 us -> 30.8 us
  Pallas kernels: 14.8 us -> 14.1 us
    ppermute x2, waiting for transfers between devices: 20.3 us -> 4.41 us  [spread(): two = lax.ppermute(panel, 'chan', [(i, i ^ 2) for i in range(4)])]
    ppermute x2, waiting for transfers between devices: 0.77 us -> 16.4 us  [spread(): one = lax.ppermute(panel, 'chan', [(i, i ^ 1) for i in range(4)])]
    ppermute x2, waiting for transfers between devices: 0.11 us -> 4.42 us  [spread(): end = lax.ppermute(two, 'chan', [(2, 3), (1, 0)])]
    unnamed x18 -> x7, local copies, waits for them, and re-layouts: 3.57 us -> 0.02 us
    ppermute x3, waiting for transfers between devices: 6.62 us -> 5.6 us  [across(): return lax.ppermute(value, 'tf', [(i, i ^ k) for i in range(n_tf)])]
    pallas_call x2 -> x3, Pallas kernels: 8.52 us -> 7.75 us  [shards(): pl.pallas_call(body, in_specs=[vmem] * (1 + len(args)) + [hbm] * len(extr...]
  transfers between devices with their start and end apart: 11 -> 11, of which waited for: 6 -> 6; matrix products, arithmetic and copies ran while one was open for 2% -> 2% of each run, Pallas kernels for 9% -> 10%
where the time goes in v6:
time: 62.5 us; the launch traced here: 62.3 us
  waiting for transfers between devices  30.8 us (49%)
  starting transfers between devices  15.8 us (25%)
  Pallas kernels  14.1 us (23%)
  local copies, waits for them, and re-layouts  1.01 us (2%)
    ppermute x2, waiting for transfers between devices, spread(): one = lax.ppermute(panel, 'chan', [(i, i ^ 1) for i in range(4)])  16.4 us
    pallas_call x3, Pallas kernels, shards(): pl.pallas_call(body, in_specs=[vmem] * (1 + len(args)) + [hbm] * len(extr...  7.75 us
    ppermute x3, waiting for transfers between devices, across(): return lax.ppermute(value, 'tf', [(i, i ^ k) for i in range(n_tf)])  5.6 us
    pallas_call x1, Pallas kernels, shards(): pl.pallas_call(lambda *refs: head_kernel((win, n_tf, bins), *refs), in_sp...  5.39 us
    ppermute x2, starting transfers between devices, spread(): two = lax.ppermute(panel, 'chan', [(i, i ^ 2) for i in range(4)])  5.17 us
    ppermute x2, waiting for transfers between devices, spread(): end = lax.ppermute(two, 'chan', [(2, 3), (1, 0)])  4.42 us
    ppermute x2, waiting for transfers between devices, spread(): two = lax.ppermute(panel, 'chan', [(i, i ^ 2) for i in range(4)])  4.41 us
    ppermute x2, starting transfers between devices, spread(): one = lax.ppermute(panel, 'chan', [(i, i ^ 1) for i in range(4)])  3.59 us
  transfers between devices with their start and end apart: 11, of which 6 were waited for; matrix products, arithmetic and copies ran while one was open for 2% of the time, Pallas kernels for 10%

profile of v6, /device:TPU:0, one launch (start us, length us, event | category | flops | bytes accessed | tf_op | source)
XLA Modules:
  0.0 62.3 jit_solution(4394110533000845373)
XLA Ops:
  0.0 0.0 copy-start.2
  0.0 0.0 copy-start
  0.0 0.0 copy-start.1
  0.0 5.4 %head.1 = (bf16[12,88,256]{2,1,0:T(8,128)(2,1)S(1)}, bf16[12,88,256]{2,1,0:T(8,128)(2,1)S(1)}, bf16[12,88,256]{2,1,0:T(8,128)(2,1)}, bf16[12,88,256]{2,1,0:T(8,128)(2,1)S(1)}) custom-call(bf16[22,512,256]{2,1,0:T(8,128)(2,1)} %refs_0_.1), custom_call_target="tpu_custom_call" | custom-call | flops 5500000256 | bytes 15000000 | tf_op jit(solution)/shard_map/head/pallas_call | solution.py:173
  5.4 0.5 collective-permute-start
  5.9 2.6 %collective-permute-start.1 = (bf16[12,88,256]{2,1,0:T(8,128)(2,1)}, bf16[12,88,256]{2,1,0:T(8,128)(2,1)S(1)}, u32[]{:S(2)}, u32[]{:S(2)}) collective-permute-start(bf16[12,88,256]{2,1,0:T(8,128)(2,1)} %get-tuple-element.19), channel_id=1, source_target_pairs={{0,2},{1,3},{2,0},{3,1},{4,6},{5,7},{6,4},{7,5},{8,10},{9,11},{10,... | collective-permute-start | bytes 1622024 | tf_op jit(solution)/shard_map/ppermute | solution.py:191
  8.5 0.1 collective-permute-start.2
  8.6 0.0 copy-done.2
  8.6 0.1 broadcast_in_dim.31
  8.7 0.0 copy-done
  8.7 0.1 eq.16
  8.8 0.6 gather_fusion
  9.4 0.0 copy-done.1
  9.4 0.1 dynamic-slice_subtract_fusion
  9.5 0.1 select_bitcast_fusion
  9.5 0.1 add_bitcast_fusion.cols
  9.6 0.1 slice.11
  9.7 0.1 pad_maximum_fusion.1
  9.8 0.0 collective-permute-done.refs_1_.refs_2_
  9.8 0.5 select.2.refs_5_
  10.2 1.9 %collective-permute-start.3 = (bf16[2,6,88,128]{3,2,1,0:T(8,128)(2,1)S(1)}, bf16[2,6,88,128]{3,2,1,0:T(8,128)(2,1)S(1)}, u32[]{:S(2)}, u32[]{:S(2)}) collective-permute-start(bf16[2,6,88,128]{3,2,1,0:T(8,128)(2,1)S(1)} %select.2.refs_5_), channel_id=1, source_target_pairs={{0,4},{4,0},{8,12},{12,8},{1,5},{5,1},{9,13},{13,9},{2,6},{6,2},{1... | collective-permute-start | bytes 811016 | tf_op jit(solution)/shard_map/ppermute | solution.py:212
  12.1 2.6 %collective-permute-start.4 = (bf16[2,6,88,128]{3,2,1,0:T(8,128)(2,1)S(1)}, bf16[2,6,88,128]{3,2,1,0:T(8,128)(2,1)S(1)}, u32[]{:S(2)}, u32[]{:S(2)}) collective-permute-start(bf16[2,6,88,128]{3,2,1,0:T(8,128)(2,1)S(1)} %select.2.refs_5_), channel_id=1, source_target_pairs={{0,8},{4,12},{8,0},{12,4},{1,9},{5,13},{9,1},{13,5},{2,10},{6,14},... | collective-permute-start | bytes 811016 | tf_op jit(solution)/shard_map/ppermute | solution.py:211
  14.7 0.1 pad_maximum_fusion
  14.8 0.1 reshape.47
  14.9 0.1 reshape.46
  15.0 9.8 %collective-permute-done.3.refs_5_ = bf16[2,6,88,128]{3,2,1,0:T(8,128)(2,1)S(1)} collective-permute-done((bf16[2,6,88,128]{3,2,1,0:T(8,128)(2,1)S(1)}, bf16[2,6,88,128]{3,2,1,0:T(8,128)(2,1)S(1)}, u32[]{:S(2)}, u32[]{:S(2)}) %collective-permute-start.3) | collective-permute-done | bytes 270368 | tf_op jit(solution)/shard_map/ppermute | solution.py:212
  24.8 2.5 %collective-permute-done.4.refs_7_ = bf16[2,6,88,128]{3,2,1,0:T(8,128)(2,1)S(1)} collective-permute-done((bf16[2,6,88,128]{3,2,1,0:T(8,128)(2,1)S(1)}, bf16[2,6,88,128]{3,2,1,0:T(8,128)(2,1)S(1)}, u32[]{:S(2)}, u32[]{:S(2)}) %collective-permute-start.4) | collective-permute-done | bytes 270368 | tf_op jit(solution)/shard_map/ppermute | solution.py:211
  27.3 0.0 collective-permute-done.1.refs_0_.refs_3_
  27.3 5.6 %collective-permute-done.2.refs_1_.refs_4_ = bf16[12,88,256]{2,1,0:T(8,128)(2,1)S(1)} collective-permute-done((bf16[12,88,256]{2,1,0:T(8,128)(2,1)S(1)}, bf16[12,88,256]{2,1,0:T(8,128)(2,1)S(1)}, u32[]{:S(2)}, u32[]{:S(2)}) %collective-permute-start.2) | collective-permute-done | bytes 540704 | tf_op jit(solution)/shard_map/ppermute | solution.py:191
  32.9 0.5 select.3.refs_6_
  33.4 1.7 %collective-permute-start.7 = (bf16[2,6,88,128]{3,2,1,0:T(8,128)(2,1)S(1)}, bf16[2,6,88,128]{3,2,1,0:T(8,128)(2,1)S(1)}, u32[]{:S(2)}, u32[]{:S(2)}) collective-permute-start(bf16[2,6,88,128]{3,2,1,0:T(8,128)(2,1)S(1)} %select.3.refs_6_), channel_id=1, source_target_pairs={{0,4},{4,0},{8,12},{12,8},{1,5},{5,1},{9,13},{13,9},{2,6},{6,2},{1... | collective-permute-start | bytes 811016 | tf_op jit(solution)/shard_map/ppermute | solution.py:212
  35.1 2.6 %collective-permute-start.8 = (bf16[2,6,88,128]{3,2,1,0:T(8,128)(2,1)S(1)}, bf16[2,6,88,128]{3,2,1,0:T(8,128)(2,1)S(1)}, u32[]{:S(2)}, u32[]{:S(2)}) collective-permute-start(bf16[2,6,88,128]{3,2,1,0:T(8,128)(2,1)S(1)} %select.3.refs_6_), channel_id=1, source_target_pairs={{0,8},{4,12},{8,0},{12,4},{1,9},{5,13},{9,1},{13,5},{2,10},{6,14},... | collective-permute-start | bytes 811016 | tf_op jit(solution)/shard_map/ppermute | solution.py:211
  37.7 1.3 %collective-permute-start.5 = (bf16[2,6,88,128]{3,2,1,0:T(8,128)(2,1)S(1)}, bf16[2,6,88,128]{3,2,1,0:T(8,128)(2,1)S(1)}, u32[]{:S(2)}, u32[]{:S(2)}) collective-permute-start(bf16[2,6,88,128]{3,2,1,0:T(8,128)(2,1)S(1)} %collective-permute-done.4.refs_7_), channel_id=1, source_target_pairs={{8,12},{4,0},{9,13},{5,1},{10,14},{6,2},{11,15},{7,3},{24,28},{20,... | collective-permute-start | bytes 811016 | tf_op jit(solution)/shard_map/ppermute | solution.py:215
  39.0 0.7 %collective-permute-start.6 = (bf16[2,6,88,128]{3,2,1,0:T(8,128)(2,1)S(1)}, bf16[2,6,88,128]{3,2,1,0:T(8,128)(2,1)S(1)}, u32[]{:S(2)}, u32[]{:S(2)}) collective-permute-start(bf16[2,6,88,128]{3,2,1,0:T(8,128)(2,1)S(1)} %select.2.refs_5_), channel_id=1, source_target_pairs={{4,8},{8,4},{5,9},{9,5},{6,10},{10,6},{7,11},{11,7},{20,24},{24,20... | collective-permute-start | bytes 811016 | tf_op jit(solution)/shard_map/ppermute | solution.py:214
  39.6 2.2 %cross.3.refs_9_ = bf16[24,2,2,256,256]{4,3,2,1,0:T(8,128)(2,1)} custom-call(f32[2,176]{1,0:T(2,128)S(1)} %constant_dynamic-update-slice_fusion.refs_0_, bf16[12,88,256]{2,1,0:T(8,128)(2,1)S(1)} %get-tuple-element.17.refs_0_.refs_1_, bf16[12,88,256]{2,1,0:T(8,128)(2,1)S(1)} %collective-permute-done.refs_1_.refs_2_, ...), custom_call_target="tpu_custom_call" | custom-call | flops 3339599872 | bytes 9108000 | tf_op jit(solution)/shard_map/cross/pallas_call | solution.py:256
  41.9 6.6 %collective-permute-done.7.refs_6_ = bf16[2,6,88,128]{3,2,1,0:T(8,128)(2,1)S(1)} collective-permute-done((bf16[2,6,88,128]{3,2,1,0:T(8,128)(2,1)S(1)}, bf16[2,6,88,128]{3,2,1,0:T(8,128)(2,1)S(1)}, u32[]{:S(2)}, u32[]{:S(2)}) %collective-permute-start.7) | collective-permute-done | bytes 270368 | tf_op jit(solution)/shard_map/ppermute | solution.py:212
  48.4 1.9 %collective-permute-done.8.refs_8_ = bf16[2,6,88,128]{3,2,1,0:T(8,128)(2,1)S(1)} collective-permute-done((bf16[2,6,88,128]{3,2,1,0:T(8,128)(2,1)S(1)}, bf16[2,6,88,128]{3,2,1,0:T(8,128)(2,1)S(1)}, u32[]{:S(2)}, u32[]{:S(2)}) %collective-permute-start.8) | collective-permute-done | bytes 270368 | tf_op jit(solution)/shard_map/ppermute | solution.py:211
  50.3 0.7 %collective-permute-start.10 = (bf16[2,6,88,128]{3,2,1,0:T(8,128)(2,1)S(1)}, bf16[2,6,88,128]{3,2,1,0:T(8,128)(2,1)S(1)}, u32[]{:S(2)}, u32[]{:S(2)}) collective-permute-start(bf16[2,6,88,128]{3,2,1,0:T(8,128)(2,1)S(1)} %select.3.refs_6_), channel_id=1, source_target_pairs={{4,8},{8,4},{5,9},{9,5},{6,10},{10,6},{7,11},{11,7},{20,24},{24,20... | collective-permute-start | bytes 811016 | tf_op jit(solution)/shard_map/ppermute | solution.py:214
  51.0 1.3 %collective-permute-start.9 = (bf16[2,6,88,128]{3,2,1,0:T(8,128)(2,1)S(1)}, bf16[2,6,88,128]{3,2,1,0:T(8,128)(2,1)S(1)}, u32[]{:S(2)}, u32[]{:S(2)}) collective-permute-start(bf16[2,6,88,128]{3,2,1,0:T(8,128)(2,1)S(1)} %collective-permute-done.8.refs_8_), channel_id=1, source_target_pairs={{8,12},{4,0},{9,13},{5,1},{10,14},{6,2},{11,15},{7,3},{24,28},{20,... | collective-permute-start | bytes 811016 | tf_op jit(solution)/shard_map/ppermute | solution.py:215
  52.3 3.3 %cross.4.refs_9_ = bf16[24,2,2,256,256]{4,3,2,1,0:T(8,128)(2,1)} custom-call(f32[2,176]{1,0:T(2,128)S(1)} %constant_dynamic-update-slice_fusion.refs_0_, bf16[12,88,256]{2,1,0:T(8,128)(2,1)S(1)} %get-tuple-element.17.refs_0_.refs_1_, bf16[12,88,256]{2,1,0:T(8,128)(2,1)S(1)} %collective-permute-done.refs_1_.refs_2_, ...), custom_call_target="tpu_custom_call", output_to_operand_aliasing={{}: (9, {})} | custom-call | flops 5029199872 | bytes 13716000 | tf_op jit(solution)/shard_map/cross/pallas_call | solution.py:256
  55.6 0.0 collective-permute-done.5.refs_5_
  55.6 0.0 collective-permute-done.6.refs_6_
  55.6 0.0 collective-permute-done.10.refs_8_
  55.6 4.4 %collective-permute-done.9.refs_7_ = bf16[2,6,88,128]{3,2,1,0:T(8,128)(2,1)S(1)} collective-permute-done((bf16[2,6,88,128]{3,2,1,0:T(8,128)(2,1)S(1)}, bf16[2,6,88,128]{3,2,1,0:T(8,128)(2,1)S(1)}, u32[]{:S(2)}, u32[]{:S(2)}) %collective-permute-start.9) | collective-permute-done | bytes 270368 | tf_op jit(solution)/shard_map/ppermute | solution.py:215
  60.0 2.2 %cross.5 = bf16[24,2,2,256,256]{4,3,2,1,0:T(8,128)(2,1)} custom-call(f32[2,176]{1,0:T(2,128)S(1)} %constant_dynamic-update-slice_fusion.refs_0_, bf16[12,88,256]{2,1,0:T(8,128)(2,1)S(1)} %get-tuple-element.17.refs_0_.refs_1_, bf16[12,88,256]{2,1,0:T(8,128)(2,1)S(1)} %collective-permute-done.refs_1_.refs_2_, ...), custom_call_target="tpu_custom_call", output_to_operand_aliasing={{}: (9, {})} | custom-call | flops 3339599872 | bytes 9108000 | tf_op jit(solution)/shard_map/cross/pallas_call | solution.py:256
  (9 shorter events, 0.0 us)
Async XLA Ops:
  0.0 8.6 %copy-start.2 = (s32[88]{0:T(128)S(1)}, s32[88]{0:T(128)}, u32[]{:S(2)}) copy-start(s32[88]{0:T(128)} %param.5) | copy-start | bytes 1060
  0.0 8.7 %copy-start = (s32[88]{0:T(128)S(1)}, s32[88]{0:T(128)}, u32[]{:S(2)}) copy-start(s32[88]{0:T(128)} %param.6) | copy-start | bytes 1060
  0.0 9.4 %copy-start.1 = (s32[256]{0:T(256)S(1)}, s32[256]{0:T(256)}, u32[]{:S(2)}) copy-start(s32[256]{0:T(256)} %param.7) | copy-start | bytes 3076
  5.4 4.4 %collective-permute-start = (bf16[12,88,256]{2,1,0:T(8,128)(2,1)S(1)}, bf16[12,88,256]{2,1,0:T(8,128)(2,1)S(1)}, u32[]{:S(2)}, u32[]{:S(2)}) collective-permute-start(bf16[12,88,256]{2,1,0:T(8,128)(2,1)S(1)} %get-tuple-element.18), channel_id=1, source_target_pairs={{0,1},{1,0},{2,3},{3,2},{4,5},{5,4},{6,7},{7,6},{8,9},{9,8},{10,11... | collective-permute-start | bytes 1622024 | tf_op jit(solution)/shard_map/ppermute | solution.py:191
  5.9 21.4 %collective-permute-start.1 = (bf16[12,88,256]{2,1,0:T(8,128)(2,1)}, bf16[12,88,256]{2,1,0:T(8,128)(2,1)S(1)}, u32[]{:S(2)}, u32[]{:S(2)}) collective-permute-start(bf16[12,88,256]{2,1,0:T(8,128)(2,1)} %get-tuple-element.19), channel_id=1, source_target_pairs={{0,2},{1,3},{2,0},{3,1},{4,6},{5,7},{6,4},{7,5},{8,10},{9,11},{10,... | collective-permute-start | bytes 1622024 | tf_op jit(solution)/shard_map/ppermute | solution.py:191
  8.5 24.4 %collective-permute-start.2 = (bf16[12,88,256]{2,1,0:T(8,128)(2,1)S(1)}, bf16[12,88,256]{2,1,0:T(8,128)(2,1)S(1)}, u32[]{:S(2)}, u32[]{:S(2)}) collective-permute-start(bf16[12,88,256]{2,1,0:T(8,128)(2,1)S(1)} %get-tuple-element.20), channel_id=1, source_target_pairs={{0,3},{1,2},{2,1},{3,0},{4,7},{5,6},{6,5},{7,4},{8,11},{9,10},{10,... | collective-permute-start | bytes 1622024 | tf_op jit(solution)/shard_map/ppermute | solution.py:191
  10.2 14.5 %collective-permute-start.3 = (bf16[2,6,88,128]{3,2,1,0:T(8,128)(2,1)S(1)}, bf16[2,6,88,128]{3,2,1,0:T(8,128)(2,1)S(1)}, u32[]{:S(2)}, u32[]{:S(2)}) collective-permute-start(bf16[2,6,88,128]{3,2,1,0:T(8,128)(2,1)S(1)} %select.2.refs_5_), channel_id=1, source_target_pairs={{0,4},{4,0},{8,12},{12,8},{1,5},{5,1},{9,13},{13,9},{2,6},{6,2},{1... | collective-permute-start | bytes 811016 | tf_op jit(solution)/shard_map/ppermute | solution.py:212
  12.1 15.2 %collective-permute-start.4 = (bf16[2,6,88,128]{3,2,1,0:T(8,128)(2,1)S(1)}, bf16[2,6,88,128]{3,2,1,0:T(8,128)(2,1)S(1)}, u32[]{:S(2)}, u32[]{:S(2)}) collective-permute-start(bf16[2,6,88,128]{3,2,1,0:T(8,128)(2,1)S(1)} %select.2.refs_5_), channel_id=1, source_target_pairs={{0,8},{4,12},{8,0},{12,4},{1,9},{5,13},{9,1},{13,5},{2,10},{6,14},... | collective-permute-start | bytes 811016 | tf_op jit(solution)/shard_map/ppermute | solution.py:211
  33.4 15.1 %collective-permute-start.7 = (bf16[2,6,88,128]{3,2,1,0:T(8,128)(2,1)S(1)}, bf16[2,6,88,128]{3,2,1,0:T(8,128)(2,1)S(1)}, u32[]{:S(2)}, u32[]{:S(2)}) collective-permute-start(bf16[2,6,88,128]{3,2,1,0:T(8,128)(2,1)S(1)} %select.3.refs_6_), channel_id=1, source_target_pairs={{0,4},{4,0},{8,12},{12,8},{1,5},{5,1},{9,13},{13,9},{2,6},{6,2},{1... | collective-permute-start | bytes 811016 | tf_op jit(solution)/shard_map/ppermute | solution.py:212
  35.1 15.2 %collective-permute-start.8 = (bf16[2,6,88,128]{3,2,1,0:T(8,128)(2,1)S(1)}, bf16[2,6,88,128]{3,2,1,0:T(8,128)(2,1)S(1)}, u32[]{:S(2)}, u32[]{:S(2)}) collective-permute-start(bf16[2,6,88,128]{3,2,1,0:T(8,128)(2,1)S(1)} %select.3.refs_6_), channel_id=1, source_target_pairs={{0,8},{4,12},{8,0},{12,4},{1,9},{5,13},{9,1},{13,5},{2,10},{6,14},... | collective-permute-start | bytes 811016 | tf_op jit(solution)/shard_map/ppermute | solution.py:211
  37.7 17.9 %collective-permute-start.5 = (bf16[2,6,88,128]{3,2,1,0:T(8,128)(2,1)S(1)}, bf16[2,6,88,128]{3,2,1,0:T(8,128)(2,1)S(1)}, u32[]{:S(2)}, u32[]{:S(2)}) collective-permute-start(bf16[2,6,88,128]{3,2,1,0:T(8,128)(2,1)S(1)} %collective-permute-done.4.refs_7_), channel_id=1, source_target_pairs={{8,12},{4,0},{9,13},{5,1},{10,14},{6,2},{11,15},{7,3},{24,28},{20,... | collective-permute-start | bytes 811016 | tf_op jit(solution)/shard_map/ppermute | solution.py:215
  39.0 16.7 %collective-permute-start.6 = (bf16[2,6,88,128]{3,2,1,0:T(8,128)(2,1)S(1)}, bf16[2,6,88,128]{3,2,1,0:T(8,128)(2,1)S(1)}, u32[]{:S(2)}, u32[]{:S(2)}) collective-permute-start(bf16[2,6,88,128]{3,2,1,0:T(8,128)(2,1)S(1)} %select.2.refs_5_), channel_id=1, source_target_pairs={{4,8},{8,4},{5,9},{9,5},{6,10},{10,6},{7,11},{11,7},{20,24},{24,20... | collective-permute-start | bytes 811016 | tf_op jit(solution)/shard_map/ppermute | solution.py:214
  50.3 5.3 %collective-permute-start.10 = (bf16[2,6,88,128]{3,2,1,0:T(8,128)(2,1)S(1)}, bf16[2,6,88,128]{3,2,1,0:T(8,128)(2,1)S(1)}, u32[]{:S(2)}, u32[]{:S(2)}) collective-permute-start(bf16[2,6,88,128]{3,2,1,0:T(8,128)(2,1)S(1)} %select.3.refs_6_), channel_id=1, source_target_pairs={{4,8},{8,4},{5,9},{9,5},{6,10},{10,6},{7,11},{11,7},{20,24},{24,20... | collective-permute-start | bytes 811016 | tf_op jit(solution)/shard_map/ppermute | solution.py:214
  51.0 9.1 %collective-permute-start.9 = (bf16[2,6,88,128]{3,2,1,0:T(8,128)(2,1)S(1)}, bf16[2,6,88,128]{3,2,1,0:T(8,128)(2,1)S(1)}, u32[]{:S(2)}, u32[]{:S(2)}) collective-permute-start(bf16[2,6,88,128]{3,2,1,0:T(8,128)(2,1)S(1)} %collective-permute-done.8.refs_8_), channel_id=1, source_target_pairs={{8,12},{4,0},{9,13},{5,1},{10,14},{6,2},{11,15},{7,3},{24,28},{20,... | collective-permute-start | bytes 811016 | tf_op jit(solution)/shard_map/ppermute | solution.py:215
